TPU v7x, 256 devices: a whole 4x4x8 slice. The times are simulated.
256 devices in a mesh: section: 64 (over z, x, core), tensor: 4 (over y).
Axes of the slice: x: 4, y: 4, z: 8, core: 2. Of those that a mesh axis runs over, the one named last changes fastest.
Arguments:
- hidden_in: bfloat16 [4096, 2048], P('section'), may hold values from -6 to 6
- queries: bfloat16 [4096, 4096], P('section', 'tensor'), may hold values from -48 to 48, as said below
- new_kv: bfloat16 [4096, 2, 512], P('section', None, 'tensor'), may hold values from -6 to 6
- cache: bfloat16 [4096, 2, 96, 512], P('section', None, None, 'tensor'), may hold values from -6 to 6
- lengths: int32 [4096], P('section'), may hold values from 2 to 96, as said below
- out_weight: bfloat16 [4096, 2048], P('tensor'), may hold values from -0.09375 to 0.09375
- moe_gain: float32 [2048], replicated, may hold values from 0.1 to 1.9
- expert_ids: int32 [4096, 8], P('section'), may hold values from 0 to 127, all different within a row; in each aligned block of 64 rows (0 to 63, 64 to 127, ...) at most 10 rows name the same one
- expert_gates: float32 [4096, 8], P('section'), may hold values from 0.1 to 1
- gate_up: bfloat16 [128, 2, 2048, 768], P('section', None, None, 'tensor'), may hold values from -0.125 to 0.125
- down: bfloat16 [128, 768, 2048], P('section', 'tensor'), may hold values from -0.21875 to 0.21875
- owners: int32 [4096], replicated, may hold values from -1 to 63, as said below
Outputs:
- thinker_out: bfloat16 [4096, 2048], P('section', 'tensor')
- talker_rows: bfloat16 [8192, 2048], P('section', 'tensor')
Inputs may be any that keep to these rules, and one draw needn't show every extreme that they name: queries and cache keys may be strongly aligned in some rows. `lengths`: among the 64 requests of each section index one has exactly 96. `expert_ids`: each row names 8 different experts; in each aligned block of 64 rows (the rows of one section index) no expert is named by more than 10 rows, a bound that some block reaches. `owners`: -1 marks a request without speech output; of the 64 requests of one section index at most 2 have the same owner, and one owner has exactly 2 from every section index, so it holds 128 rows.
All inputs are finite; a program needn't handle non-finite values.
Results may differ from a plain program's by a relative error of at most 0.015.
Values may be sent and summed in bfloat16 or wider, within the bound.
No kernel may reach another device: no remote copies, remote signals or barrier semaphores. Data moves between devices by JAX's collectives and lax.ppermute only.
A program may use at most 128 MiB of HBM per device.

v0:
```python
import math

import jax
import jax.numpy as jnp
from jax import lax
from jax.sharding import PartitionSpec as P

HD = 128
HCAP = 2
CAP = 10


def attend_local(queries, new_kv, cache, lengths):
    req_count = queries.shape[0]
    cached_count = cache.shape[2]
    kv_local = new_kv.shape[2] // HD
    group_size = queries.shape[1] // (kv_local * HD)
    query_heads = queries.reshape(req_count, kv_local, group_size, HD)
    cache_keys = cache[:, 0].reshape(req_count, cached_count, kv_local, HD)
    cache_values = cache[:, 1].reshape(req_count, cached_count, kv_local, HD)
    fresh_keys = new_kv[:, 0].reshape(req_count, kv_local, HD)
    fresh_values = new_kv[:, 1].reshape(req_count, kv_local, HD)
    scale_factor = 1.0 / math.sqrt(HD)
    cache_scores = (
        jnp.einsum("rkgd,rckd->rkgc", query_heads, cache_keys, preferred_element_type=jnp.float32)
        * scale_factor
    )
    valid_cells = jnp.arange(cached_count)[None, :] < lengths[:, None]
    cache_scores = jnp.where(valid_cells[:, None, None, :], cache_scores, -jnp.inf)
    fresh_scores = (
        jnp.einsum("rkgd,rkd->rkg", query_heads, fresh_keys, preferred_element_type=jnp.float32)
        * scale_factor
    )
    top_score = jnp.maximum(jnp.max(cache_scores, axis=-1), fresh_scores)
    cache_exp = jnp.exp(cache_scores - top_score[..., None])
    fresh_exp = jnp.exp(fresh_scores - top_score)
    total_mass = jnp.sum(cache_exp, axis=-1) + fresh_exp
    cache_weights = (cache_exp / total_mass[..., None]).astype(jnp.bfloat16)
    fresh_weights = (fresh_exp / total_mass).astype(jnp.bfloat16)
    context = jnp.einsum(
        "rkgc,rckd->rkgd", cache_weights, cache_values, preferred_element_type=jnp.float32
    )
    context = (
        context
        + fresh_weights.astype(jnp.float32)[..., None]
        * fresh_values.astype(jnp.float32)[:, :, None, :]
    )
    return context.reshape(req_count, kv_local * group_size * HD).astype(jnp.bfloat16)


def rms_scale(middle, moe_gain):
    values = middle.astype(jnp.float32)
    mean_square = jnp.mean(values * values, axis=-1, keepdims=True)
    return (values * lax.rsqrt(mean_square + 1e-06) * moe_gain).astype(jnp.bfloat16)


def expert_block(received, gate_up, down):
    stacked = jnp.einsum("nsqd,sgdh->nsqgh", received, gate_up, preferred_element_type=jnp.float32)
    activation = (jax.nn.silu(stacked[..., 0, :]) * stacked[..., 1, :]).astype(jnp.bfloat16)
    return jnp.einsum("nsqh,shd->nsqd", activation, down, preferred_element_type=jnp.float32)


def local(
    hidden_in,
    queries,
    new_kv,
    cache,
    lengths,
    out_weight,
    moe_gain,
    expert_ids,
    expert_gates,
    gate_up,
    down,
    owners,
):
    req_rows = hidden_in.shape[0]
    model_width = hidden_in.shape[1]
    top_count = expert_ids.shape[1]
    local_experts = gate_up.shape[0]
    section_count = lax.axis_size("section")
    section_index = lax.axis_index("section")
    tensor_index = lax.axis_index("tensor")
    quarter = model_width // lax.axis_size("tensor")
    expert_total = local_experts * section_count
    context = attend_local(queries, new_kv, cache, lengths)
    attention = lax.psum(
        jnp.dot(context, out_weight, preferred_element_type=jnp.float32).astype(jnp.bfloat16),
        "tensor",
    ).astype(jnp.float32)
    middle = (hidden_in.astype(jnp.float32) + attention).astype(jnp.bfloat16)
    normed = rms_scale(middle, moe_gain)
    gates = expert_gates / jnp.sum(expert_gates, axis=1, keepdims=True)
    flat_ids = expert_ids.reshape(req_rows * top_count)
    expert_onehot = (
        flat_ids[:, None] == jnp.arange(expert_total, dtype=jnp.int32)[None, :]
    ).astype(jnp.int32)
    order_within = jnp.sum((jnp.cumsum(expert_onehot, axis=0) - 1) * expert_onehot, axis=1)
    target = flat_ids * CAP + order_within
    row_of = jnp.arange(req_rows * top_count, dtype=jnp.int32) // top_count
    send_buffer = (
        jnp.zeros((expert_total * CAP, model_width), jnp.bfloat16).at[target].set(normed[row_of])
    )
    send_buffer = send_buffer.reshape(section_count, local_experts, CAP, model_width)
    partial_out = expert_block(
        lax.all_to_all(send_buffer, "section", split_axis=0, concat_axis=0, tiled=True),
        gate_up,
        down,
    ).astype(jnp.bfloat16)
    shares = (
        lax.psum_scatter(partial_out, "tensor", scatter_dimension=3, tiled=True)
        .astype(jnp.float32)
        .astype(jnp.bfloat16)
    )
    returned = lax.all_to_all(shares, "section", split_axis=0, concat_axis=0, tiled=True)
    back_rows = returned.reshape(expert_total * CAP, quarter)[target].reshape(
        req_rows, top_count, quarter
    )
    mixture = jnp.sum(gates[:, :, None] * back_rows.astype(jnp.float32), axis=1)
    middle_part = lax.dynamic_slice_in_dim(middle, tensor_index * quarter, quarter, 1)
    out_part = (middle_part.astype(jnp.float32) + mixture).astype(jnp.bfloat16)
    own_owner = lax.dynamic_slice_in_dim(owners, section_index * req_rows, req_rows)
    owner_onehot = (
        own_owner[:, None] == jnp.arange(section_count, dtype=jnp.int32)[None, :]
    ).astype(jnp.int32)
    position = jnp.sum((jnp.cumsum(owner_onehot, axis=0) - 1) * owner_onehot, axis=1)
    send_target = jnp.where(own_owner >= 0, own_owner * HCAP + position, section_count * HCAP)
    send_rows = (
        jnp.zeros((section_count * HCAP, quarter), jnp.bfloat16)
        .at[send_target]
        .set(out_part, mode="drop")
    )
    arrived = lax.all_to_all(
        send_rows.reshape(section_count, HCAP, quarter),
        "section",
        split_axis=0,
        concat_axis=0,
        tiled=True,
    )
    mine = (owners == section_index).reshape(section_count, req_rows).astype(jnp.int32)
    counts = jnp.sum(mine, axis=1)
    offsets = jnp.cumsum(counts) - counts
    slot_index = jnp.arange(HCAP, dtype=jnp.int32)
    placement = offsets[:, None] + slot_index[None, :]
    placement = jnp.where(slot_index[None, :] < counts[:, None], placement, section_count * HCAP)
    talker_part = jnp.zeros((section_count * HCAP, quarter), jnp.bfloat16)
    talker_part = talker_part.at[placement.reshape(section_count * HCAP)].set(
        arrived.reshape(section_count * HCAP, quarter), mode="drop"
    )
    return (out_part, talker_part)


def solution(mesh):
    in_specs = (
        P("section", None),
        P("section", "tensor"),
        P("section", None, "tensor"),
        P("section", None, None, "tensor"),
        P("section"),
        P("tensor", None),
        P(),
        P("section", None),
        P("section", None),
        P("section", None, None, "tensor"),
        P("section", "tensor", None),
        P(),
    )
    out_specs = (P("section", "tensor"), P("section", "tensor"))
    return jax.shard_map(local, mesh=mesh, in_specs=in_specs, out_specs=out_specs, check_vma=False)
```

profile of v0, /device:TPU:1, one launch (start us, length us, event | category | flops | bytes accessed | tf_op | source)
XLA Modules:
  0.0 383.8 jit_solution(1023480080390890564)
XLA Ops:
  7.2 1.1 copy.86
  9.0 0.9 fusion.58
  10.2 2.6 fusion.59
  13.0 2.0 fusion.29
  15.0 1.5 convolution_convert_fusion
  17.9 47.4 %all-reduce.2.cloned.1.call-done = bf16[64,2048]{1,0:T(8,128)(2,1)} async-done(((bf16[64,2048]{1,0:T(8,128)(2,1)}), bf16[64,2048]{1,0:T(8,128)(2,1)}) %all-reduce.2.cloned.1.call-update) | async-done | bytes 262160 | tf_op jit(solution)/shard_map/psum | solution.py:87
  65.3 1.2 fusion.35
  67.4 13.7 %scatter_custom_fusion = bf16[1280,2048]{1,0:T(8,128)(2,1)} fusion(s32[512]{0:T(512)S(1)} %bitcast.94, bf16[]{:T(256)} %constant.35.clone.1, bf16[64,2048]{1,0:T(8,128)(2,1)} %fusion.37, s32[1024]{0:T(1024)S(1)} %pad_clamp_fusion.1), kind=kCustom, calls=%fused_computation.9 | custom fusion | bytes 5243392 | tf_op jit(solution)/shard_map/scatter | solution.py:102
  81.1 9.5 %reshape.295 = bf16[64,2,10,2048]{3,2,1,0:T(8,128)(2,1)} reshape(bf16[1280,2048]{1,0:T(8,128)(2,1)} %scatter_custom_fusion) | data formatting | bytes 10485760 | tf_op jit(solution)/shard_map/reshape | solution.py:104
  90.6 10.3 %copy.69 = bf16[64,2,10,2048]{3,1,2,0:T(2,128)(2,1)S(1)} copy(bf16[64,2,10,2048]{3,2,1,0:T(8,128)(2,1)} %reshape.295) | data formatting | bytes 10485760 | tf_op jit(solution)/shard_map/reshape | solution.py:104
  100.9 130.3 %all_to_all.15 = bf16[64,2,10,2048]{3,1,2,0:T(2,128)(2,1)S(1)} all-to-all(bf16[64,2,10,2048]{3,1,2,0:T(2,128)(2,1)S(1)} %copy.69), channel_id=1, replica_groups=mesh['section'=64,'tensor'=4] {'section'}, dimensions={0} | all-to-all | bytes 10485760 | tf_op jit(solution)/shard_map/all_to_all | solution.py:106
  231.3 6.1 %fusion.6 = f32[64,2,10,2,192]{4,0,3,2,1:T(8,128)S(1)} fusion(bf16[2,2,2048,192]{2,3,1,0:T(8,128)(2,1)S(1)} %copy-done, bf16[64,2,10,2048,1]{3,1,2,0,4:T(2,128)(2,1)S(1)} %bitcast.84), kind=kOutput, calls=%fused_computation.13 | convolution fusion | flops 2013265920 | bytes 10354688 | tf_op jit(solution)/shard_map/nsqd,sgdh->nsqgh/dot_general | solution.py:58
  237.4 3.9 %convert_bitcast_fusion = bf16[64,2,10,2048]{3,0,2,1:T(8,128)(2,1)} fusion(bf16[2,192,2048]{2,1,0:T(8,128)(2,1)S(1)} %copy-done.10, f32[64,2,10,2,192]{4,0,3,2,1:T(8,128)S(1)} %fusion.6), kind=kOutput, calls=%fused_computation.7 | convolution fusion | flops 1010728960 | bytes 8781824 | tf_op jit(solution)/shard_map/nsqh,shd->nsqd/dot_general | solution.py:60
  241.3 54.5 %reduce-scatter.2.cloned.1.call-done = bf16[64,2,10,512]{3,0,2,1:T(8,128)(2,1)} async-done(((bf16[64,2,10,2048]{3,0,2,1:T(8,128)(2,1)}), bf16[64,2,10,512]{3,0,2,1:T(8,128)(2,1)}) %reduce-scatter.2.cloned.1.call-update) | async-done | bytes 1310736 | tf_op jit(solution)/shard_map/reduce_scatter | solution.py:111
  295.8 3.7 copy.72
  299.5 10.8 %all-to-all-start.1 = ((bf16[64,2,10,512]{3,1,2,0:T(2,128)(2,1)}), bf16[64,2,10,512]{3,1,2,0:T(2,128)(2,1)}, u32[]{:S(2)}, u32[]{:S(2)}) async-start(bf16[64,2,10,512]{3,1,2,0:T(2,128)(2,1)} %copy.72), calls=%async_computation.2 | async-start | bytes 2621440 | tf_op jit(solution)/shard_map/all_to_all | solution.py:115
  315.1 28.8 %all-to-all-done.1 = bf16[64,2,10,512]{3,1,2,0:T(2,128)(2,1)} async-done(((bf16[64,2,10,512]{3,1,2,0:T(2,128)(2,1)}), bf16[64,2,10,512]{3,1,2,0:T(2,128)(2,1)}, u32[]{:S(2)}, u32[]{:S(2)}) %all-to-all-start.1) | async-done | bytes 1310752 | tf_op jit(solution)/shard_map/all_to_all | solution.py:115
  343.9 3.2 copy.73
  347.0 3.6 reshape.296
  350.6 4.1 %gather_fusion = bf16[512,512]{1,0:T(8,128)(2,1)} fusion(bf16[1280,512]{1,0:T(8,128)(2,1)} %reshape.296, s32[1024]{0:T(1024)S(1)} %pad_clamp_fusion), kind=kCustom, calls=%fused_computation.1 | custom fusion | bytes 1050624 | tf_op jit(solution)/shard_map/gather | solution.py:116
  354.8 1.4 fusion.32
  357.8 6.3 %all-to-all-start.2 = ((bf16[64,2,512]{2,1,0:T(2,128)(2,1)}), bf16[64,2,512]{2,1,0:T(2,128)(2,1)S(1)}, u32[]{:S(2)}, u32[]{:S(2)}) async-start(bf16[64,2,512]{2,1,0:T(2,128)(2,1)} %reshape.299), calls=%async_computation.3 | async-start | bytes 262144 | tf_op jit(solution)/shard_map/all_to_all | solution.py:133
  364.4 10.9 %all-to-all-done.2 = bf16[64,2,512]{2,1,0:T(2,128)(2,1)S(1)} async-done(((bf16[64,2,512]{2,1,0:T(2,128)(2,1)}), bf16[64,2,512]{2,1,0:T(2,128)(2,1)S(1)}, u32[]{:S(2)}, u32[]{:S(2)}) %all-to-all-start.2) | async-done | bytes 131104 | tf_op jit(solution)/shard_map/all_to_all | solution.py:133
  375.3 1.7 scatter_custom_fusion.2
  (74 shorter events, 9.9 us)
Async XLA Ops:
  7.2 224.1 %copy-start = (bf16[2,2,2048,192]{2,3,1,0:T(8,128)(2,1)S(1)}, bf16[2,2,2048,192]{2,3,1,0:T(8,128)(2,1)}, u32[]{:S(2)}) copy-start(bf16[2,2,2048,192]{2,3,1,0:T(8,128)(2,1)} %param.21) | copy-start | bytes 9437188
  7.2 58.1 %all-reduce.2.cloned.1.call-start = ((), (), s32[]{:S(2)}) async-start(), calls=%async_computation.4 | async-start | bytes 524288 | tf_op jit(solution)/shard_map/psum | solution.py:87
  10.2 4.9 %copy-start.1 = (bf16[1024,2048]{1,0:T(8,128)(2,1)S(1)}, bf16[1024,2048]{1,0:T(8,128)(2,1)}, u32[]{:S(2)}) copy-start(bf16[1024,2048]{1,0:T(8,128)(2,1)} %param.17) | copy-start | bytes 12582916
  15.0 1.6 copy-start.4
  16.6 50.0 %copy-start.6 = (f32[2048]{0:T(1024)S(1)}, f32[2048]{0:T(1024)}, u32[]{:S(2)}) copy-start(f32[2048]{0:T(1024)} %param.18) | copy-start | bytes 24580
  16.6 279.2 %reduce-scatter.2.cloned.1.call-start = ((), (), s32[]{:S(2)}) async-start(), calls=%async_computation.5 | async-start | bytes 6553600 | tf_op jit(solution)/shard_map/reduce_scatter | solution.py:111
  17.9 63.2 %copy-start.7 = (s32[512,1]{0,1:T(1,128)}, s32[512,1]{0,1:T(1,128)S(1)}, u32[]{:S(2)}) copy-start(s32[512,1]{0,1:T(1,128)S(1)} %compare_select_fusion.1) | copy-start | bytes 6148
  231.3 6.1 %copy-start.10 = (bf16[2,192,2048]{2,1,0:T(8,128)(2,1)S(1)}, bf16[2,192,2048]{2,1,0:T(8,128)(2,1)}, u32[]{:S(2)}) copy-start(bf16[2,192,2048]{2,1,0:T(8,128)(2,1)} %param.22) | copy-start | bytes 4718596
  241.3 69.1 %copy-start.5 = (f32[64,8]{0,1:T(8,128)S(1)}, f32[64,8]{0,1:T(8,128)}, u32[]{:S(2)}) copy-start(f32[64,8]{0,1:T(8,128)} %param.20) | copy-start | bytes 6148
  241.3 69.2 %copy-start.3 = (s32[4096]{0:T(1024)S(1)}, s32[4096]{0:T(1024)}, u32[]{:S(2)}) copy-start(s32[4096]{0:T(1024)} %param.23) | copy-start | bytes 49156
  299.5 44.3 %all-to-all-start.1 = ((bf16[64,2,10,512]{3,1,2,0:T(2,128)(2,1)}), bf16[64,2,10,512]{3,1,2,0:T(2,128)(2,1)}, u32[]{:S(2)}, u32[]{:S(2)}) async-start(bf16[64,2,10,512]{3,1,2,0:T(2,128)(2,1)} %copy.72), calls=%async_computation.2 | async-start | bytes 2621440 | tf_op jit(solution)/shard_map/all_to_all | solution.py:115
  310.5 0.5 copy-start.9
  350.6 13.5 %copy-start.8 = (s32[64]{0:T(128)S(1)}, s32[64]{0:T(128)}, u32[]{:S(2)}) copy-start(s32[64]{0:T(128)} %reduce_sum.71) | copy-start | bytes 772
  356.2 20.8 %copy-start.2 = (bf16[64,512]{1,0:T(8,128)(2,1)}, bf16[64,512]{1,0:T(8,128)(2,1)S(1)}, u32[]{:S(2)}) copy-start(bf16[64,512]{1,0:T(8,128)(2,1)S(1)} %add_convert_fusion.1) | copy-start | bytes 196612
  357.8 17.4 %all-to-all-start.2 = ((bf16[64,2,512]{2,1,0:T(2,128)(2,1)}), bf16[64,2,512]{2,1,0:T(2,128)(2,1)S(1)}, u32[]{:S(2)}, u32[]{:S(2)}) async-start(bf16[64,2,512]{2,1,0:T(2,128)(2,1)} %reshape.299), calls=%async_computation.3 | async-start | bytes 262144 | tf_op jit(solution)/shard_map/all_to_all | solution.py:133
Sparse Core Ops, SparseCore 0:
  16.7 48.5 all-reduce.1
  241.4 54.3 reduce-scatter.1
where the time goes:
time: 385 us; the launch traced here: 384 us
  waiting for transfers between devices  142 us (37%)
  blocking collectives  130 us (34%)
  local copies, waits for them, and re-layouts  54.8 us (14%)
  starting transfers between devices  17.2 us (4%)
  matrix products  16.3 us (4%)
  between operations  14.3 us (4%)
  other arithmetic  9.28 us (2%)
    all_to_all x1, blocking collectives, local(): lax.all_to_all(send_buffer, 'section', split_axis=0, concat_axis=0, tiled...  130 us
    reduce_scatter x1, waiting for transfers between devices, local(): lax.psum_scatter(partial_out, 'tensor', scatter_dimension=3, tiled=True)  54.5 us
    psum x1, waiting for transfers between devices, local(): lax.psum(jnp.dot(context, out_weight, preferred_element_type=jnp.float32)...  47.4 us
    all_to_all x1, waiting for transfers between devices, local(): lax.all_to_all(shares, 'section', split_axis=0, concat_axis=0, tiled=True)  28.8 us
    reshape x2, local copies, waits for them, and re-layouts, local(): send_buffer.reshape(section_count, local_experts, CAP, model_width)  19.8 us
    scatter x1, local copies, waits for them, and re-layouts, local(): jnp.zeros((expert_total * CAP, model_width), jnp.bfloat16).at[target]  13.7 us
    all_to_all x1, waiting for transfers between devices, local(): lax.all_to_all(send_rows.reshape(section_count, HCAP, quarter), 'section'...  10.9 us
    all_to_all x1, starting transfers between devices, local(): lax.all_to_all(shares, 'section', split_axis=0, concat_axis=0, tiled=True)  10.8 us
  transfers between devices with their start and end apart: 4, of which 4 were waited for; matrix products, arithmetic and copies ran while one was open for 1% of the time, Pallas kernels for 0%

commit v1 on v0

v1 whole, which is shorter than its diff:
```python
import math

import jax
import jax.numpy as jnp
from jax import lax
from jax.experimental import pallas as pl
from jax.experimental.pallas import tpu as pltpu
from jax.sharding import Mesh
from jax.sharding import PartitionSpec as P

HD = 128
HCAP = 2
CAP = 10
NZ, NX, NC, NY = 8, 4, 2, 4
REQ = 64
SECTIONS = NZ * NX * NC
TOKENS = NZ * REQ
PLANE = NX * NY
BLOCK = NZ * CAP
QUARTER = 512
WIDTH = 2048
EHQ = 192
VMEM_LIMIT = 56 * 1024 * 1024


def attend_local(queries, new_kv, cache, lengths):
    req_count = queries.shape[0]
    cached_count = cache.shape[2]
    kv_local = new_kv.shape[2] // HD
    group_size = queries.shape[1] // (kv_local * HD)
    query_heads = queries.reshape(req_count, kv_local, group_size, HD)
    cache_keys = cache[:, 0].reshape(req_count, cached_count, kv_local, HD)
    cache_values = cache[:, 1].reshape(req_count, cached_count, kv_local, HD)
    fresh_keys = new_kv[:, 0].reshape(req_count, kv_local, HD)
    fresh_values = new_kv[:, 1].reshape(req_count, kv_local, HD)
    scale_factor = 1.0 / math.sqrt(HD)
    cache_scores = (
        jnp.einsum("rkgd,rckd->rkgc", query_heads, cache_keys, preferred_element_type=jnp.float32)
        * scale_factor
    )
    valid_cells = jnp.arange(cached_count)[None, :] < lengths[:, None]
    cache_scores = jnp.where(valid_cells[:, None, None, :], cache_scores, -jnp.inf)
    fresh_scores = (
        jnp.einsum("rkgd,rkd->rkg", query_heads, fresh_keys, preferred_element_type=jnp.float32)
        * scale_factor
    )
    top_score = jnp.maximum(jnp.max(cache_scores, axis=-1), fresh_scores)
    cache_exp = jnp.exp(cache_scores - top_score[..., None])
    fresh_exp = jnp.exp(fresh_scores - top_score)
    total_mass = jnp.sum(cache_exp, axis=-1) + fresh_exp
    cache_weights = (cache_exp / total_mass[..., None]).astype(jnp.bfloat16)
    fresh_weights = (fresh_exp / total_mass).astype(jnp.bfloat16)
    context = jnp.einsum(
        "rkgc,rckd->rkgd", cache_weights, cache_values, preferred_element_type=jnp.float32
    )
    context = (
        context
        + fresh_weights.astype(jnp.float32)[..., None]
        * fresh_values.astype(jnp.float32)[:, :, None, :]
    )
    return context.reshape(req_count, kv_local * group_size * HD).astype(jnp.bfloat16)


def plan_kernel(base_ref, meta_ref, target_ref, gate_ref):
    base = base_ref[0].astype(jnp.float32)
    expert = base + lax.broadcasted_iota(jnp.int32, (PLANE, TOKENS), 0).astype(jnp.float32)
    chosen = jnp.zeros((PLANE, TOKENS), jnp.float32)
    gate = jnp.zeros((PLANE, TOKENS), jnp.float32)
    total = jnp.sum(meta_ref[8:16, :], axis=0, keepdims=True)
    for k in range(8):
        hit = meta_ref[k : k + 1, :] == expert
        chosen = jnp.where(hit, 1.0, chosen)
        gate = jnp.where(hit, meta_ref[8 + k : 9 + k, :] / total, gate)
    earlier = lax.broadcasted_iota(jnp.int32, (TOKENS, TOKENS), 0)
    column = lax.broadcasted_iota(jnp.int32, (TOKENS, TOKENS), 1)
    same = (earlier // REQ) == (column // REQ)
    before = jnp.where(same & (earlier < column), 1.0, 0.0).astype(jnp.bfloat16)
    rank = jnp.dot(chosen.astype(jnp.bfloat16), before, preferred_element_type=jnp.float32)
    block = lax.broadcasted_iota(jnp.int32, (PLANE, TOKENS), 1) // REQ
    slot = rank.astype(jnp.int32) + block * CAP
    target_ref[...] = jnp.where(chosen > 0.0, slot, -1)
    gate_ref[...] = gate


def gather_kernel(target_ref, rows_ref, out_ref, pick_ref):
    slot = lax.broadcasted_iota(jnp.int32, (BLOCK, TOKENS), 0)
    for e in range(PLANE):
        hit = target_ref[e : e + 1, :] == slot
        pick_ref[e * BLOCK : (e + 1) * BLOCK, :] = jnp.where(hit, 1.0, 0.0).astype(jnp.bfloat16)
    rows = jnp.dot(pick_ref[...], rows_ref[...], preferred_element_type=jnp.float32)
    out_ref[...] = rows.astype(jnp.bfloat16)


def combine_kernel(target_ref, gate_ref, rows_ref, out_ref, high_ref, low_ref):
    slot = lax.broadcasted_iota(jnp.int32, (BLOCK, TOKENS), 0)
    for e in range(PLANE):
        hit = target_ref[e : e + 1, :] == slot
        weight = jnp.where(hit, gate_ref[e : e + 1, :], 0.0)
        high = weight.astype(jnp.bfloat16)
        high_ref[e * BLOCK : (e + 1) * BLOCK, :] = high
        low_ref[e * BLOCK : (e + 1) * BLOCK, :] = (weight - high.astype(jnp.float32)).astype(
            jnp.bfloat16
        )
    dims = (((0,), (0,)), ((), ()))
    rows = rows_ref[...]
    total = lax.dot_general(high_ref[...], rows, dims, preferred_element_type=jnp.float32)
    total = total + lax.dot_general(low_ref[...], rows, dims, preferred_element_type=jnp.float32)
    out_ref[...] = total.astype(jnp.bfloat16)


def expert_kernel(rows_ref, gain_ref, g0, g1, g2, g3, d0, d1, d2, d3, out_ref, *scratch):
    normed_ref, gu_ref, down_ref, total_ref, gu_sem, down_sem = scratch
    gates = (g0, g1, g2, g3)
    downs = (d0, d1, d2, d3)
    gate_copies = [pltpu.make_async_copy(gates[q], gu_ref.at[q], gu_sem.at[q]) for q in range(4)]
    down_copies = [pltpu.make_async_copy(downs[q], down_ref.at[q], down_sem.at[q]) for q in range(4)]
    for q in range(4):
        gate_copies[q].start()
        down_copies[q].start()
    for x in range(NX):
        parts = [rows_ref[x * NY + y].astype(jnp.float32) for y in range(NY)]
        square = sum(jnp.sum(part * part, axis=-1, keepdims=True) for part in parts)
        scale = lax.rsqrt(square * (1.0 / WIDTH) + 1e-06)
        for y in range(NY):
            columns = slice(y * QUARTER, (y + 1) * QUARTER)
            normed_ref[x * BLOCK : (x + 1) * BLOCK, columns] = (
                parts[y] * scale * gain_ref[:, columns]
            ).astype(jnp.bfloat16)
    for q in range(4):
        gate_copies[q].wait()
        both = jnp.dot(normed_ref[...], gu_ref[q], preferred_element_type=jnp.float32)
        gate, up = both[:, :EHQ], both[:, EHQ:]
        activation = (gate / (1.0 + jnp.exp(-gate)) * up).astype(jnp.bfloat16)
        down_copies[q].wait()
        part = jnp.dot(activation, down_ref[q], preferred_element_type=jnp.float32)
        if q == 0:
            total_ref[...] = part
        elif q < 3:
            total_ref[...] += part
        else:
            part = (total_ref[...] + part).astype(jnp.bfloat16)
            for x in range(NX):
                for y in range(NY):
                    out_ref[x * NY + y] = part[
                        x * BLOCK : (x + 1) * BLOCK, y * QUARTER : (y + 1) * QUARTER
                    ]


def vmem():
    return pl.BlockSpec(memory_space=pltpu.VMEM)


def params():
    return pltpu.CompilerParams(vmem_limit_bytes=VMEM_LIMIT)


def make_plan(base, meta):
    return pl.pallas_call(
        plan_kernel,
        out_shape=(
            jax.ShapeDtypeStruct((PLANE, TOKENS), jnp.int32),
            jax.ShapeDtypeStruct((PLANE, TOKENS), jnp.float32),
        ),
        in_specs=[pl.BlockSpec(memory_space=pltpu.SMEM), vmem()],
        out_specs=(vmem(), vmem()),
        compiler_params=params(),
        name="plan",
    )(base, meta)


def gather_rows(target, rows):
    return pl.pallas_call(
        gather_kernel,
        out_shape=jax.ShapeDtypeStruct((PLANE * BLOCK, QUARTER), jnp.bfloat16),
        in_specs=[vmem(), vmem()],
        out_specs=vmem(),
        scratch_shapes=[pltpu.VMEM((PLANE * BLOCK, TOKENS), jnp.bfloat16)],
        compiler_params=params(),
        name="gather_rows",
    )(target, rows)


def combine_rows(target, gate, rows):
    return pl.pallas_call(
        combine_kernel,
        out_shape=jax.ShapeDtypeStruct((TOKENS, QUARTER), jnp.bfloat16),
        in_specs=[vmem(), vmem(), vmem()],
        out_specs=vmem(),
        scratch_shapes=[pltpu.VMEM((PLANE * BLOCK, TOKENS), jnp.bfloat16)] * 2,
        compiler_params=params(),
        name="combine_rows",
    )(target, gate, rows)


def run_expert(rows, gain, gate_blocks, down_blocks):
    return pl.pallas_call(
        expert_kernel,
        out_shape=jax.ShapeDtypeStruct((PLANE, BLOCK, QUARTER), jnp.bfloat16),
        in_specs=[vmem(), vmem()] + [pl.BlockSpec(memory_space=pl.ANY)] * 8,
        out_specs=vmem(),
        scratch_shapes=[
            pltpu.VMEM((NX * BLOCK, WIDTH), jnp.bfloat16),
            pltpu.VMEM((4, WIDTH, 2 * EHQ), jnp.bfloat16),
            pltpu.VMEM((4, EHQ, WIDTH), jnp.bfloat16),
            pltpu.VMEM((NX * BLOCK, WIDTH), jnp.float32),
            pltpu.SemaphoreType.DMA((4,)),
            pltpu.SemaphoreType.DMA((4,)),
        ],
        compiler_params=params(),
        name="expert",
    )(rows, gain, *gate_blocks, *down_blocks)


def expert_weights(gate_up, down):
    y = lax.axis_index("y")
    even, odd = [], []
    for c in range(NC):
        for y_from in range(NY):
            source = c * NY + y_from
            core = y_from // 2
            even.append((source, core * NY + 2 * c + y_from % 2))
            odd.append((source, core * NY + 2 * c + 1 - y_from % 2))
    swap = [(0, 1), (1, 0)]
    gates, downs = [], []
    for index, moves in ((y % 2, even), (1 - y % 2, odd)):
        chosen = lax.dynamic_index_in_dim(gate_up, index, 0, keepdims=False)
        gate_block = jnp.concatenate([chosen[0], chosen[1]], axis=1)
        down_block = lax.dynamic_index_in_dim(down, index, 0, keepdims=False)
        gates.append(lax.ppermute(gate_block, ("c", "y"), moves))
        downs.append(lax.ppermute(down_block, ("c", "y"), moves))
    gates = gates + [lax.ppermute(block, "c", swap) for block in gates]
    downs = downs + [lax.ppermute(block, "c", swap) for block in downs]
    return gates, downs


def talker_plan(owners, section):
    own = lax.dynamic_slice_in_dim(owners, section * REQ, REQ)
    order = jnp.arange(REQ, dtype=jnp.int32)
    same = (own[:, None] == own[None, :]) & (order[:, None] > order[None, :])
    position = jnp.sum(same.astype(jnp.int32), axis=1)
    slot = jnp.where(own >= 0, own * HCAP + position, -1)
    send = (jnp.arange(SECTIONS * HCAP, dtype=jnp.int32)[:, None] == slot[None, :]).astype(
        jnp.bfloat16
    )
    counts = jnp.sum((owners == section).reshape(SECTIONS, REQ).astype(jnp.int32), axis=1)
    place = jnp.arange(SECTIONS, dtype=jnp.int32)
    offsets = jnp.sum(jnp.where(place[None, :] < place[:, None], counts[None, :], 0), axis=1)
    index = jnp.arange(HCAP, dtype=jnp.int32)
    put = jnp.where(index[None, :] < counts[:, None], offsets[:, None] + index[None, :], -1)
    put = put.reshape(SECTIONS * HCAP)
    take = (jnp.arange(SECTIONS * HCAP, dtype=jnp.int32)[:, None] == put[None, :]).astype(
        jnp.bfloat16
    )
    return send, take


def local(
    hidden_in,
    queries,
    new_kv,
    cache,
    lengths,
    out_weight,
    moe_gain,
    expert_ids,
    expert_gates,
    gate_up,
    down,
    owners,
):
    z, x, c, y = (lax.axis_index(name) for name in ("z", "x", "c", "y"))
    section = (z * NX + x) * NC + c
    gate_blocks, down_blocks = expert_weights(gate_up, down)

    meta = jnp.concatenate([expert_ids.astype(jnp.float32), expert_gates], axis=1).T
    meta = lax.all_to_all(jnp.broadcast_to(meta[None], (NZ, 16, REQ)), "z", 0, 0, tiled=True)
    meta = meta.transpose(1, 0, 2).reshape(16, TOKENS)

    context = attend_local(queries, new_kv, cache, lengths)
    attention = jnp.dot(context, out_weight, preferred_element_type=jnp.float32)
    pieces = attention.astype(jnp.bfloat16).reshape(REQ, NY, QUARTER).transpose(1, 0, 2)
    pieces = lax.all_to_all(pieces, "y", 0, 0, tiled=True)
    hidden = lax.dynamic_slice_in_dim(hidden_in, y * QUARTER, QUARTER, 1)
    middle = hidden.astype(jnp.float32) + jnp.sum(pieces.astype(jnp.float32), axis=0)
    middle = middle.astype(jnp.bfloat16)

    spread = lax.all_to_all(
        jnp.broadcast_to(middle[None], (NZ, REQ, QUARTER)), "z", 0, 0, tiled=True
    )
    target, gate = make_plan((z * PLANE).astype(jnp.int32).reshape(1), meta)
    send = gather_rows(target, spread.reshape(TOKENS, QUARTER))
    rows = lax.all_to_all(
        send.reshape(PLANE, BLOCK, QUARTER), ("x", "y"), 0, 0, tiled=True
    )
    done = run_expert(rows, moe_gain.reshape(1, WIDTH), gate_blocks, down_blocks)
    back = lax.all_to_all(done, ("x", "y"), 0, 0, tiled=True)
    part = combine_rows(target, gate, back.reshape(PLANE * BLOCK, QUARTER))
    part = lax.all_to_all(part.reshape(NZ, REQ, QUARTER), "z", 0, 0, tiled=True)
    out = middle.astype(jnp.float32) + jnp.sum(part.astype(jnp.float32), axis=0)
    out = out.astype(jnp.bfloat16)

    send_pick, take_pick = talker_plan(owners, section)
    leaving = jnp.dot(send_pick, out, preferred_element_type=jnp.float32).astype(jnp.bfloat16)
    arrived = lax.all_to_all(
        leaving.reshape(SECTIONS, HCAP, QUARTER), ("z", "x", "c"), 0, 0, tiled=True
    )
    talker = jnp.dot(
        take_pick, arrived.reshape(SECTIONS * HCAP, QUARTER), preferred_element_type=jnp.float32
    ).astype(jnp.bfloat16)
    return (out, talker)


def solution(mesh):
    section = ("z", "x", "c")
    fine = Mesh(mesh.devices.reshape(NZ, NX, NC, NY), ("z", "x", "c", "y"))
    in_specs = (
        P(section, None),
        P(section, "y"),
        P(section, None, "y"),
        P(section, None, None, "y"),
        P(section),
        P("y", None),
        P(),
        P(section, None),
        P(section, None),
        P(section, None, None, "y"),
        P(section, "y", None),
        P(),
    )
    out_specs = (P(section, "y"), P(section, "y"))
    return jax.shard_map(local, mesh=fine, in_specs=in_specs, out_specs=out_specs, check_vma=False)
```

time: 385 us -> 193 us (0.50)
  blocking collectives: 130 us -> 21.4 us
  waiting for transfers between devices: 142 us -> 68.5 us
  starting transfers between devices: 17.2 us -> 55.4 us
  local copies, waits for them, and re-layouts: 54.8 us -> 18 us
  Pallas kernels: 0 us -> 17.7 us
  between operations: 14.3 us -> 1.03 us
  matrix products: 16.3 us -> 3.63 us
    all_to_all x1, blocking collectives: 130 us -> 21.4 us  [local(): back = lax.all_to_all(done, ('x', 'y'), 0, 0, tiled=True)]
    reduce_scatter x1 -> x0, waiting for transfers between devices: 54.5 us -> none  [local(): lax.psum_scatter(partial_out, 'tensor', scatter_dimension=3, tiled=True)]
    psum x1 -> x0, waiting for transfers between devices: 47.4 us -> none  [local(): lax.psum(jnp.dot(context, out_weight, preferred_element_type=jnp.float32)...]
    all_to_all x2 -> x6, waiting for transfers between devices: 39.7 us -> 66.3 us  [the longest x1 24.1 us: local(): pieces = lax.all_to_all(pieces, 'y', 0, 0, tiled=True)]
    reshape x5 -> x4, local copies, waits for them, and re-layouts: 24.2 us -> 2.21 us  [the longest x1 0.75 us: local(): attention.astype(jnp.bfloat16).reshape(REQ, NY, QUARTER).transpose(1, 0, 2)]
    all_to_all x2 -> x6, starting transfers between devices: 17.1 us -> 37.4 us  [the longest x1 10.8 us: local(): lax.all_to_all(leaving.reshape(SECTIONS, HCAP, QUARTER), ('z', 'x', 'c'),...]
    ppermute x0 -> x8, starting transfers between devices: none -> 18 us  [the longest x2 6.2 us: expert_weights(): gates.append(lax.ppermute(gate_block, ('c', 'y'), moves))]
    pallas_call x0 -> x4, Pallas kernels: none -> 17.7 us  [the longest x1 9.43 us: run_expert(): pl.pallas_call(expert_kernel, out_shape=jax.ShapeDtypeStruct((PLANE, BLOC...]
  transfers between devices with their start and end apart: 4 -> 14, of which waited for: 4 -> 7; matrix products, arithmetic and copies ran while one was open for 1% -> 8% of each run, Pallas kernels for 0% -> 2%
where the time goes in v1:
time: 193 us; the launch traced here: 192 us
  waiting for transfers between devices  68.5 us (35%)
  starting transfers between devices  55.4 us (29%)
  blocking collectives  21.4 us (11%)
  local copies, waits for them, and re-layouts  18 us (9%)
  Pallas kernels  17.7 us (9%)
  other arithmetic  6.17 us (3%)
  matrix products  3.63 us (2%)
    all_to_all x1, waiting for transfers between devices, local(): pieces = lax.all_to_all(pieces, 'y', 0, 0, tiled=True)  24.1 us
    all_to_all x1, blocking collectives, local(): back = lax.all_to_all(done, ('x', 'y'), 0, 0, tiled=True)  21.4 us
    all_to_all x1, waiting for transfers between devices, local(): lax.all_to_all(send.reshape(PLANE, BLOCK, QUARTER), ('x', 'y'), 0, 0, til...  14.1 us
    all_to_all x1, waiting for transfers between devices, local(): part = lax.all_to_all(part.reshape(NZ, REQ, QUARTER), 'z', 0, 0, tiled=True)  11.2 us
    all_to_all x1, waiting for transfers between devices, local(): lax.all_to_all(leaving.reshape(SECTIONS, HCAP, QUARTER), ('z', 'x', 'c'),...  11 us
    all_to_all x1, starting transfers between devices, local(): lax.all_to_all(leaving.reshape(SECTIONS, HCAP, QUARTER), ('z', 'x', 'c'),...  10.8 us
    pallas_call x1, Pallas kernels, run_expert(): pl.pallas_call(expert_kernel, out_shape=jax.ShapeDtypeStruct((PLANE, BLOC...  9.43 us
    unnamed x34, local copies, waits for them, and re-layouts  7.91 us
  transfers between devices with their start and end apart: 14, of which 7 were waited for; matrix products, arithmetic and copies ran while one was open for 8% of the time, Pallas kernels for 2%

profile of v1, /device:TPU:1, one launch (start us, length us, event | category | flops | bytes accessed | tf_op | source)
XLA Modules:
  0.0 191.9 jit_solution(8011843459878961679)
XLA Ops:
  0.7 3.3 %constant_dynamic-slice_fusion.1 = (bf16[1,1,2048,192]{2,3,1,0:T(8,128)(2,1)S(1)}, bf16[1,1,2048,192]{2,3,1,0:T(8,128)(2,1)}, bf16[1,1,2048,192]{2,3,1,0:T(8,128)(2,1)S(1)}, bf16[1,1,2048,192]{2,3,1,0:T(8,128)(2,1)}) fusion(bf16[2,2,2048,192]{2,3,1,0:T(8,128)(2,1)} %param.21, s32[]{:T(128)S(6)} %select_n.53, s32[]{:T(128)S(6)} %select_n.52, s32[]{:T(128)S(6)} %add.75), kind=kLoop, calls=%fused_computation.54 | loop fusion | bytes 6291468 | tf_op jit(solution)/shard_map/slice | solution.py:227
  7.7 4.1 %collective-permute-start.1 = (bf16[2048,384]{1,0:T(8,128)(2,1)}, bf16[2048,384]{1,0:T(8,128)(2,1)}, u32[]{:S(2)}, u32[]{:S(2)}) collective-permute-start(bf16[2048,384]{1,0:T(8,128)(2,1)} %pad_maximum_fusion.1), channel_id=1, source_target_pairs={{0,1},{1,0},{2,5},{3,4},{4,3},{5,2},{6,7},{7,6},{8,9},{9,8},{10,13... | collective-permute-start | bytes 4718600 | tf_op jit(solution)/shard_map/ppermute | solution.py:229
  13.8 1.8 pad_maximum_fusion
  15.6 2.1 %collective-permute-start = (bf16[2048,384]{1,0:T(8,128)(2,1)}, bf16[2048,384]{1,0:T(8,128)(2,1)S(1)}, u32[]{:S(2)}, u32[]{:S(2)}) collective-permute-start(bf16[2048,384]{1,0:T(8,128)(2,1)} %pad_maximum_fusion), channel_id=1, source_target_pairs={{0,0},{1,1},{2,4},{3,5},{4,2},{5,3},{6,6},{7,7},{8,8},{9,9},{10,12... | collective-permute-start | bytes 4718600 | tf_op jit(solution)/shard_map/ppermute | solution.py:229
  21.8 3.4 %all-to-all-start = ((bf16[4,64,512]{2,1,0:T(8,128)(2,1)}), bf16[4,64,512]{2,1,0:T(8,128)(2,1)S(1)}, u32[]{:S(2)}, u32[]{:S(2)}) async-start(bf16[4,64,512]{2,1,0:T(8,128)(2,1)} %bitcast.60), calls=%async_computation | async-start | bytes 524288 | tf_op jit(solution)/shard_map/all_to_all | solution.py:282
  26.0 24.1 %all-to-all-done = bf16[4,64,512]{2,1,0:T(8,128)(2,1)S(1)} async-done(((bf16[4,64,512]{2,1,0:T(8,128)(2,1)}), bf16[4,64,512]{2,1,0:T(8,128)(2,1)S(1)}, u32[]{:S(2)}, u32[]{:S(2)}) %all-to-all-start) | async-done | bytes 262176 | tf_op jit(solution)/shard_map/all_to_all | solution.py:282
  50.1 7.2 %all-to-all-start.1 = ((f32[8,1,1024]{2,1,0:T(1,128)}), f32[8,1,1024]{2,1,0:T(1,128)S(1)}, u32[]{:S(2)}, u32[]{:S(2)}) async-start(f32[8,1,1024]{2,1,0:T(1,128)} %reshape.185), calls=%async_computation.1 | async-start | bytes 65536 | tf_op jit(solution)/shard_map/all_to_all | solution.py:276
  58.2 6.0 %all-to-all-done.1 = f32[8,1,1024]{2,1,0:T(1,128)S(1)} async-done(((f32[8,1,1024]{2,1,0:T(1,128)}), f32[8,1,1024]{2,1,0:T(1,128)S(1)}, u32[]{:S(2)}, u32[]{:S(2)}) %all-to-all-start.1) | async-done | bytes 32800 | tf_op jit(solution)/shard_map/all_to_all | solution.py:276
  65.1 3.5 %all-to-all-start.2 = ((bf16[8,64,512]{2,1,0:T(8,128)(2,1)}), bf16[8,64,512]{2,1,0:T(8,128)(2,1)S(1)}, u32[]{:S(2)}, u32[]{:S(2)}) async-start(bf16[8,64,512]{2,1,0:T(8,128)(2,1)} %broadcast_in_dim.34), calls=%async_computation.2 | async-start | bytes 1048576 | tf_op jit(solution)/shard_map/all_to_all | solution.py:287
  68.6 2.7 %dynamic-slice_bitcast_fusion = (bf16[192,2048]{1,0:T(8,128)(2,1)}, bf16[192,2048]{1,0:T(8,128)(2,1)}) fusion(bf16[2,192,2048]{2,1,0:T(8,128)(2,1)} %param.22, s32[]{:T(128)S(6)} %select_n.53, s32[]{:T(128)S(6)} %select_n.52), kind=kLoop, calls=%fused_computation.16 | loop fusion | bytes 3145736 | tf_op jit(solution)/shard_map/jit(dynamic_index_in_dim)/squeeze | solution.py:228
  71.3 2.6 %collective-permute-start.5 = (bf16[192,2048]{1,0:T(8,128)(2,1)}, bf16[192,2048]{1,0:T(8,128)(2,1)}, u32[]{:S(2)}, u32[]{:S(2)}) collective-permute-start(bf16[192,2048]{1,0:T(8,128)(2,1)} %get-tuple-element.10), channel_id=1, source_target_pairs={{0,1},{1,0},{2,5},{3,4},{4,3},{5,2},{6,7},{7,6},{8,9},{9,8},{10,13... | collective-permute-start | bytes 2359304 | tf_op jit(solution)/shard_map/ppermute | solution.py:230
  73.9 2.0 %collective-permute-start.4 = (bf16[192,2048]{1,0:T(8,128)(2,1)}, bf16[192,2048]{1,0:T(8,128)(2,1)}, u32[]{:S(2)}, u32[]{:S(2)}) collective-permute-start(bf16[192,2048]{1,0:T(8,128)(2,1)} %get-tuple-element.11), channel_id=1, source_target_pairs={{0,0},{1,1},{2,4},{3,5},{4,2},{5,3},{6,6},{7,7},{8,8},{9,9},{10,12... | collective-permute-start | bytes 2359304 | tf_op jit(solution)/shard_map/ppermute | solution.py:230
  76.0 6.0 %collective-permute-start.3 = (bf16[2048,384]{1,0:T(8,128)(2,1)}, bf16[2048,384]{1,0:T(8,128)(2,1)}, u32[]{:S(2)}, u32[]{:S(2)}) collective-permute-start(bf16[2048,384]{1,0:T(8,128)(2,1)} %collective-permute-done.1.g1), channel_id=1, source_target_pairs={{0,4},{4,0},{1,5},{5,1},{2,6},{6,2},{3,7},{7,3},{8,12},{12,8},{9,1... | collective-permute-start | bytes 4718600 | tf_op jit(solution)/shard_map/ppermute | solution.py:231
  86.6 3.0 %gather_rows.1 = bf16[1280,512]{1,0:T(8,128)(2,1)} custom-call(s32[16,512]{1,0:T(8,128)} %get-tuple-element.4.target_ref, bf16[512,512]{1,0:T(8,128)(2,1)} %bitcast.68), custom_call_target="tpu_custom_call" | custom-call | tf_op jit(solution)/shard_map/gather_rows/pallas_call | solution.py:172
  89.6 7.6 %all-to-all-start.3 = ((bf16[16,80,512]{2,1,0:T(8,128)(2,1)}), bf16[16,80,512]{2,1,0:T(8,128)(2,1)S(1)}, u32[]{:S(2)}, u32[]{:S(2)}) async-start(bf16[16,80,512]{2,1,0:T(8,128)(2,1)} %bitcast.62), calls=%async_computation.3 | async-start | bytes 2621440 | tf_op jit(solution)/shard_map/all_to_all | solution.py:292
  98.3 1.8 collective-permute-done.7.d3
  101.4 14.1 %all-to-all-done.3.rows_ref = bf16[16,80,512]{2,1,0:T(8,128)(2,1)S(1)} async-done(((bf16[16,80,512]{2,1,0:T(8,128)(2,1)}), bf16[16,80,512]{2,1,0:T(8,128)(2,1)S(1)}, u32[]{:S(2)}, u32[]{:S(2)}) %all-to-all-start.3) | async-done | bytes 1310752 | tf_op jit(solution)/shard_map/all_to_all | solution.py:292
  116.7 9.4 %expert.1 = bf16[16,80,512]{2,1,0:T(8,128)(2,1)} custom-call(bf16[16,80,512]{2,1,0:T(8,128)(2,1)} %copy-done, f32[1,2048]{1,0:T(1,128)} %bitcast.80, bf16[2048,384]{1,0:T(8,128)(2,1)} %copy-done.3, bf16[2048,384]{1,0:T(8,128)(2,1)} %collective-permute-done.1.g1, bf16[2048,384]{1,0:T(8,128)(2,1)} %collective-permute-done.2.g2, ...), custom_call_target="tpu_custom_call" | custom-call | tf_op jit(solution)/shard_map/expert/pallas_call | solution.py:196
  126.1 21.4 %all_to_all.35 = bf16[16,80,512]{2,1,0:T(8,128)(2,1)} all-to-all(bf16[16,80,512]{2,1,0:T(8,128)(2,1)} %expert.1), channel_id=1, replica_groups=mesh['z'=8,'x'=4,'c'=2,'y'=4] {'x','y'}, dimensions={0} | all-to-all | bytes 2621440 | tf_op jit(solution)/shard_map/all_to_all | solution.py:296
  147.6 3.8 %combine_rows.1 = bf16[512,512]{1,0:T(8,128)(2,1)} custom-call(s32[16,512]{1,0:T(8,128)} %get-tuple-element.4.target_ref, f32[16,512]{1,0:T(8,128)} %get-tuple-element.5.gate_ref, bf16[1280,512]{1,0:T(8,128)(2,1)} %bitcast.63), custom_call_target="tpu_custom_call" | custom-call | tf_op jit(solution)/shard_map/combine_rows/pallas_call | solution.py:184
  151.3 4.9 %all-to-all-start.5 = ((bf16[8,64,512]{2,1,0:T(8,128)(2,1)}), bf16[8,64,512]{2,1,0:T(8,128)(2,1)S(1)}, u32[]{:S(2)}, u32[]{:S(2)}) async-start(bf16[8,64,512]{2,1,0:T(8,128)(2,1)} %bitcast.69), calls=%async_computation.5 | async-start | bytes 1048576 | tf_op jit(solution)/shard_map/all_to_all | solution.py:298
  156.7 11.2 %all-to-all-done.5 = bf16[8,64,512]{2,1,0:T(8,128)(2,1)S(1)} async-done(((bf16[8,64,512]{2,1,0:T(8,128)(2,1)}), bf16[8,64,512]{2,1,0:T(8,128)(2,1)S(1)}, u32[]{:S(2)}, u32[]{:S(2)}) %all-to-all-start.5) | async-done | bytes 524320 | tf_op jit(solution)/shard_map/all_to_all | solution.py:298
  168.9 10.8 %all-to-all-start.6 = ((bf16[64,2,512]{2,1,0:T(2,128)(2,1)}), bf16[64,2,512]{2,1,0:T(2,128)(2,1)S(1)}, u32[]{:S(2)}, u32[]{:S(2)}) async-start(bf16[64,2,512]{2,1,0:T(2,128)(2,1)} %reshape.179), calls=%async_computation.6 | async-start | bytes 262144 | tf_op jit(solution)/shard_map/all_to_all | solution.py:304
  180.0 11.0 %all-to-all-done.6 = bf16[64,2,512]{2,1,0:T(2,128)(2,1)S(1)} async-done(((bf16[64,2,512]{2,1,0:T(2,128)(2,1)}), bf16[64,2,512]{2,1,0:T(2,128)(2,1)S(1)}, u32[]{:S(2)}, u32[]{:S(2)}) %all-to-all-start.6) | async-done | bytes 131104 | tf_op jit(solution)/shard_map/all_to_all | solution.py:304
  (82 shorter events, 23.1 us)
Async XLA Ops:
  7.7 68.3 %collective-permute-start.1 = (bf16[2048,384]{1,0:T(8,128)(2,1)}, bf16[2048,384]{1,0:T(8,128)(2,1)}, u32[]{:S(2)}, u32[]{:S(2)}) collective-permute-start(bf16[2048,384]{1,0:T(8,128)(2,1)} %pad_maximum_fusion.1), channel_id=1, source_target_pairs={{0,1},{1,0},{2,5},{3,4},{4,3},{5,2},{6,7},{7,6},{8,9},{9,8},{10,13... | collective-permute-start | bytes 4718600 | tf_op jit(solution)/shard_map/ppermute | solution.py:229
  13.7 3.9 %copy-start.12 = (s32[64]{0:T(128)S(1)}, s32[64]{0:T(128)}, u32[]{:S(2)}) copy-start(s32[64]{0:T(128)} %param.16) | copy-start | bytes 772
  13.8 4.0 %copy-start.8 = (bf16[64,2,128]{2,1,0:T(2,128)(2,1)S(1)}, bf16[64,2,128]{2,1,0:T(2,128)(2,1)}, u32[]{:S(2)}) copy-start(bf16[64,2,128]{2,1,0:T(2,128)(2,1)} %param.14) | copy-start | bytes 98308
  13.8 4.0 %copy-start.7 = (bf16[64,1024]{1,0:T(8,128)(2,1)S(1)}, bf16[64,1024]{1,0:T(8,128)(2,1)}, u32[]{:S(2)}) copy-start(bf16[64,1024]{1,0:T(8,128)(2,1)} %param.13) | copy-start | bytes 393220
  13.8 4.3 %copy-start.5 = (bf16[64,2,96,128]{3,2,1,0:T(8,128)(2,1)S(1)}, bf16[64,2,96,128]{3,2,1,0:T(8,128)(2,1)}, u32[]{:S(2)}) copy-start(bf16[64,2,96,128]{3,2,1,0:T(8,128)(2,1)} %param.15) | copy-start | bytes 9437188
  15.6 66.4 %collective-permute-start = (bf16[2048,384]{1,0:T(8,128)(2,1)}, bf16[2048,384]{1,0:T(8,128)(2,1)S(1)}, u32[]{:S(2)}, u32[]{:S(2)}) collective-permute-start(bf16[2048,384]{1,0:T(8,128)(2,1)} %pad_maximum_fusion), channel_id=1, source_target_pairs={{0,0},{1,1},{2,4},{3,5},{4,2},{5,3},{6,6},{7,7},{8,8},{9,9},{10,12... | collective-permute-start | bytes 4718600 | tf_op jit(solution)/shard_map/ppermute | solution.py:229
  18.1 2.2 %copy-start.1 = (bf16[1024,2048]{1,0:T(8,128)(2,1)S(1)}, bf16[1024,2048]{1,0:T(8,128)(2,1)}, u32[]{:S(2)}) copy-start(bf16[1024,2048]{1,0:T(8,128)(2,1)} %param.17) | copy-start | bytes 12582916
  20.3 5.0 %copy-start.10 = (s32[64,8]{0,1:T(8,128)S(1)}, s32[64,8]{0,1:T(8,128)}, u32[]{:S(2)}) copy-start(s32[64,8]{0,1:T(8,128)} %param.19) | copy-start | bytes 6148
  20.3 5.0 %copy-start.11 = (f32[64,8]{0,1:T(8,128)S(1)}, f32[64,8]{0,1:T(8,128)}, u32[]{:S(2)}) copy-start(f32[64,8]{0,1:T(8,128)} %param.20) | copy-start | bytes 6148
  21.8 28.3 %all-to-all-start = ((bf16[4,64,512]{2,1,0:T(8,128)(2,1)}), bf16[4,64,512]{2,1,0:T(8,128)(2,1)S(1)}, u32[]{:S(2)}, u32[]{:S(2)}) async-start(bf16[4,64,512]{2,1,0:T(8,128)(2,1)} %bitcast.60), calls=%async_computation | async-start | bytes 524288 | tf_op jit(solution)/shard_map/all_to_all | solution.py:282
  50.1 14.1 %all-to-all-start.1 = ((f32[8,1,1024]{2,1,0:T(1,128)}), f32[8,1,1024]{2,1,0:T(1,128)S(1)}, u32[]{:S(2)}, u32[]{:S(2)}) async-start(f32[8,1,1024]{2,1,0:T(1,128)} %reshape.185), calls=%async_computation.1 | async-start | bytes 65536 | tf_op jit(solution)/shard_map/all_to_all | solution.py:276
  65.1 20.7 %all-to-all-start.2 = ((bf16[8,64,512]{2,1,0:T(8,128)(2,1)}), bf16[8,64,512]{2,1,0:T(8,128)(2,1)S(1)}, u32[]{:S(2)}, u32[]{:S(2)}) async-start(bf16[8,64,512]{2,1,0:T(8,128)(2,1)} %broadcast_in_dim.34), calls=%async_computation.2 | async-start | bytes 1048576 | tf_op jit(solution)/shard_map/all_to_all | solution.py:287
  71.3 25.9 %collective-permute-start.5 = (bf16[192,2048]{1,0:T(8,128)(2,1)}, bf16[192,2048]{1,0:T(8,128)(2,1)}, u32[]{:S(2)}, u32[]{:S(2)}) collective-permute-start(bf16[192,2048]{1,0:T(8,128)(2,1)} %get-tuple-element.10), channel_id=1, source_target_pairs={{0,1},{1,0},{2,5},{3,4},{4,3},{5,2},{6,7},{7,6},{8,9},{9,8},{10,13... | collective-permute-start | bytes 2359304 | tf_op jit(solution)/shard_map/ppermute | solution.py:230
  73.9 24.1 %collective-permute-start.4 = (bf16[192,2048]{1,0:T(8,128)(2,1)}, bf16[192,2048]{1,0:T(8,128)(2,1)}, u32[]{:S(2)}, u32[]{:S(2)}) collective-permute-start(bf16[192,2048]{1,0:T(8,128)(2,1)} %get-tuple-element.11), channel_id=1, source_target_pairs={{0,0},{1,1},{2,4},{3,5},{4,2},{5,3},{6,6},{7,7},{8,8},{9,9},{10,12... | collective-permute-start | bytes 2359304 | tf_op jit(solution)/shard_map/ppermute | solution.py:230
  76.0 39.6 %collective-permute-start.3 = (bf16[2048,384]{1,0:T(8,128)(2,1)}, bf16[2048,384]{1,0:T(8,128)(2,1)}, u32[]{:S(2)}, u32[]{:S(2)}) collective-permute-start(bf16[2048,384]{1,0:T(8,128)(2,1)} %collective-permute-done.1.g1), channel_id=1, source_target_pairs={{0,4},{4,0},{1,5},{5,1},{2,6},{6,2},{3,7},{7,3},{8,12},{12,8},{9,1... | collective-permute-start | bytes 4718600 | tf_op jit(solution)/shard_map/ppermute | solution.py:231
  82.0 33.5 %copy-start.3 = (bf16[2048,384]{1,0:T(8,128)(2,1)}, bf16[2048,384]{1,0:T(8,128)(2,1)S(1)}, u32[]{:S(2)}) copy-start(bf16[2048,384]{1,0:T(8,128)(2,1)S(1)} %collective-permute-done.g0) | copy-start | bytes 4718596
  82.0 33.5 %collective-permute-start.2 = (bf16[2048,384]{1,0:T(8,128)(2,1)S(1)}, bf16[2048,384]{1,0:T(8,128)(2,1)}, u32[]{:S(2)}, u32[]{:S(2)}) collective-permute-start(bf16[2048,384]{1,0:T(8,128)(2,1)S(1)} %collective-permute-done.g0), channel_id=1, source_target_pairs={{0,4},{4,0},{1,5},{5,1},{2,6},{6,2},{3,7},{7,3},{8,12},{12,8},{9,1... | collective-permute-start | bytes 4718600 | tf_op jit(solution)/shard_map/ppermute | solution.py:231
  89.6 25.9 %all-to-all-start.3 = ((bf16[16,80,512]{2,1,0:T(8,128)(2,1)}), bf16[16,80,512]{2,1,0:T(8,128)(2,1)S(1)}, u32[]{:S(2)}, u32[]{:S(2)}) async-start(bf16[16,80,512]{2,1,0:T(8,128)(2,1)} %bitcast.62), calls=%async_computation.3 | async-start | bytes 2621440 | tf_op jit(solution)/shard_map/all_to_all | solution.py:292
  97.2 2.9 %collective-permute-start.7 = (bf16[192,2048]{1,0:T(8,128)(2,1)}, bf16[192,2048]{1,0:T(8,128)(2,1)S(1)}, u32[]{:S(2)}, u32[]{:S(2)}) collective-permute-start(bf16[192,2048]{1,0:T(8,128)(2,1)} %collective-permute-done.5.d1), channel_id=1, source_target_pairs={{0,4},{4,0},{1,5},{5,1},{2,6},{6,2},{3,7},{7,3},{8,12},{12,8},{9,1... | collective-permute-start | bytes 2359304 | tf_op jit(solution)/shard_map/ppermute | solution.py:232
  98.0 3.4 %collective-permute-start.6 = (bf16[192,2048]{1,0:T(8,128)(2,1)}, bf16[192,2048]{1,0:T(8,128)(2,1)}, u32[]{:S(2)}, u32[]{:S(2)}) collective-permute-start(bf16[192,2048]{1,0:T(8,128)(2,1)} %collective-permute-done.4.d0), channel_id=1, source_target_pairs={{0,4},{4,0},{1,5},{5,1},{2,6},{6,2},{3,7},{7,3},{8,12},{12,8},{9,1... | collective-permute-start | bytes 2359304 | tf_op jit(solution)/shard_map/ppermute | solution.py:232
  147.6 8.6 %copy-start.9 = (s32[4096]{0:T(1024)S(1)}, s32[4096]{0:T(1024)}, u32[]{:S(2)}) copy-start(s32[4096]{0:T(1024)} %param.23) | copy-start | bytes 49156
  151.3 16.6 %all-to-all-start.5 = ((bf16[8,64,512]{2,1,0:T(8,128)(2,1)}), bf16[8,64,512]{2,1,0:T(8,128)(2,1)S(1)}, u32[]{:S(2)}, u32[]{:S(2)}) async-start(bf16[8,64,512]{2,1,0:T(8,128)(2,1)} %bitcast.69), calls=%async_computation.5 | async-start | bytes 1048576 | tf_op jit(solution)/shard_map/all_to_all | solution.py:298
  168.0 24.0 %copy-start.6 = (bf16[64,512]{1,0:T(8,128)(2,1)}, bf16[64,512]{1,0:T(8,128)(2,1)S(1)}, u32[]{:S(2)}) copy-start(bf16[64,512]{1,0:T(8,128)(2,1)S(1)} %add_convert_fusion) | copy-start | bytes 196612
  168.9 22.2 %all-to-all-start.6 = ((bf16[64,2,512]{2,1,0:T(2,128)(2,1)}), bf16[64,2,512]{2,1,0:T(2,128)(2,1)S(1)}, u32[]{:S(2)}, u32[]{:S(2)}) async-start(bf16[64,2,512]{2,1,0:T(2,128)(2,1)} %reshape.179), calls=%async_computation.6 | async-start | bytes 262144 | tf_op jit(solution)/shard_map/all_to_all | solution.py:304
  (3 other events, 2.9 us)

commit v2 on v1

v2 whole, which is shorter than its diff:
```python
import math

import jax
import jax.numpy as jnp
from jax import lax
from jax.experimental import pallas as pl
from jax.experimental.pallas import tpu as pltpu
from jax.sharding import Mesh
from jax.sharding import PartitionSpec as P

HD = 128
HCAP = 2
CAP = 10
NZ, NX, NC, NY = 8, 4, 2, 4
REQ = 64
SECTIONS = NZ * NX * NC
TOKENS = NZ * REQ
PLANE = NX * NY
BLOCK = NZ * CAP
QUARTER = 512
WIDTH = 2048
EHQ = 192


def attend_local(queries, new_kv, cache, lengths):
    req_count = queries.shape[0]
    cached_count = cache.shape[2]
    kv_local = new_kv.shape[2] // HD
    group_size = queries.shape[1] // (kv_local * HD)
    query_heads = queries.reshape(req_count, kv_local, group_size, HD)
    cache_keys = cache[:, 0].reshape(req_count, cached_count, kv_local, HD)
    cache_values = cache[:, 1].reshape(req_count, cached_count, kv_local, HD)
    fresh_keys = new_kv[:, 0].reshape(req_count, kv_local, HD)
    fresh_values = new_kv[:, 1].reshape(req_count, kv_local, HD)
    scale_factor = 1.0 / math.sqrt(HD)
    cache_scores = (
        jnp.einsum("rkgd,rckd->rkgc", query_heads, cache_keys, preferred_element_type=jnp.float32)
        * scale_factor
    )
    valid_cells = jnp.arange(cached_count)[None, :] < lengths[:, None]
    cache_scores = jnp.where(valid_cells[:, None, None, :], cache_scores, -jnp.inf)
    fresh_scores = (
        jnp.einsum("rkgd,rkd->rkg", query_heads, fresh_keys, preferred_element_type=jnp.float32)
        * scale_factor
    )
    top_score = jnp.maximum(jnp.max(cache_scores, axis=-1), fresh_scores)
    cache_exp = jnp.exp(cache_scores - top_score[..., None])
    fresh_exp = jnp.exp(fresh_scores - top_score)
    total_mass = jnp.sum(cache_exp, axis=-1) + fresh_exp
    cache_weights = (cache_exp / total_mass[..., None]).astype(jnp.bfloat16)
    fresh_weights = (fresh_exp / total_mass).astype(jnp.bfloat16)
    context = jnp.einsum(
        "rkgc,rckd->rkgd", cache_weights, cache_values, preferred_element_type=jnp.float32
    )
    context = (
        context
        + fresh_weights.astype(jnp.float32)[..., None]
        * fresh_values.astype(jnp.float32)[:, :, None, :]
    )
    return context.reshape(req_count, kv_local * group_size * HD).astype(jnp.bfloat16)


def plan_kernel(ids_ref, gates_ref, out_ref):
    ids = jnp.concatenate([ids_ref[...], ids_ref[...]], axis=1)
    gates = jnp.concatenate([gates_ref[...], gates_ref[...]], axis=1)
    gates = gates / jnp.sum(gates, axis=0, keepdims=True)
    experts = NZ * PLANE
    expert = lax.broadcasted_iota(jnp.int32, (experts, 2 * REQ), 0)
    chosen = jnp.zeros((experts, 2 * REQ), jnp.float32)
    gate = jnp.zeros((experts, 2 * REQ), jnp.float32)
    for k in range(8):
        hit = ids[k : k + 1, :] == expert
        chosen = jnp.where(hit, 1.0, chosen)
        gate = jnp.where(hit, gates[k : k + 1, :], gate)
    earlier = lax.broadcasted_iota(jnp.int32, (2 * REQ, 2 * REQ), 0)
    token = lax.broadcasted_iota(jnp.int32, (2 * REQ, 2 * REQ), 1)
    token = jnp.where(token >= REQ, token - REQ, token)
    before = jnp.where(earlier < token, 1.0, 0.0).astype(jnp.bfloat16)
    rank = jnp.dot(chosen.astype(jnp.bfloat16), before, preferred_element_type=jnp.float32)
    slot = jnp.where(chosen > 0.0, rank, -1.0).astype(jnp.bfloat16)
    gate = gate.astype(jnp.bfloat16)
    out_ref[...] = jnp.zeros((NZ, PLANE, QUARTER), jnp.bfloat16)
    for z in range(NZ):
        out_ref[z, :, : 2 * REQ] = slot[z * PLANE : (z + 1) * PLANE, :]
        out_ref[z, :, 2 * REQ : 4 * REQ] = gate[z * PLANE : (z + 1) * PLANE, :]


def pick_kernel(first_ref, after_ref, gate_up, down, even_ref, odd_ref, sems):
    first = first_ref[0]
    copies = []
    for k, out in ((0, even_ref), (1, odd_ref)):
        index = first if k == 0 else 1 - first
        copies.append(pltpu.make_async_copy(gate_up.at[index], out.at[pl.ds(0, 2)], sems.at[2 * k]))
        copies.append(pltpu.make_async_copy(down.at[index], out.at[2], sems.at[2 * k + 1]))
    for copy in copies:
        copy.start()
    for copy in copies:
        copy.wait()


def middle_kernel(pieces_ref, hidden_ref, plan_ref, *refs):
    message_ref, middle_ref = refs[2:4]
    total = hidden_ref[...].astype(jnp.float32)
    for y in range(NY):
        total = total + pieces_ref[y].astype(jnp.float32)
    middle = total.astype(jnp.bfloat16)
    middle_ref[...] = middle
    for z in range(NZ):
        message_ref[z, :REQ, :] = middle
        message_ref[z, REQ:, :] = plan_ref[z]


def gather_kernel(spread_ref, out_ref, target_ref, gate_ref, pick_ref, rows_ref):
    low = lax.broadcasted_iota(jnp.int32, (PLANE, 2 * REQ), 1) < REQ
    for pair in range(NZ // 2):
        left, right = spread_ref[2 * pair, REQ:, :], spread_ref[2 * pair + 1, REQ:, :]
        left, right = left.astype(jnp.float32), right.astype(jnp.float32)
        both = jnp.where(low, left[:, : 2 * REQ], right[:, : 2 * REQ])
        block = jnp.where(low, float(2 * pair * CAP), float((2 * pair + 1) * CAP))
        columns = slice(pair * 2 * REQ, (pair + 1) * 2 * REQ)
        target_ref[:, columns] = jnp.where(both >= 0.0, both + block, -1.0)
        gate_ref[:, columns] = jnp.where(
            low, left[:, 2 * REQ : 4 * REQ], right[:, 2 * REQ : 4 * REQ]
        )
    for z in range(NZ):
        rows_ref[z * REQ : (z + 1) * REQ, :] = spread_ref[z, :REQ, :]
    slot = lax.broadcasted_iota(jnp.int32, (BLOCK, TOKENS), 0).astype(jnp.float32)
    for e in range(PLANE):
        hit = target_ref[e : e + 1, :] == slot
        pick_ref[e * BLOCK : (e + 1) * BLOCK, :] = jnp.where(hit, 1.0, 0.0).astype(jnp.bfloat16)
    for e in range(0, PLANE, 4):
        rows = jnp.dot(
            pick_ref[e * BLOCK : (e + 4) * BLOCK, :],
            rows_ref[...],
            preferred_element_type=jnp.float32,
        ).astype(jnp.bfloat16)
        for k in range(4):
            out_ref[e + k] = rows[k * BLOCK : (k + 1) * BLOCK, :]


def hold_kernel(*refs):
    del refs


def combine_kernel(target_ref, gate_ref, rows_ref, out_ref, weight_ref, packed_ref):
    slot = lax.broadcasted_iota(jnp.int32, (BLOCK, TOKENS), 0).astype(jnp.float32)
    for e in range(PLANE):
        hit = target_ref[e : e + 1, :] == slot
        weight = jnp.where(hit, gate_ref[e : e + 1, :], 0.0)
        weight_ref[e * BLOCK : (e + 1) * BLOCK, :] = weight.astype(jnp.bfloat16)
        packed_ref[e * BLOCK : (e + 1) * BLOCK, :] = rows_ref[e]
    dims = (((0,), (0,)), ((), ()))
    total = lax.dot_general(
        weight_ref[...], packed_ref[...], dims, preferred_element_type=jnp.float32
    ).astype(jnp.bfloat16)
    for z in range(NZ):
        out_ref[z] = total[z * REQ : (z + 1) * REQ, :]


def expert_kernel(rows_ref, gain_ref, w0, w1, w2, w3, out_ref, *scratch):
    normed_ref, weight_ref, act_ref, sems = scratch
    copies = []
    for part in range(3):
        for q, block in enumerate((w0, w1, w2, w3)):
            copies.append(
                pltpu.make_async_copy(
                    block.at[part], weight_ref.at[part, pl.ds(q * EHQ, EHQ)], sems.at[part, q]
                )
            )
    for copy in copies:
        copy.start()
    for x in range(NX):
        parts = [rows_ref[x * NY + y].astype(jnp.float32) for y in range(NY)]
        square = sum(jnp.sum(part * part, axis=-1, keepdims=True) for part in parts)
        scale = lax.rsqrt(square * (1.0 / WIDTH) + 1e-06)
        for y in range(NY):
            columns = slice(y * QUARTER, (y + 1) * QUARTER)
            normed_ref[x * BLOCK : (x + 1) * BLOCK, columns] = (
                parts[y] * scale * gain_ref[:, columns]
            ).astype(jnp.bfloat16)
    dims = (((1,), (1,)), ((), ()))
    for copy in copies[:4]:
        copy.wait()
    gate = lax.dot_general(
        normed_ref[...], weight_ref[0], dims, preferred_element_type=jnp.float32
    )
    for copy in copies[4:8]:
        copy.wait()
    up = lax.dot_general(normed_ref[...], weight_ref[1], dims, preferred_element_type=jnp.float32)
    act_ref[...] = (gate / (1.0 + jnp.exp(-gate)) * up).astype(jnp.bfloat16)
    for copy in copies[8:]:
        copy.wait()
    for y in range(NY):
        part = jnp.dot(
            act_ref[...],
            weight_ref[2, :, y * QUARTER : (y + 1) * QUARTER],
            preferred_element_type=jnp.float32,
        ).astype(jnp.bfloat16)
        for x in range(NX):
            out_ref[x * NY + y] = part[x * BLOCK : (x + 1) * BLOCK, :]


def vmem():
    return pl.BlockSpec(memory_space=pltpu.VMEM)


def anywhere():
    return pl.BlockSpec(memory_space=pl.ANY)


def params(mib=16):
    return pltpu.CompilerParams(vmem_limit_bytes=mib * 1024 * 1024)


def shape(*dims, dtype=jnp.bfloat16):
    return jax.ShapeDtypeStruct(dims, dtype)


def make_plan(ids, gates):
    return pl.pallas_call(
        plan_kernel,
        out_shape=shape(NZ, PLANE, QUARTER),
        in_specs=[vmem(), vmem()],
        out_specs=vmem(),
        compiler_params=params(),
        name="plan",
    )(ids, gates)


def pick_weights(first, after, gate_up, down):
    block = shape(3, EHQ, WIDTH)
    return pl.pallas_call(
        pick_kernel,
        out_shape=(block, block),
        in_specs=[pl.BlockSpec(memory_space=pltpu.SMEM)] + [anywhere()] * 3,
        out_specs=(anywhere(), anywhere()),
        scratch_shapes=[pltpu.SemaphoreType.DMA((4,))],
        compiler_params=params(),
        name="pick_weights",
    )(first, after, gate_up, down)


def sum_middle(pieces, hidden, plan, blocks):
    return pl.pallas_call(
        middle_kernel,
        out_shape=(
            shape(NZ, REQ + PLANE, QUARTER),
            shape(REQ, QUARTER),
            *[shape(*block.shape) for block in blocks],
        ),
        in_specs=[vmem()] * 3 + [anywhere()] * 2,
        out_specs=(vmem(), vmem()) + (anywhere(),) * 2,
        input_output_aliases={3 + k: 2 + k for k in range(2)},
        compiler_params=params(),
        name="sum_middle",
    )(pieces, hidden, plan, *blocks)


def gather_rows(spread):
    return pl.pallas_call(
        gather_kernel,
        out_shape=(
            shape(PLANE, BLOCK, QUARTER),
            shape(PLANE, TOKENS, dtype=jnp.float32),
            shape(PLANE, TOKENS, dtype=jnp.float32),
        ),
        in_specs=[vmem()],
        out_specs=(vmem(), vmem(), vmem()),
        scratch_shapes=[
            pltpu.VMEM((PLANE * BLOCK, TOKENS), jnp.bfloat16),
            pltpu.VMEM((TOKENS, QUARTER), jnp.bfloat16),
        ],
        compiler_params=params(),
        name="gather_rows",
    )(spread)


def hold(after, blocks):
    return pl.pallas_call(
        hold_kernel,
        out_shape=tuple(shape(*block.shape) for block in blocks),
        in_specs=[anywhere()] * 3,
        out_specs=(anywhere(),) * 2,
        input_output_aliases={1 + k: k for k in range(2)},
        compiler_params=params(),
        name="hold",
    )(after, *blocks)


def combine_rows(target, gate, rows):
    return pl.pallas_call(
        combine_kernel,
        out_shape=shape(NZ, REQ, QUARTER),
        in_specs=[vmem(), vmem(), vmem()],
        out_specs=vmem(),
        scratch_shapes=[
            pltpu.VMEM((PLANE * BLOCK, TOKENS), jnp.bfloat16),
            pltpu.VMEM((PLANE * BLOCK, QUARTER), jnp.bfloat16),
        ],
        compiler_params=params(),
        name="combine_rows",
    )(target, gate, rows)


def run_expert(rows, gain, blocks):
    return pl.pallas_call(
        expert_kernel,
        out_shape=shape(PLANE, BLOCK, QUARTER),
        in_specs=[vmem(), vmem()] + [anywhere()] * 4,
        out_specs=vmem(),
        scratch_shapes=[
            pltpu.VMEM((NX * BLOCK, WIDTH), jnp.bfloat16),
            pltpu.VMEM((3, 4 * EHQ, WIDTH), jnp.bfloat16),
            pltpu.VMEM((NX * BLOCK, 4 * EHQ), jnp.bfloat16),
            pltpu.SemaphoreType.DMA((3, 4)),
        ],
        compiler_params=params(32),
        name="expert",
    )(rows, gain, *blocks)


def move_weights(blocks):
    even, odd = [], []
    for c in range(NC):
        for y in range(NY):
            core = (y // 2) * NY
            even.append((c * NY + y, core + 2 * c + y % 2))
            odd.append((c * NY + y, core + 2 * c + 1 - y % 2))
    return [lax.ppermute(block, ("c", "y"), to) for block, to in zip(blocks, (even, odd))]


def talker_plan(owners, section):
    own = lax.dynamic_slice_in_dim(owners, section * REQ, REQ)
    order = jnp.arange(REQ, dtype=jnp.int32)
    same = (own[:, None] == own[None, :]) & (order[:, None] > order[None, :])
    position = jnp.sum(same.astype(jnp.int32), axis=1)
    slot = jnp.where(own >= 0, own * HCAP + position, -1)
    send = (jnp.arange(SECTIONS * HCAP, dtype=jnp.int32)[:, None] == slot[None, :]).astype(
        jnp.bfloat16
    )
    counts = jnp.sum((owners == section).reshape(SECTIONS, REQ).astype(jnp.int32), axis=1)
    place = jnp.arange(SECTIONS, dtype=jnp.int32)
    offsets = jnp.sum(jnp.where(place[None, :] < place[:, None], counts[None, :], 0), axis=1)
    index = jnp.arange(HCAP, dtype=jnp.int32)
    put = jnp.where(index[None, :] < counts[:, None], offsets[:, None] + index[None, :], -1)
    put = put.reshape(SECTIONS * HCAP)
    take = (jnp.arange(SECTIONS * HCAP, dtype=jnp.int32)[:, None] == put[None, :]).astype(
        jnp.bfloat16
    )
    return send, take


def local(
    hidden_in,
    queries,
    new_kv,
    cache,
    lengths,
    out_weight,
    moe_gain,
    expert_ids,
    expert_gates,
    gate_up,
    down,
    owners,
):
    z, x, c, y = (lax.axis_index(name) for name in ("z", "x", "c", "y"))
    section = (z * NX + x) * NC + c
    plan = make_plan(expert_ids.T, expert_gates.T)
    context = attend_local(queries, new_kv, cache, lengths)
    attention = jnp.dot(context, out_weight, preferred_element_type=jnp.float32)
    pieces = attention.astype(jnp.bfloat16).reshape(REQ, NY, QUARTER).transpose(1, 0, 2)
    first = (y % 2).astype(jnp.int32).reshape(1)
    blocks = pick_weights(first, pieces, gate_up.transpose(0, 1, 3, 2), down)
    pieces = lax.all_to_all(pieces, "y", 0, 0, tiled=True)
    hidden = lax.dynamic_slice_in_dim(hidden_in, y * QUARTER, QUARTER, 1)
    message, middle, *blocks = sum_middle(pieces, hidden, plan, blocks)
    blocks = move_weights(blocks)

    spread = lax.all_to_all(message, "z", 0, 0, tiled=True)
    send, target, gate = gather_rows(spread)
    blocks = hold(send, blocks)
    swapped = [lax.ppermute(block, "c", [(0, 1), (1, 0)]) for block in blocks]
    rows = lax.all_to_all(send, ("x", "y"), 0, 0, tiled=True)
    done = run_expert(rows, moe_gain.reshape(1, WIDTH), (*blocks, *swapped))
    back = lax.all_to_all(done, ("x", "y"), 0, 0, tiled=True)
    part = combine_rows(target, gate, back)
    part = lax.all_to_all(part, "z", 0, 0, tiled=True)
    out = middle.astype(jnp.float32) + jnp.sum(part.astype(jnp.float32), axis=0)
    out = out.astype(jnp.bfloat16)

    send_pick, take_pick = talker_plan(owners, section)
    leaving = jnp.dot(send_pick, out, preferred_element_type=jnp.float32).astype(jnp.bfloat16)
    arrived = lax.all_to_all(
        leaving.reshape(SECTIONS, HCAP, QUARTER), ("z", "x", "c"), 0, 0, tiled=True
    )
    talker = jnp.dot(
        take_pick, arrived.reshape(SECTIONS * HCAP, QUARTER), preferred_element_type=jnp.float32
    ).astype(jnp.bfloat16)
    return (out, talker)


def solution(mesh):
    section = ("z", "x", "c")
    fine = Mesh(mesh.devices.reshape(NZ, NX, NC, NY), ("z", "x", "c", "y"))
    in_specs = (
        P(section, None),
        P(section, "y"),
        P(section, None, "y"),
        P(section, None, None, "y"),
        P(section),
        P("y", None),
        P(),
        P(section, None),
        P(section, None),
        P(section, None, None, "y"),
        P(section, "y", None),
        P(),
    )
    out_specs = (P(section, "y"), P(section, "y"))
    return jax.shard_map(local, mesh=fine, in_specs=in_specs, out_specs=out_specs, check_vma=False)
```

time: 193 us -> 180 us (0.933)
  blocking collectives: 21.4 us -> 70.7 us
  starting transfers between devices: 55.4 us -> 29.4 us
  waiting for transfers between devices: 68.5 us -> 49.7 us
  local copies, waits for them, and re-layouts: 18 us -> 8.22 us
  Pallas kernels: 17.7 us -> 10.8 us
  other arithmetic: 6.17 us -> 2.56 us
  matrix products: 3.63 us -> 6.6 us
    all_to_all x0 -> x2, blocking collectives: none -> 49.9 us  [the longest x1 27.5 us: local(): spread = lax.all_to_all(message, 'z', 0, 0, tiled=True)]
    all_to_all x1, waiting for transfers between devices: 24.1 us -> 0.13 us  [local(): pieces = lax.all_to_all(pieces, 'y', 0, 0, tiled=True)]
    ppermute x8 -> x4, waiting for transfers between devices: 2.22 us -> 25 us  [the longest x2 25 us: move_weights(): lax.ppermute(block, ('c', 'y'), to)]
    all_to_all x4 -> x1, waiting for transfers between devices: 31.2 us -> 13.5 us  [local(): part = lax.all_to_all(part, 'z', 0, 0, tiled=True)]
    all_to_all x4 -> x1, starting transfers between devices: 23.2 us -> 8.18 us  [local(): part = lax.all_to_all(part, 'z', 0, 0, tiled=True)]
    ppermute x8 -> x4, starting transfers between devices: 18 us -> 7.75 us  [the longest x2 7.24 us: move_weights(): lax.ppermute(block, ('c', 'y'), to)]
    pallas_call x4 -> x7, Pallas kernels: 17.7 us -> 10.8 us  [the longest x1 5.55 us: run_expert(): pl.pallas_call(expert_kernel, out_shape=shape(PLANE, BLOCK, QUARTER), in_...]
    concatenate x2 -> x0, other arithmetic: 3.51 us -> none  [expert_weights(): gate_block = jnp.concatenate([chosen[0], chosen[1]], axis=1)]
  transfers between devices with their start and end apart: 14 -> 7, of which waited for: 7 -> 5; matrix products, arithmetic and copies ran while one was open for 8% -> 0% of each run, Pallas kernels for 2% -> 1%
where the time goes in v2:
time: 180 us; the launch traced here: 179 us
  blocking collectives  70.7 us (39%)
  waiting for transfers between devices  49.7 us (28%)
  starting transfers between devices  29.4 us (16%)
  Pallas kernels  10.8 us (6%)
  local copies, waits for them, and re-layouts  8.22 us (5%)
  matrix products  6.6 us (4%)
  other arithmetic  2.56 us (1%)
    all_to_all x1, blocking collectives, local(): spread = lax.all_to_all(message, 'z', 0, 0, tiled=True)  27.5 us
    ppermute x2, waiting for transfers between devices, move_weights(): lax.ppermute(block, ('c', 'y'), to)  25 us
    all_to_all x1, blocking collectives, local(): rows = lax.all_to_all(send, ('x', 'y'), 0, 0, tiled=True)  22.4 us
    all_to_all x1, blocking collectives, local(): back = lax.all_to_all(done, ('x', 'y'), 0, 0, tiled=True)  20.8 us
    all_to_all x1, waiting for transfers between devices, local(): part = lax.all_to_all(part, 'z', 0, 0, tiled=True)  13.5 us
    all_to_all x1, waiting for transfers between devices, local(): lax.all_to_all(leaving.reshape(SECTIONS, HCAP, QUARTER), ('z', 'x', 'c'),...  11 us
    all_to_all x1, starting transfers between devices, local(): lax.all_to_all(leaving.reshape(SECTIONS, HCAP, QUARTER), ('z', 'x', 'c'),...  8.43 us
    all_to_all x1, starting transfers between devices, local(): part = lax.all_to_all(part, 'z', 0, 0, tiled=True)  8.18 us
  transfers between devices with their start and end apart: 7, of which 5 were waited for; matrix products, arithmetic and copies ran while one was open for 0% of the time, Pallas kernels for 1%

profile of v2, /device:TPU:1, one launch (start us, length us, event | category | flops | bytes accessed | tf_op | source)
XLA Modules:
  0.0 178.8 jit_solution(10018264882324150840)
XLA Ops:
  0.6 1.0 copy.34
  2.4 0.9 fusion.30
  3.5 2.6 %fusion.31 = (f32[64,8]{1,0:T(8,128)S(1)}, f32[64,8,96]{2,1,0:T(8,128)S(1)}) fusion(bf16[64,8,128]{2,1,0:T(8,128)(2,1)S(1)} %bitcast.58, bf16[64,2,96,128]{3,2,1,0:T(8,128)(2,1)} %param.15, pred[64,96]{1,0:T(8,128)(4,1)S(1)} %iota_compare_fusion.7), kind=kOutput, calls=%fused_computation.48 | convolution fusion | flops 12729856 | bytes 1908736 | tf_op jit(solution)/shard_map/rkgd,rckd->rkgc/dot_general | solution.py:37
  6.3 2.0 %fusion.15 = bf16[64,8,128]{2,1,0:T(8,128)(2,1)S(1)} fusion(bf16[64,2,96,128]{3,2,1,0:T(8,128)(2,1)} %param.15, f32[64,8,96]{2,1,0:T(8,128)S(1)} %get-tuple-element.29, f32[64,128]{1,0:T(8,128)S(1)} %bitcast.63, f32[64,8]{1,0:T(8,128)S(1)} %get-tuple-element.25, f32[64,8]{1,0:T(8,128)S(1)} %get-tuple-element.24, f32[64,8]{1,0:T(8,128)S(1)} %multiply_maximum_fusion), kind=kOutput, calls=%fused_computation.11 | convolution fusion | flops 12926976 | bytes 1939456 | tf_op jit(solution)/shard_map/rkgc,rckd->rkgd/dot_general | solution.py:52
  8.4 0.8 convolution_convert_fusion
  9.9 5.0 %all-to-all-start = ((bf16[4,64,512]{2,1,0:T(8,128)(2,1)}), bf16[4,64,512]{2,1,0:T(8,128)(2,1)}, u32[]{:S(2)}, u32[]{:S(2)}) async-start(bf16[4,64,512]{2,1,0:T(8,128)(2,1)} %bitcast.51), calls=%async_computation | async-start | bytes 524288 | tf_op jit(solution)/shard_map/all_to_all | solution.py:375
  15.2 0.9 copy-done.2
  16.2 1.4 copy-done.5
  17.6 1.4 pick_weights.1
  19.1 1.4 copy-done.3
  20.6 1.7 copy-done.4
  22.3 1.0 sum_middle.1
  23.3 7.1 %collective-permute-start = (bf16[3,192,2048]{2,1,0:T(8,128)(2,1)}, bf16[3,192,2048]{2,1,0:T(8,128)(2,1)S(1)}, u32[]{:S(2)}, u32[]{:S(2)}) collective-permute-start(bf16[3,192,2048]{2,1,0:T(8,128)(2,1)} %get-tuple-element.20), channel_id=1, source_target_pairs={{0,0},{1,1},{2,4},{3,5},{4,2},{5,3},{6,6},{7,7},{8,8},{9,9},{10,12... | collective-permute-start | bytes 7077896 | tf_op jit(solution)/shard_map/ppermute | solution.py:329
  30.5 27.5 %all_to_all.30.spread_ref = bf16[8,80,512]{2,1,0:T(8,128)(2,1)S(1)} all-to-all(bf16[8,80,512]{2,1,0:T(8,128)(2,1)S(1)} %get-tuple-element.16), channel_id=1, replica_groups=mesh['z'=8,'x'=4,'c'=2,'y'=4] {'z'}, dimensions={0} | all-to-all | bytes 1310720 | tf_op jit(solution)/shard_map/all_to_all | solution.py:380
  58.9 22.2 %collective-permute-done.refs_1_ = bf16[3,192,2048]{2,1,0:T(8,128)(2,1)S(1)} collective-permute-done((bf16[3,192,2048]{2,1,0:T(8,128)(2,1)}, bf16[3,192,2048]{2,1,0:T(8,128)(2,1)S(1)}, u32[]{:S(2)}, u32[]{:S(2)}) %collective-permute-start) | collective-permute-done | bytes 2359328 | tf_op jit(solution)/shard_map/ppermute | solution.py:329
  81.1 2.8 %collective-permute-done.1.refs_2_ = bf16[3,192,2048]{2,1,0:T(8,128)(2,1)S(1)} collective-permute-done((bf16[3,192,2048]{2,1,0:T(8,128)(2,1)S(1)}, bf16[3,192,2048]{2,1,0:T(8,128)(2,1)S(1)}, u32[]{:S(2)}, u32[]{:S(2)}) %collective-permute-start.1) | collective-permute-done | bytes 2359328 | tf_op jit(solution)/shard_map/ppermute | solution.py:329
  84.4 22.4 %all_to_all.31.rows_ref = bf16[16,80,512]{2,1,0:T(8,128)(2,1)S(1)} all-to-all(bf16[16,80,512]{2,1,0:T(8,128)(2,1)S(1)} %get-tuple-element.19.refs_0_), channel_id=1, replica_groups=mesh['z'=8,'x'=4,'c'=2,'y'=4] {'x','y'}, dimensions={0} | all-to-all | bytes 2621440 | tf_op jit(solution)/shard_map/all_to_all | solution.py:384
  106.8 5.6 %expert.1 = bf16[16,80,512]{2,1,0:T(8,128)(2,1)S(1)} custom-call(bf16[16,80,512]{2,1,0:T(8,128)(2,1)S(1)} %all_to_all.31.rows_ref, f32[1,2048]{1,0:T(1,128)S(1)} %bitcast.53, bf16[3,192,2048]{2,1,0:T(8,128)(2,1)S(1)} %get-tuple-element.22.w0, bf16[3,192,2048]{2,1,0:T(8,128)(2,1)S(1)} %get-tuple-element.23.w1, ...), custom_call_target="tpu_custom_call" | custom-call | tf_op jit(solution)/shard_map/expert/pallas_call | solution.py:306
  112.4 20.8 %all_to_all.32.rows_ref = bf16[16,80,512]{2,1,0:T(8,128)(2,1)S(1)} all-to-all(bf16[16,80,512]{2,1,0:T(8,128)(2,1)S(1)} %expert.1), channel_id=1, replica_groups=mesh['z'=8,'x'=4,'c'=2,'y'=4] {'x','y'}, dimensions={0} | all-to-all | bytes 2621440 | tf_op jit(solution)/shard_map/all_to_all | solution.py:386
  133.2 1.7 combine_rows.1
  134.9 8.2 %all-to-all-start.4 = ((bf16[8,64,512]{2,1,0:T(8,128)(2,1)}), bf16[8,64,512]{2,1,0:T(8,128)(2,1)S(1)}, u32[]{:S(2)}, u32[]{:S(2)}) async-start(bf16[8,64,512]{2,1,0:T(8,128)(2,1)} %combine_rows.1), calls=%async_computation.4 | async-start | bytes 1048576 | tf_op jit(solution)/shard_map/all_to_all | solution.py:388
  143.6 13.5 %all-to-all-done.4 = bf16[8,64,512]{2,1,0:T(8,128)(2,1)S(1)} async-done(((bf16[8,64,512]{2,1,0:T(8,128)(2,1)}), bf16[8,64,512]{2,1,0:T(8,128)(2,1)S(1)}, u32[]{:S(2)}, u32[]{:S(2)}) %all-to-all-start.4) | async-done | bytes 524320 | tf_op jit(solution)/shard_map/all_to_all | solution.py:388
  158.1 8.4 %all-to-all-start.5 = ((bf16[64,2,512]{2,1,0:T(2,128)(2,1)}), bf16[64,2,512]{2,1,0:T(2,128)(2,1)S(1)}, u32[]{:S(2)}, u32[]{:S(2)}) async-start(bf16[64,2,512]{2,1,0:T(2,128)(2,1)} %reshape.149), calls=%async_computation.5 | async-start | bytes 262144 | tf_op jit(solution)/shard_map/all_to_all | solution.py:394
  166.9 11.0 %all-to-all-done.5 = bf16[64,2,512]{2,1,0:T(2,128)(2,1)S(1)} async-done(((bf16[64,2,512]{2,1,0:T(2,128)(2,1)}), bf16[64,2,512]{2,1,0:T(2,128)(2,1)S(1)}, u32[]{:S(2)}, u32[]{:S(2)}) %all-to-all-start.5) | async-done | bytes 131104 | tf_op jit(solution)/shard_map/all_to_all | solution.py:394
  (52 shorter events, 6.6 us)
Async XLA Ops:
  0.6 19.8 %copy-start = (bf16[64,2048]{1,0:T(8,128)(2,1)S(1)}, bf16[64,2048]{1,0:T(8,128)(2,1)}, u32[]{:S(2)}) copy-start(bf16[64,2048]{1,0:T(8,128)(2,1)} %param.12) | copy-start | bytes 786436
  3.5 4.9 %copy-start.9 = (bf16[1024,2048]{1,0:T(8,128)(2,1)S(1)}, bf16[1024,2048]{1,0:T(8,128)(2,1)}, u32[]{:S(2)}) copy-start(bf16[1024,2048]{1,0:T(8,128)(2,1)} %param.17) | copy-start | bytes 12582916
  8.3 6.6 %copy-start.7 = (s32[64,8]{0,1:T(8,128)S(1)}, s32[64,8]{0,1:T(8,128)}, u32[]{:S(2)}) copy-start(s32[64,8]{0,1:T(8,128)} %param.19) | copy-start | bytes 6148
  8.3 6.6 %copy-start.8 = (f32[64,8]{0,1:T(8,128)S(1)}, f32[64,8]{0,1:T(8,128)}, u32[]{:S(2)}) copy-start(f32[64,8]{0,1:T(8,128)} %param.20) | copy-start | bytes 6148
  8.4 6.9 %copy-start.1 = (bf16[2,2,2048,192]{2,3,1,0:T(8,128)(2,1)S(1)}, bf16[2,2,2048,192]{2,3,1,0:T(8,128)(2,1)}, u32[]{:S(2)}) copy-start(bf16[2,2,2048,192]{2,3,1,0:T(8,128)(2,1)} %param.21) | copy-start | bytes 9437188
  9.9 10.6 %all-to-all-start = ((bf16[4,64,512]{2,1,0:T(8,128)(2,1)}), bf16[4,64,512]{2,1,0:T(8,128)(2,1)}, u32[]{:S(2)}, u32[]{:S(2)}) async-start(bf16[4,64,512]{2,1,0:T(8,128)(2,1)} %bitcast.51), calls=%async_computation | async-start | bytes 524288 | tf_op jit(solution)/shard_map/all_to_all | solution.py:375
  15.2 1.0 copy-start.2
  16.2 1.4 copy-start.5
  19.0 1.4 copy-start.3
  20.6 1.7 copy-start.4
  23.3 57.8 %collective-permute-start = (bf16[3,192,2048]{2,1,0:T(8,128)(2,1)}, bf16[3,192,2048]{2,1,0:T(8,128)(2,1)S(1)}, u32[]{:S(2)}, u32[]{:S(2)}) collective-permute-start(bf16[3,192,2048]{2,1,0:T(8,128)(2,1)} %get-tuple-element.20), channel_id=1, source_target_pairs={{0,0},{1,1},{2,4},{3,5},{4,2},{5,3},{6,6},{7,7},{8,8},{9,9},{10,12... | collective-permute-start | bytes 7077896 | tf_op jit(solution)/shard_map/ppermute | solution.py:329
  30.4 53.5 %collective-permute-start.1 = (bf16[3,192,2048]{2,1,0:T(8,128)(2,1)S(1)}, bf16[3,192,2048]{2,1,0:T(8,128)(2,1)S(1)}, u32[]{:S(2)}, u32[]{:S(2)}) collective-permute-start(bf16[3,192,2048]{2,1,0:T(8,128)(2,1)S(1)} %get-tuple-element.21), channel_id=1, source_target_pairs={{0,1},{1,0},{2,5},{3,4},{4,3},{5,2},{6,7},{7,6},{8,9},{9,8},{10,13... | collective-permute-start | bytes 7077896 | tf_op jit(solution)/shard_map/ppermute | solution.py:329
  83.9 22.9 %copy-start.6 = (f32[2048]{0:T(1024)S(1)}, f32[2048]{0:T(1024)}, u32[]{:S(2)}) copy-start(f32[2048]{0:T(1024)} %param.18) | copy-start | bytes 24580
  83.9 22.9 %collective-permute-start.2 = (bf16[3,192,2048]{2,1,0:T(8,128)(2,1)S(1)}, bf16[3,192,2048]{2,1,0:T(8,128)(2,1)S(1)}, u32[]{:S(2)}, u32[]{:S(2)}) collective-permute-start(bf16[3,192,2048]{2,1,0:T(8,128)(2,1)S(1)} %get-tuple-element.22.w0), channel_id=1, source_target_pairs={{0,4},{4,0},{1,5},{5,1},{2,6},{6,2},{3,7},{7,3},{8,12},{12,8},{9,1... | collective-permute-start | bytes 7077896 | tf_op jit(solution)/shard_map/ppermute | solution.py:383
  83.9 22.9 %collective-permute-start.3 = (bf16[3,192,2048]{2,1,0:T(8,128)(2,1)S(1)}, bf16[3,192,2048]{2,1,0:T(8,128)(2,1)S(1)}, u32[]{:S(2)}, u32[]{:S(2)}) collective-permute-start(bf16[3,192,2048]{2,1,0:T(8,128)(2,1)S(1)} %get-tuple-element.23.w1), channel_id=1, source_target_pairs={{0,4},{4,0},{1,5},{5,1},{2,6},{6,2},{3,7},{7,3},{8,12},{12,8},{9,1... | collective-permute-start | bytes 7077896 | tf_op jit(solution)/shard_map/ppermute | solution.py:383
  112.4 30.7 %copy-start.11 = (s32[4096]{0:T(1024)S(1)}, s32[4096]{0:T(1024)}, u32[]{:S(2)}) copy-start(s32[4096]{0:T(1024)} %param.23) | copy-start | bytes 49156
  134.9 22.2 %all-to-all-start.4 = ((bf16[8,64,512]{2,1,0:T(8,128)(2,1)}), bf16[8,64,512]{2,1,0:T(8,128)(2,1)S(1)}, u32[]{:S(2)}, u32[]{:S(2)}) async-start(bf16[8,64,512]{2,1,0:T(8,128)(2,1)} %combine_rows.1), calls=%async_computation.4 | async-start | bytes 1048576 | tf_op jit(solution)/shard_map/all_to_all | solution.py:388
  157.2 21.6 %copy-start.10 = (bf16[64,512]{1,0:T(8,128)(2,1)}, bf16[64,512]{1,0:T(8,128)(2,1)S(1)}, u32[]{:S(2)}) copy-start(bf16[64,512]{1,0:T(8,128)(2,1)S(1)} %add_convert_fusion) | copy-start | bytes 196612
  158.1 19.8 %all-to-all-start.5 = ((bf16[64,2,512]{2,1,0:T(2,128)(2,1)}), bf16[64,2,512]{2,1,0:T(2,128)(2,1)S(1)}, u32[]{:S(2)}, u32[]{:S(2)}) async-start(bf16[64,2,512]{2,1,0:T(2,128)(2,1)} %reshape.149), calls=%async_computation.5 | async-start | bytes 262144 | tf_op jit(solution)/shard_map/all_to_all | solution.py:394

commit v3 on v2

--- a/solution.py
+++ b/solution.py
@@ -98,8 +98,7 @@
         copy.wait()
 
 
-def middle_kernel(pieces_ref, hidden_ref, plan_ref, *refs):
-    message_ref, middle_ref = refs[2:4]
+def middle_kernel(pieces_ref, hidden_ref, plan_ref, message_ref, middle_ref):
     total = hidden_ref[...].astype(jnp.float32)
     for y in range(NY):
         total = total + pieces_ref[y].astype(jnp.float32)
@@ -157,11 +156,10 @@
         out_ref[z] = total[z * REQ : (z + 1) * REQ, :]
 
 
-def expert_kernel(rows_ref, gain_ref, w0, w1, w2, w3, out_ref, *scratch):
-    normed_ref, weight_ref, act_ref, sems = scratch
+def load_weights(blocks, weight_ref, sems):
     copies = []
     for part in range(3):
-        for q, block in enumerate((w0, w1, w2, w3)):
+        for q, block in enumerate(blocks):
             copies.append(
                 pltpu.make_async_copy(
                     block.at[part], weight_ref.at[part, pl.ds(q * EHQ, EHQ)], sems.at[part, q]
@@ -169,6 +167,26 @@
             )
     for copy in copies:
         copy.start()
+    return copies
+
+
+def activate(normed_ref, weight_ref, act_ref, copies):
+    dims = (((1,), (1,)), ((), ()))
+    for copy in copies[:2]:
+        copy.wait()
+    gate = lax.dot_general(
+        normed_ref[...], weight_ref[0], dims, preferred_element_type=jnp.float32
+    )
+    for copy in copies[2:4]:
+        copy.wait()
+    up = lax.dot_general(normed_ref[...], weight_ref[1], dims, preferred_element_type=jnp.float32)
+    act_ref[...] = (gate / (1.0 + jnp.exp(-gate)) * up).astype(jnp.bfloat16)
+    for copy in copies[4:]:
+        copy.wait()
+
+
+def first_half_kernel(rows_ref, gain_ref, w0, w1, normed_ref, part_ref, weight_ref, act_ref, sems):
+    copies = load_weights((w0, w1), weight_ref, sems)
     for x in range(NX):
         parts = [rows_ref[x * NY + y].astype(jnp.float32) for y in range(NY)]
         square = sum(jnp.sum(part * part, axis=-1, keepdims=True) for part in parts)
@@ -178,24 +196,19 @@
             normed_ref[x * BLOCK : (x + 1) * BLOCK, columns] = (
                 parts[y] * scale * gain_ref[:, columns]
             ).astype(jnp.bfloat16)
-    dims = (((1,), (1,)), ((), ()))
-    for copy in copies[:4]:
-        copy.wait()
-    gate = lax.dot_general(
-        normed_ref[...], weight_ref[0], dims, preferred_element_type=jnp.float32
-    )
-    for copy in copies[4:8]:
-        copy.wait()
-    up = lax.dot_general(normed_ref[...], weight_ref[1], dims, preferred_element_type=jnp.float32)
-    act_ref[...] = (gate / (1.0 + jnp.exp(-gate)) * up).astype(jnp.bfloat16)
-    for copy in copies[8:]:
-        copy.wait()
+    activate(normed_ref, weight_ref, act_ref, copies)
+    part_ref[...] = jnp.dot(act_ref[...], weight_ref[2], preferred_element_type=jnp.float32)
+
+
+def second_half_kernel(normed_ref, part_ref, w2, w3, out_ref, weight_ref, act_ref, sems):
+    copies = load_weights((w2, w3), weight_ref, sems)
+    activate(normed_ref, weight_ref, act_ref, copies)
     for y in range(NY):
-        part = jnp.dot(
-            act_ref[...],
-            weight_ref[2, :, y * QUARTER : (y + 1) * QUARTER],
-            preferred_element_type=jnp.float32,
-        ).astype(jnp.bfloat16)
+        columns = slice(y * QUARTER, (y + 1) * QUARTER)
+        part = part_ref[:, columns] + jnp.dot(
+            act_ref[...], weight_ref[2, :, columns], preferred_element_type=jnp.float32
+        )
+        part = part.astype(jnp.bfloat16)
         for x in range(NX):
             out_ref[x * NY + y] = part[x * BLOCK : (x + 1) * BLOCK, :]
 
@@ -232,7 +245,8 @@
     return pl.pallas_call(
         pick_kernel,
         out_shape=(block, block),
-        in_specs=[pl.BlockSpec(memory_space=pltpu.SMEM)] + [anywhere()] * 3,
+        in_specs=[pl.BlockSpec(memory_space=pltpu.SMEM), anywhere()]
+        + [pl.BlockSpec(memory_space=pltpu.HBM)] * 2,
         out_specs=(anywhere(), anywhere()),
         scratch_shapes=[pltpu.SemaphoreType.DMA((4,))],
         compiler_params=params(),
@@ -240,20 +254,15 @@
     )(first, after, gate_up, down)
 
 
-def sum_middle(pieces, hidden, plan, blocks):
+def sum_middle(pieces, hidden, plan):
     return pl.pallas_call(
         middle_kernel,
-        out_shape=(
-            shape(NZ, REQ + PLANE, QUARTER),
-            shape(REQ, QUARTER),
-            *[shape(*block.shape) for block in blocks],
-        ),
-        in_specs=[vmem()] * 3 + [anywhere()] * 2,
-        out_specs=(vmem(), vmem()) + (anywhere(),) * 2,
-        input_output_aliases={3 + k: 2 + k for k in range(2)},
+        out_shape=(shape(NZ, REQ + PLANE, QUARTER), shape(REQ, QUARTER)),
+        in_specs=[vmem()] * 3,
+        out_specs=(vmem(), vmem()),
         compiler_params=params(),
         name="sum_middle",
-    )(pieces, hidden, plan, *blocks)
+    )(pieces, hidden, plan)
 
 
 def gather_rows(spread):
@@ -302,21 +311,36 @@
     )(target, gate, rows)
 
 
-def run_expert(rows, gain, blocks):
-    return pl.pallas_call(
-        expert_kernel,
+def half_scratch():
+    return [
+        pltpu.VMEM((3, 2 * EHQ, WIDTH), jnp.bfloat16),
+        pltpu.VMEM((NX * BLOCK, 2 * EHQ), jnp.bfloat16),
+        pltpu.SemaphoreType.DMA((3, 2)),
+    ]
+
+
+def first_half(rows, gain, blocks):
+    return pl.pallas_call(
+        first_half_kernel,
+        out_shape=(shape(NX * BLOCK, WIDTH), shape(NX * BLOCK, WIDTH, dtype=jnp.float32)),
+        in_specs=[vmem(), vmem()] + [anywhere()] * 2,
+        out_specs=(vmem(), vmem()),
+        scratch_shapes=half_scratch(),
+        compiler_params=params(24),
+        name="first_half",
+    )(rows, gain, *blocks)
+
+
+def second_half(normed, part, blocks):
+    return pl.pallas_call(
+        second_half_kernel,
         out_shape=shape(PLANE, BLOCK, QUARTER),
-        in_specs=[vmem(), vmem()] + [anywhere()] * 4,
+        in_specs=[vmem(), vmem()] + [anywhere()] * 2,
         out_specs=vmem(),
-        scratch_shapes=[
-            pltpu.VMEM((NX * BLOCK, WIDTH), jnp.bfloat16),
-            pltpu.VMEM((3, 4 * EHQ, WIDTH), jnp.bfloat16),
-            pltpu.VMEM((NX * BLOCK, 4 * EHQ), jnp.bfloat16),
-            pltpu.SemaphoreType.DMA((3, 4)),
-        ],
-        compiler_params=params(32),
-        name="expert",
-    )(rows, gain, *blocks)
+        scratch_shapes=half_scratch(),
+        compiler_params=params(24),
+        name="second_half",
+    )(normed, part, *blocks)
 
 
 def move_weights(blocks):
@@ -374,15 +398,16 @@
     blocks = pick_weights(first, pieces, gate_up.transpose(0, 1, 3, 2), down)
     pieces = lax.all_to_all(pieces, "y", 0, 0, tiled=True)
     hidden = lax.dynamic_slice_in_dim(hidden_in, y * QUARTER, QUARTER, 1)
-    message, middle, *blocks = sum_middle(pieces, hidden, plan, blocks)
+    message, middle = sum_middle(pieces, hidden, plan)
     blocks = move_weights(blocks)
 
     spread = lax.all_to_all(message, "z", 0, 0, tiled=True)
     send, target, gate = gather_rows(spread)
-    blocks = hold(send, blocks)
+    rows = lax.all_to_all(send, ("x", "y"), 0, 0, tiled=True)
+    blocks = hold(rows, blocks)
     swapped = [lax.ppermute(block, "c", [(0, 1), (1, 0)]) for block in blocks]
-    rows = lax.all_to_all(send, ("x", "y"), 0, 0, tiled=True)
-    done = run_expert(rows, moe_gain.reshape(1, WIDTH), (*blocks, *swapped))
+    normed, half = first_half(rows, moe_gain.reshape(1, WIDTH), blocks)
+    done = second_half(normed, half, swapped)
     back = lax.all_to_all(done, ("x", "y"), 0, 0, tiled=True)
     part = combine_rows(target, gate, back)
     part = lax.all_to_all(part, "z", 0, 0, tiled=True)

time: 180 us -> 191 us (1.061)
  blocking collectives: 70.7 us -> 25.1 us
  waiting for transfers between devices: 49.7 us -> 85.9 us
  starting transfers between devices: 29.4 us -> 44.5 us
  Pallas kernels: 10.8 us -> 15.2 us
    all_to_all x2 -> x0, blocking collectives: 49.9 us -> none  [the longest x1 27.5 us: local(): spread = lax.all_to_all(message, 'z', 0, 0, tiled=True)]
    all_to_all x0 -> x2, starting transfers between devices: none -> 19.4 us  [the longest x1 11.2 us: local(): rows = lax.all_to_all(send, ('x', 'y'), 0, 0, tiled=True)]
    ppermute x2, waiting for transfers between devices: 25 us -> 41.4 us  [move_weights(): lax.ppermute(block, ('c', 'y'), to)]
    all_to_all x0 -> x2, waiting for transfers between devices: none -> 9.97 us  [the longest x1 8.76 us: local(): spread = lax.all_to_all(message, 'z', 0, 0, tiled=True)]
    all_to_all x1, waiting for transfers between devices: 0.13 us -> 4.72 us  [local(): pieces = lax.all_to_all(pieces, 'y', 0, 0, tiled=True)]
    all_to_all x1, blocking collectives: 20.8 us -> 25.1 us  [local(): back = lax.all_to_all(done, ('x', 'y'), 0, 0, tiled=True)]
    ppermute x2, waiting for transfers between devices: 0.01 us -> 3.71 us  [local(): swapped = [lax.ppermute(block, 'c', [(0, 1), (1, 0)]) for block in blocks]]
    pallas_call x1, Pallas kernels: 0.84 us -> 3.03 us  [gather_rows(): pl.pallas_call(gather_kernel, out_shape=(shape(PLANE, BLOCK, QUARTER), sh...]
  transfers between devices with their start and end apart: 7 -> 9, of which waited for: 5 -> 9; matrix products, arithmetic and copies ran while one was open for 0% -> 1% of each run, Pallas kernels for 1% -> 5%
where the time goes in v3:
time: 191 us; the launch traced here: 189 us
  waiting for transfers between devices  85.9 us (45%)
  starting transfers between devices  44.5 us (23%)
  blocking collectives  25.1 us (13%)
  Pallas kernels  15.2 us (8%)
  local copies, waits for them, and re-layouts  8.14 us (4%)
  matrix products  6.6 us (3%)
  other arithmetic  2.56 us (1%)
    ppermute x2, waiting for transfers between devices, move_weights(): lax.ppermute(block, ('c', 'y'), to)  41.4 us
    all_to_all x1, blocking collectives, local(): back = lax.all_to_all(done, ('x', 'y'), 0, 0, tiled=True)  25.1 us
    all_to_all x1, waiting for transfers between devices, local(): part = lax.all_to_all(part, 'z', 0, 0, tiled=True)  15.2 us
    all_to_all x1, starting transfers between devices, local(): rows = lax.all_to_all(send, ('x', 'y'), 0, 0, tiled=True)  11.2 us
    all_to_all x1, waiting for transfers between devices, local(): lax.all_to_all(leaving.reshape(SECTIONS, HCAP, QUARTER), ('z', 'x', 'c'),...  11 us
    all_to_all x1, waiting for transfers between devices, local(): spread = lax.all_to_all(message, 'z', 0, 0, tiled=True)  8.76 us
    all_to_all x1, starting transfers between devices, local(): spread = lax.all_to_all(message, 'z', 0, 0, tiled=True)  8.21 us
    all_to_all x1, starting transfers between devices, local(): part = lax.all_to_all(part, 'z', 0, 0, tiled=True)  6.94 us
  transfers between devices with their start and end apart: 9, of which 9 were waited for; matrix products, arithmetic and copies ran while one was open for 1% of the time, Pallas kernels for 5%

profile of v3, /device:TPU:1, one launch (start us, length us, event | category | flops | bytes accessed | tf_op | source)
XLA Modules:
  0.0 188.9 jit_solution(8469118686563833562)
XLA Ops:
  3.5 2.6 %fusion.31 = (f32[64,8]{1,0:T(8,128)S(1)}, f32[64,8,96]{2,1,0:T(8,128)S(1)}) fusion(bf16[64,8,128]{2,1,0:T(8,128)(2,1)S(1)} %bitcast.58, bf16[64,2,96,128]{3,2,1,0:T(8,128)(2,1)} %param.15, pred[64,96]{1,0:T(8,128)(4,1)S(1)} %iota_compare_fusion.7), kind=kOutput, calls=%fused_computation.48 | convolution fusion | flops 12729856 | bytes 1908736 | tf_op jit(solution)/shard_map/rkgd,rckd->rkgc/dot_general | solution.py:37
  6.3 2.0 %fusion.15 = bf16[64,8,128]{2,1,0:T(8,128)(2,1)S(1)} fusion(bf16[64,2,96,128]{3,2,1,0:T(8,128)(2,1)} %param.15, f32[64,8,96]{2,1,0:T(8,128)S(1)} %get-tuple-element.29, f32[64,128]{1,0:T(8,128)S(1)} %bitcast.63, f32[64,8]{1,0:T(8,128)S(1)} %get-tuple-element.25, f32[64,8]{1,0:T(8,128)S(1)} %get-tuple-element.24, f32[64,8]{1,0:T(8,128)S(1)} %multiply_maximum_fusion), kind=kOutput, calls=%fused_computation.11 | convolution fusion | flops 12926976 | bytes 1939456 | tf_op jit(solution)/shard_map/rkgc,rckd->rkgd/dot_general | solution.py:52
  10.0 5.0 %all-to-all-start = ((bf16[4,64,512]{2,1,0:T(8,128)(2,1)}), bf16[4,64,512]{2,1,0:T(8,128)(2,1)}, u32[]{:S(2)}, u32[]{:S(2)}) async-start(bf16[4,64,512]{2,1,0:T(8,128)(2,1)} %bitcast.51), calls=%async_computation | async-start | bytes 524288 | tf_op jit(solution)/shard_map/all_to_all | solution.py:399
  15.9 4.7 %all-to-all-done.pieces_ref = bf16[4,64,512]{2,1,0:T(8,128)(2,1)} async-done(((bf16[4,64,512]{2,1,0:T(8,128)(2,1)}), bf16[4,64,512]{2,1,0:T(8,128)(2,1)}, u32[]{:S(2)}, u32[]{:S(2)}) %all-to-all-start) | async-done | bytes 262176 | tf_op jit(solution)/shard_map/all_to_all | solution.py:399
  24.0 8.2 %all-to-all-start.1 = ((bf16[8,80,512]{2,1,0:T(8,128)(2,1)}), bf16[8,80,512]{2,1,0:T(8,128)(2,1)}, u32[]{:S(2)}, u32[]{:S(2)}) async-start(bf16[8,80,512]{2,1,0:T(8,128)(2,1)} %copy-done.4), calls=%async_computation.1 | async-start | bytes 1310720 | tf_op jit(solution)/shard_map/all_to_all | solution.py:404
  33.1 1.4 copy-done.3
  34.5 2.2 %pick_weights.1 = (bf16[3,192,2048]{2,1,0:T(8,128)(2,1)}, bf16[3,192,2048]{2,1,0:T(8,128)(2,1)}) custom-call(s32[1]{0:T(128)} %bitcast.11.first_ref, bf16[4,64,512]{2,1,0:T(8,128)(2,1)S(1)} %bitcast.52, bf16[2,2,192,2048]{3,2,1,0:T(8,128)(2,1)S(1)} %bitcast.50, bf16[2,192,2048]{2,1,0:T(8,128)(2,1)S(1)} %copy-done.3), custom_call_target="tpu_custom_call" | custom-call | tf_op jit(solution)/shard_map/pick_weights/pallas_call | solution.py:245
  36.7 4.4 %collective-permute-start = (bf16[3,192,2048]{2,1,0:T(8,128)(2,1)}, bf16[3,192,2048]{2,1,0:T(8,128)(2,1)}, u32[]{:S(2)}, u32[]{:S(2)}) collective-permute-start(bf16[3,192,2048]{2,1,0:T(8,128)(2,1)} %get-tuple-element.18), channel_id=1, source_target_pairs={{0,0},{1,1},{2,4},{3,5},{4,2},{5,3},{6,6},{7,7},{8,8},{9,9},{10,12... | collective-permute-start | bytes 7077896 | tf_op jit(solution)/shard_map/ppermute | solution.py:353
  41.9 8.8 %all-to-all-done.1.spread_ref = bf16[8,80,512]{2,1,0:T(8,128)(2,1)} async-done(((bf16[8,80,512]{2,1,0:T(8,128)(2,1)}), bf16[8,80,512]{2,1,0:T(8,128)(2,1)}, u32[]{:S(2)}, u32[]{:S(2)}) %all-to-all-start.1) | async-done | bytes 655392 | tf_op jit(solution)/shard_map/all_to_all | solution.py:404
  50.6 3.0 %gather_rows.1 = (bf16[16,80,512]{2,1,0:T(8,128)(2,1)}, f32[16,512]{1,0:T(8,128)S(1)}, f32[16,512]{1,0:T(8,128)S(1)}) custom-call(bf16[8,80,512]{2,1,0:T(8,128)(2,1)} %all-to-all-done.1.spread_ref), custom_call_target="tpu_custom_call" | custom-call | tf_op jit(solution)/shard_map/gather_rows/pallas_call | solution.py:269
  53.7 11.2 %all-to-all-start.2 = ((bf16[16,80,512]{2,1,0:T(8,128)(2,1)}), bf16[16,80,512]{2,1,0:T(8,128)(2,1)S(1)}, u32[]{:S(2)}, u32[]{:S(2)}) async-start(bf16[16,80,512]{2,1,0:T(8,128)(2,1)} %get-tuple-element.17), calls=%async_computation.2 | async-start | bytes 2621440 | tf_op jit(solution)/shard_map/all_to_all | solution.py:406
  64.9 24.1 %collective-permute-done.refs_1_ = bf16[3,192,2048]{2,1,0:T(8,128)(2,1)} collective-permute-done((bf16[3,192,2048]{2,1,0:T(8,128)(2,1)}, bf16[3,192,2048]{2,1,0:T(8,128)(2,1)}, u32[]{:S(2)}, u32[]{:S(2)}) %collective-permute-start) | collective-permute-done | bytes 2359328 | tf_op jit(solution)/shard_map/ppermute | solution.py:353
  89.0 17.3 %collective-permute-done.1.refs_2_ = bf16[3,192,2048]{2,1,0:T(8,128)(2,1)} collective-permute-done((bf16[3,192,2048]{2,1,0:T(8,128)(2,1)}, bf16[3,192,2048]{2,1,0:T(8,128)(2,1)}, u32[]{:S(2)}, u32[]{:S(2)}) %collective-permute-start.1) | collective-permute-done | bytes 2359328 | tf_op jit(solution)/shard_map/ppermute | solution.py:353
  106.3 1.2 all-to-all-done.2.refs_0_.rows_ref
  107.5 1.1 collective-permute-start.2
  108.6 4.0 %first_half.1 = (bf16[320,2048]{1,0:T(8,128)(2,1)S(1)}, f32[320,2048]{1,0:T(8,128)S(1)}) custom-call(bf16[16,80,512]{2,1,0:T(8,128)(2,1)S(1)} %all-to-all-done.2.refs_0_.rows_ref, f32[1,2048]{1,0:T(1,128)S(1)} %bitcast.53, bf16[3,192,2048]{2,1,0:T(8,128)(2,1)} %get-tuple-element.20.w0, bf16[3,192,2048]{2,1,0:T(8,128)(2,1)} %get-tuple-element.21.w1), custom_call_target="tpu_custom_call" | custom-call | tf_op jit(solution)/shard_map/first_half/pallas_call | solution.py:323
  113.0 3.4 %collective-permute-done.3.w3 = bf16[3,192,2048]{2,1,0:T(8,128)(2,1)S(1)} collective-permute-done((bf16[3,192,2048]{2,1,0:T(8,128)(2,1)}, bf16[3,192,2048]{2,1,0:T(8,128)(2,1)S(1)}, u32[]{:S(2)}, u32[]{:S(2)}) %collective-permute-start.3) | collective-permute-done | bytes 2359328 | tf_op jit(solution)/shard_map/ppermute | solution.py:408
  116.4 3.0 %second_half.1 = bf16[16,80,512]{2,1,0:T(8,128)(2,1)S(1)} custom-call(bf16[320,2048]{1,0:T(8,128)(2,1)S(1)} %get-tuple-element.22.normed_ref, f32[320,2048]{1,0:T(8,128)S(1)} %get-tuple-element.23.part_ref, bf16[3,192,2048]{2,1,0:T(8,128)(2,1)S(1)} %collective-permute-done.2.w2, bf16[3,192,2048]{2,1,0:T(8,128)(2,1)S(1)} %collective-permute-done.3.w3), custom_call_target="tpu_custom_call" | custom-call | tf_op jit(solution)/shard_map/second_half/pallas_call | solution.py:335
  119.4 25.1 %all_to_all.30.rows_ref = bf16[16,80,512]{2,1,0:T(8,128)(2,1)S(1)} all-to-all(bf16[16,80,512]{2,1,0:T(8,128)(2,1)S(1)} %second_half.1), channel_id=1, replica_groups=mesh['z'=8,'x'=4,'c'=2,'y'=4] {'x','y'}, dimensions={0} | all-to-all | bytes 2621440 | tf_op jit(solution)/shard_map/all_to_all | solution.py:411
  144.5 1.7 combine_rows.1
  146.2 6.9 %all-to-all-start.4 = ((bf16[8,64,512]{2,1,0:T(8,128)(2,1)}), bf16[8,64,512]{2,1,0:T(8,128)(2,1)S(1)}, u32[]{:S(2)}, u32[]{:S(2)}) async-start(bf16[8,64,512]{2,1,0:T(8,128)(2,1)} %combine_rows.1), calls=%async_computation.4 | async-start | bytes 1048576 | tf_op jit(solution)/shard_map/all_to_all | solution.py:413
  153.7 15.2 %all-to-all-done.4 = bf16[8,64,512]{2,1,0:T(8,128)(2,1)S(1)} async-done(((bf16[8,64,512]{2,1,0:T(8,128)(2,1)}), bf16[8,64,512]{2,1,0:T(8,128)(2,1)S(1)}, u32[]{:S(2)}, u32[]{:S(2)}) %all-to-all-start.4) | async-done | bytes 524320 | tf_op jit(solution)/shard_map/all_to_all | solution.py:413
  169.9 6.8 %all-to-all-start.5 = ((bf16[64,2,512]{2,1,0:T(2,128)(2,1)}), bf16[64,2,512]{2,1,0:T(2,128)(2,1)S(1)}, u32[]{:S(2)}, u32[]{:S(2)}) async-start(bf16[64,2,512]{2,1,0:T(2,128)(2,1)} %reshape.149), calls=%async_computation.5 | async-start | bytes 262144 | tf_op jit(solution)/shard_map/all_to_all | solution.py:419
  177.0 11.0 %all-to-all-done.5 = bf16[64,2,512]{2,1,0:T(2,128)(2,1)S(1)} async-done(((bf16[64,2,512]{2,1,0:T(2,128)(2,1)}), bf16[64,2,512]{2,1,0:T(2,128)(2,1)S(1)}, u32[]{:S(2)}, u32[]{:S(2)}) %all-to-all-start.5) | async-done | bytes 131104 | tf_op jit(solution)/shard_map/all_to_all | solution.py:419
  (59 shorter events, 13.6 us)
Async XLA Ops:
  0.6 14.6 %copy-start = (bf16[64,2048]{1,0:T(8,128)(2,1)S(1)}, bf16[64,2048]{1,0:T(8,128)(2,1)}, u32[]{:S(2)}) copy-start(bf16[64,2048]{1,0:T(8,128)(2,1)} %param.12) | copy-start | bytes 786436
  3.5 4.9 %copy-start.11 = (bf16[1024,2048]{1,0:T(8,128)(2,1)S(1)}, bf16[1024,2048]{1,0:T(8,128)(2,1)}, u32[]{:S(2)}) copy-start(bf16[1024,2048]{1,0:T(8,128)(2,1)} %param.17) | copy-start | bytes 12582916
  8.3 6.7 %copy-start.9 = (s32[64,8]{0,1:T(8,128)S(1)}, s32[64,8]{0,1:T(8,128)}, u32[]{:S(2)}) copy-start(s32[64,8]{0,1:T(8,128)} %param.19) | copy-start | bytes 6148
  8.3 6.6 %copy-start.10 = (f32[64,8]{0,1:T(8,128)S(1)}, f32[64,8]{0,1:T(8,128)}, u32[]{:S(2)}) copy-start(f32[64,8]{0,1:T(8,128)} %param.20) | copy-start | bytes 6148
  8.4 23.8 %copy-start.1 = (bf16[2,2,2048,192]{2,3,1,0:T(8,128)(2,1)S(1)}, bf16[2,2,2048,192]{2,3,1,0:T(8,128)(2,1)}, u32[]{:S(2)}) copy-start(bf16[2,2,2048,192]{2,3,1,0:T(8,128)(2,1)} %param.21) | copy-start | bytes 9437188
  10.0 10.6 %all-to-all-start = ((bf16[4,64,512]{2,1,0:T(8,128)(2,1)}), bf16[4,64,512]{2,1,0:T(8,128)(2,1)}, u32[]{:S(2)}, u32[]{:S(2)}) async-start(bf16[4,64,512]{2,1,0:T(8,128)(2,1)} %bitcast.51), calls=%async_computation | async-start | bytes 524288 | tf_op jit(solution)/shard_map/all_to_all | solution.py:399
  20.6 0.8 copy-start.5
  22.5 0.9 copy-start.4
  23.3 0.6 copy-start.6
  24.0 26.7 %all-to-all-start.1 = ((bf16[8,80,512]{2,1,0:T(8,128)(2,1)}), bf16[8,80,512]{2,1,0:T(8,128)(2,1)}, u32[]{:S(2)}, u32[]{:S(2)}) async-start(bf16[8,80,512]{2,1,0:T(8,128)(2,1)} %copy-done.4), calls=%async_computation.1 | async-start | bytes 1310720 | tf_op jit(solution)/shard_map/all_to_all | solution.py:404
  32.2 1.0 copy-start.2
  33.1 1.4 copy-start.3
  36.7 52.3 %collective-permute-start = (bf16[3,192,2048]{2,1,0:T(8,128)(2,1)}, bf16[3,192,2048]{2,1,0:T(8,128)(2,1)}, u32[]{:S(2)}, u32[]{:S(2)}) collective-permute-start(bf16[3,192,2048]{2,1,0:T(8,128)(2,1)} %get-tuple-element.18), channel_id=1, source_target_pairs={{0,0},{1,1},{2,4},{3,5},{4,2},{5,3},{6,6},{7,7},{8,8},{9,9},{10,12... | collective-permute-start | bytes 7077896 | tf_op jit(solution)/shard_map/ppermute | solution.py:353
  41.2 65.1 %collective-permute-start.1 = (bf16[3,192,2048]{2,1,0:T(8,128)(2,1)}, bf16[3,192,2048]{2,1,0:T(8,128)(2,1)}, u32[]{:S(2)}, u32[]{:S(2)}) collective-permute-start(bf16[3,192,2048]{2,1,0:T(8,128)(2,1)} %get-tuple-element.19), channel_id=1, source_target_pairs={{0,1},{1,0},{2,5},{3,4},{4,3},{5,2},{6,7},{7,6},{8,9},{9,8},{10,13... | collective-permute-start | bytes 7077896 | tf_op jit(solution)/shard_map/ppermute | solution.py:353
  53.7 53.8 %all-to-all-start.2 = ((bf16[16,80,512]{2,1,0:T(8,128)(2,1)}), bf16[16,80,512]{2,1,0:T(8,128)(2,1)S(1)}, u32[]{:S(2)}, u32[]{:S(2)}) async-start(bf16[16,80,512]{2,1,0:T(8,128)(2,1)} %get-tuple-element.17), calls=%async_computation.2 | async-start | bytes 2621440 | tf_op jit(solution)/shard_map/all_to_all | solution.py:406
  64.9 43.7 %copy-start.8 = (f32[2048]{0:T(1024)S(1)}, f32[2048]{0:T(1024)}, u32[]{:S(2)}) copy-start(f32[2048]{0:T(1024)} %param.18) | copy-start | bytes 24580
  107.5 5.5 %collective-permute-start.2 = (bf16[3,192,2048]{2,1,0:T(8,128)(2,1)}, bf16[3,192,2048]{2,1,0:T(8,128)(2,1)S(1)}, u32[]{:S(2)}, u32[]{:S(2)}) collective-permute-start(bf16[3,192,2048]{2,1,0:T(8,128)(2,1)} %get-tuple-element.20.w0), channel_id=1, source_target_pairs={{0,4},{4,0},{1,5},{5,1},{2,6},{6,2},{3,7},{7,3},{8,12},{12,8},{9,1... | collective-permute-start | bytes 7077896 | tf_op jit(solution)/shard_map/ppermute | solution.py:408
  108.6 7.7 %collective-permute-start.3 = (bf16[3,192,2048]{2,1,0:T(8,128)(2,1)}, bf16[3,192,2048]{2,1,0:T(8,128)(2,1)S(1)}, u32[]{:S(2)}, u32[]{:S(2)}) collective-permute-start(bf16[3,192,2048]{2,1,0:T(8,128)(2,1)} %get-tuple-element.21.w1), channel_id=1, source_target_pairs={{0,4},{4,0},{1,5},{5,1},{2,6},{6,2},{3,7},{7,3},{8,12},{12,8},{9,1... | collective-permute-start | bytes 7077896 | tf_op jit(solution)/shard_map/ppermute | solution.py:408
  119.4 33.8 %copy-start.13 = (s32[4096]{0:T(1024)S(1)}, s32[4096]{0:T(1024)}, u32[]{:S(2)}) copy-start(s32[4096]{0:T(1024)} %param.23) | copy-start | bytes 49156
  144.5 24.4 %copy-start.7 = (bf16[64,512]{1,0:T(8,128)(2,1)S(1)}, bf16[64,512]{1,0:T(8,128)(2,1)}, u32[]{:S(2)}) copy-start(bf16[64,512]{1,0:T(8,128)(2,1)} %copy-done.6) | copy-start | bytes 196612
  146.2 22.6 %all-to-all-start.4 = ((bf16[8,64,512]{2,1,0:T(8,128)(2,1)}), bf16[8,64,512]{2,1,0:T(8,128)(2,1)S(1)}, u32[]{:S(2)}, u32[]{:S(2)}) async-start(bf16[8,64,512]{2,1,0:T(8,128)(2,1)} %combine_rows.1), calls=%async_computation.4 | async-start | bytes 1048576 | tf_op jit(solution)/shard_map/all_to_all | solution.py:413
  169.0 19.9 %copy-start.12 = (bf16[64,512]{1,0:T(8,128)(2,1)}, bf16[64,512]{1,0:T(8,128)(2,1)S(1)}, u32[]{:S(2)}) copy-start(bf16[64,512]{1,0:T(8,128)(2,1)S(1)} %add_convert_fusion) | copy-start | bytes 196612
  169.9 18.1 %all-to-all-start.5 = ((bf16[64,2,512]{2,1,0:T(2,128)(2,1)}), bf16[64,2,512]{2,1,0:T(2,128)(2,1)S(1)}, u32[]{:S(2)}, u32[]{:S(2)}) async-start(bf16[64,2,512]{2,1,0:T(2,128)(2,1)} %reshape.149), calls=%async_computation.5 | async-start | bytes 262144 | tf_op jit(solution)/shard_map/all_to_all | solution.py:419

commit v4 on v3

--- a/solution.py
+++ b/solution.py
@@ -17,6 +17,7 @@
 TOKENS = NZ * REQ
 PLANE = NX * NY
 BLOCK = NZ * CAP
+ROWS = REQ // PLANE
 QUARTER = 512
 WIDTH = 2048
 EHQ = 192
@@ -77,12 +78,11 @@
     token = jnp.where(token >= REQ, token - REQ, token)
     before = jnp.where(earlier < token, 1.0, 0.0).astype(jnp.bfloat16)
     rank = jnp.dot(chosen.astype(jnp.bfloat16), before, preferred_element_type=jnp.float32)
-    slot = jnp.where(chosen > 0.0, rank, -1.0).astype(jnp.bfloat16)
-    gate = gate.astype(jnp.bfloat16)
-    out_ref[...] = jnp.zeros((NZ, PLANE, QUARTER), jnp.bfloat16)
+    slot = jnp.where(chosen > 0.0, rank, -1.0)
+    first = lax.broadcasted_iota(jnp.int32, (experts, 2 * REQ), 1) < REQ
+    both = jnp.where(first, slot, gate).astype(jnp.bfloat16)
     for z in range(NZ):
-        out_ref[z, :, : 2 * REQ] = slot[z * PLANE : (z + 1) * PLANE, :]
-        out_ref[z, :, 2 * REQ : 4 * REQ] = gate[z * PLANE : (z + 1) * PLANE, :]
+        out_ref[z] = both[z * PLANE : (z + 1) * PLANE, :]
 
 
 def pick_kernel(first_ref, after_ref, gate_up, down, even_ref, odd_ref, sems):
@@ -98,31 +98,32 @@
         copy.wait()
 
 
-def middle_kernel(pieces_ref, hidden_ref, plan_ref, message_ref, middle_ref):
+def middle_kernel(pieces_ref, hidden_ref, plan_ref, even, odd, message_ref, middle_ref, *same):
     total = hidden_ref[...].astype(jnp.float32)
     for y in range(NY):
         total = total + pieces_ref[y].astype(jnp.float32)
     middle = total.astype(jnp.bfloat16)
     middle_ref[...] = middle
     for z in range(NZ):
-        message_ref[z, :REQ, :] = middle
-        message_ref[z, REQ:, :] = plan_ref[z]
-
-
-def gather_kernel(spread_ref, out_ref, target_ref, gate_ref, pick_ref, rows_ref):
+        for k in range(ROWS):
+            message_ref[z, :, k * QUARTER : (k + 1) * QUARTER] = middle[k * PLANE : (k + 1) * PLANE, :]
+        message_ref[z, :, WIDTH:] = plan_ref[z]
+
+
+def gather_kernel(spread_ref, after_ref, out_ref, target_ref, gate_ref, pick_ref, rows_ref):
     low = lax.broadcasted_iota(jnp.int32, (PLANE, 2 * REQ), 1) < REQ
     for pair in range(NZ // 2):
-        left, right = spread_ref[2 * pair, REQ:, :], spread_ref[2 * pair + 1, REQ:, :]
-        left, right = left.astype(jnp.float32), right.astype(jnp.float32)
-        both = jnp.where(low, left[:, : 2 * REQ], right[:, : 2 * REQ])
+        left = spread_ref[2 * pair, :, WIDTH:].astype(jnp.float32)
+        right = spread_ref[2 * pair + 1, :, WIDTH:].astype(jnp.float32)
+        both = jnp.concatenate([left[:, :REQ], right[:, :REQ]], axis=1)
         block = jnp.where(low, float(2 * pair * CAP), float((2 * pair + 1) * CAP))
         columns = slice(pair * 2 * REQ, (pair + 1) * 2 * REQ)
         target_ref[:, columns] = jnp.where(both >= 0.0, both + block, -1.0)
-        gate_ref[:, columns] = jnp.where(
-            low, left[:, 2 * REQ : 4 * REQ], right[:, 2 * REQ : 4 * REQ]
-        )
+        gate_ref[:, columns] = jnp.concatenate([left[:, REQ:], right[:, REQ:]], axis=1)
     for z in range(NZ):
-        rows_ref[z * REQ : (z + 1) * REQ, :] = spread_ref[z, :REQ, :]
+        for k in range(ROWS):
+            first = z * REQ + k * PLANE
+            rows_ref[first : first + PLANE, :] = spread_ref[z, :, k * QUARTER : (k + 1) * QUARTER]
     slot = lax.broadcasted_iota(jnp.int32, (BLOCK, TOKENS), 0).astype(jnp.float32)
     for e in range(PLANE):
         hit = target_ref[e : e + 1, :] == slot
@@ -232,7 +233,7 @@
 def make_plan(ids, gates):
     return pl.pallas_call(
         plan_kernel,
-        out_shape=shape(NZ, PLANE, QUARTER),
+        out_shape=shape(NZ, PLANE, 2 * REQ),
         in_specs=[vmem(), vmem()],
         out_specs=vmem(),
         compiler_params=params(),
@@ -254,18 +255,23 @@
     )(first, after, gate_up, down)
 
 
-def sum_middle(pieces, hidden, plan):
+def sum_middle(pieces, hidden, plan, blocks):
     return pl.pallas_call(
         middle_kernel,
-        out_shape=(shape(NZ, REQ + PLANE, QUARTER), shape(REQ, QUARTER)),
-        in_specs=[vmem()] * 3,
-        out_specs=(vmem(), vmem()),
+        out_shape=(
+            shape(NZ, PLANE, WIDTH + 2 * REQ),
+            shape(REQ, QUARTER),
+            *[shape(*block.shape) for block in blocks],
+        ),
+        in_specs=[vmem()] * 3 + [anywhere()] * 2,
+        out_specs=(vmem(), vmem()) + (anywhere(),) * 2,
+        input_output_aliases={3: 2, 4: 3},
         compiler_params=params(),
         name="sum_middle",
-    )(pieces, hidden, plan)
-
-
-def gather_rows(spread):
+    )(pieces, hidden, plan, *blocks)
+
+
+def gather_rows(spread, after):
     return pl.pallas_call(
         gather_kernel,
         out_shape=(
@@ -273,7 +279,7 @@
             shape(PLANE, TOKENS, dtype=jnp.float32),
             shape(PLANE, TOKENS, dtype=jnp.float32),
         ),
-        in_specs=[vmem()],
+        in_specs=[vmem(), anywhere()],
         out_specs=(vmem(), vmem(), vmem()),
         scratch_shapes=[
             pltpu.VMEM((PLANE * BLOCK, TOKENS), jnp.bfloat16),
@@ -281,19 +287,19 @@
         ],
         compiler_params=params(),
         name="gather_rows",
-    )(spread)
-
-
-def hold(after, blocks):
+    )(spread, after)
+
+
+def hold(after, block):
     return pl.pallas_call(
         hold_kernel,
-        out_shape=tuple(shape(*block.shape) for block in blocks),
-        in_specs=[anywhere()] * 3,
-        out_specs=(anywhere(),) * 2,
-        input_output_aliases={1 + k: k for k in range(2)},
+        out_shape=shape(*block.shape),
+        in_specs=[anywhere()] * 2,
+        out_specs=anywhere(),
+        input_output_aliases={1: 0},
         compiler_params=params(),
         name="hold",
-    )(after, *blocks)
+    )(after, block)
 
 
 def combine_rows(target, gate, rows):
@@ -398,16 +404,18 @@
     blocks = pick_weights(first, pieces, gate_up.transpose(0, 1, 3, 2), down)
     pieces = lax.all_to_all(pieces, "y", 0, 0, tiled=True)
     hidden = lax.dynamic_slice_in_dim(hidden_in, y * QUARTER, QUARTER, 1)
-    message, middle = sum_middle(pieces, hidden, plan)
-    blocks = move_weights(blocks)
+    message, middle, *blocks = sum_middle(pieces, hidden, plan, blocks)
+    even, odd = move_weights(blocks)
+    swap = [(0, 1), (1, 0)]
 
     spread = lax.all_to_all(message, "z", 0, 0, tiled=True)
-    send, target, gate = gather_rows(spread)
+    send, target, gate = gather_rows(spread, odd)
     rows = lax.all_to_all(send, ("x", "y"), 0, 0, tiled=True)
-    blocks = hold(rows, blocks)
-    swapped = [lax.ppermute(block, "c", [(0, 1), (1, 0)]) for block in blocks]
-    normed, half = first_half(rows, moe_gain.reshape(1, WIDTH), blocks)
-    done = second_half(normed, half, swapped)
+    even = hold(rows, even)
+    odd_swapped = lax.ppermute(odd, "c", swap)
+    even_swapped = lax.ppermute(even, "c", swap)
+    normed, half = first_half(rows, moe_gain.reshape(1, WIDTH), (odd, odd_swapped))
+    done = second_half(normed, half, (even, even_swapped))
     back = lax.all_to_all(done, ("x", "y"), 0, 0, tiled=True)
     part = combine_rows(target, gate, back)
     part = lax.all_to_all(part, "z", 0, 0, tiled=True)

time: 191 us -> 185 us (0.969)
  blocking collectives: 25.1 us -> 42 us
  starting transfers between devices: 44.5 us -> 30.6 us
  waiting for transfers between devices: 85.9 us -> 76.1 us
  local copies, waits for them, and re-layouts: 8.14 us -> 10.4 us
    all_to_all x1, waiting for transfers between devices: 1.21 us -> 20.9 us  [local(): rows = lax.all_to_all(send, ('x', 'y'), 0, 0, tiled=True)]
    all_to_all x0 -> x1, blocking collectives: none -> 19.2 us  [local(): spread = lax.all_to_all(message, 'z', 0, 0, tiled=True)]
    ppermute x2, waiting for transfers between devices: 41.4 us -> 30.4 us  [move_weights(): lax.ppermute(block, ('c', 'y'), to)]
    all_to_all x1 -> x0, waiting for transfers between devices: 8.76 us -> none  [local(): spread = lax.all_to_all(message, 'z', 0, 0, tiled=True)]
    all_to_all x1 -> x0, starting transfers between devices: 8.21 us -> none  [local(): spread = lax.all_to_all(message, 'z', 0, 0, tiled=True)]
    all_to_all x1, starting transfers between devices: 11.2 us -> 3.7 us  [local(): rows = lax.all_to_all(send, ('x', 'y'), 0, 0, tiled=True)]
    all_to_all x1, waiting for transfers between devices: 4.72 us -> 0.1 us  [local(): pieces = lax.all_to_all(pieces, 'y', 0, 0, tiled=True)]
    ppermute x2, waiting for transfers between devices: 3.71 us -> 0.01 us  [the longest x1 0.01 us: local(): odd_swapped = lax.ppermute(odd, 'c', swap)]
  transfers between devices with their start and end apart: 9 -> 8, of which waited for: 9 -> 5; matrix products, arithmetic and copies ran while one was open for 1% -> 0% of each run, Pallas kernels for 5% -> 4%
where the time goes in v4:
time: 185 us; the launch traced here: 183 us
  waiting for transfers between devices  76.1 us (41%)
  blocking collectives  42 us (23%)
  starting transfers between devices  30.6 us (17%)
  Pallas kernels  14 us (8%)
  local copies, waits for them, and re-layouts  10.4 us (6%)
  matrix products  6.6 us (4%)
  other arithmetic  2.56 us (1%)
    ppermute x2, waiting for transfers between devices, move_weights(): lax.ppermute(block, ('c', 'y'), to)  30.4 us
    all_to_all x1, blocking collectives, local(): back = lax.all_to_all(done, ('x', 'y'), 0, 0, tiled=True)  22.8 us
    all_to_all x1, waiting for transfers between devices, local(): rows = lax.all_to_all(send, ('x', 'y'), 0, 0, tiled=True)  20.9 us
    all_to_all x1, blocking collectives, local(): spread = lax.all_to_all(message, 'z', 0, 0, tiled=True)  19.2 us
    all_to_all x1, waiting for transfers between devices, local(): part = lax.all_to_all(part, 'z', 0, 0, tiled=True)  13.7 us
    all_to_all x1, waiting for transfers between devices, local(): lax.all_to_all(leaving.reshape(SECTIONS, HCAP, QUARTER), ('z', 'x', 'c'),...  11 us
    unnamed x30, local copies, waits for them, and re-layouts  8.55 us
    all_to_all x1, starting transfers between devices, local(): lax.all_to_all(leaving.reshape(SECTIONS, HCAP, QUARTER), ('z', 'x', 'c'),...  8.25 us
  transfers between devices with their start and end apart: 8, of which 5 were waited for; matrix products, arithmetic and copies ran while one was open for 0% of the time, Pallas kernels for 4%

profile of v4, /device:TPU:1, one launch (start us, length us, event | category | flops | bytes accessed | tf_op | source)
XLA Modules:
  0.0 183.0 jit_solution(16451046268028508885)
XLA Ops:
  3.5 2.6 %fusion.31 = (f32[64,8]{1,0:T(8,128)S(1)}, f32[64,8,96]{2,1,0:T(8,128)S(1)}) fusion(bf16[64,8,128]{2,1,0:T(8,128)(2,1)S(1)} %bitcast.58, bf16[64,2,96,128]{3,2,1,0:T(8,128)(2,1)} %param.15, pred[64,96]{1,0:T(8,128)(4,1)S(1)} %iota_compare_fusion.7), kind=kOutput, calls=%fused_computation.48 | convolution fusion | flops 12729856 | bytes 1908736 | tf_op jit(solution)/shard_map/rkgd,rckd->rkgc/dot_general | solution.py:38
  6.3 2.0 %fusion.15 = bf16[64,8,128]{2,1,0:T(8,128)(2,1)S(1)} fusion(bf16[64,2,96,128]{3,2,1,0:T(8,128)(2,1)} %param.15, f32[64,8,96]{2,1,0:T(8,128)S(1)} %get-tuple-element.29, f32[64,128]{1,0:T(8,128)S(1)} %bitcast.63, f32[64,8]{1,0:T(8,128)S(1)} %get-tuple-element.25, f32[64,8]{1,0:T(8,128)S(1)} %get-tuple-element.24, f32[64,8]{1,0:T(8,128)S(1)} %multiply_maximum_fusion), kind=kOutput, calls=%fused_computation.11 | convolution fusion | flops 12926976 | bytes 1939456 | tf_op jit(solution)/shard_map/rkgc,rckd->rkgd/dot_general | solution.py:53
  9.9 5.0 %all-to-all-start = ((bf16[4,64,512]{2,1,0:T(8,128)(2,1)}), bf16[4,64,512]{2,1,0:T(8,128)(2,1)}, u32[]{:S(2)}, u32[]{:S(2)}) async-start(bf16[4,64,512]{2,1,0:T(8,128)(2,1)} %bitcast.51), calls=%async_computation | async-start | bytes 524288 | tf_op jit(solution)/shard_map/all_to_all | solution.py:405
  16.2 1.4 copy-done.7
  17.6 1.5 pick_weights.1
  19.1 1.4 copy-done.4
  20.6 1.7 copy-done.5
  23.3 5.1 %collective-permute-start = (bf16[3,192,2048]{2,1,0:T(8,128)(2,1)S(1)}, bf16[3,192,2048]{2,1,0:T(8,128)(2,1)S(1)}, u32[]{:S(2)}, u32[]{:S(2)}) collective-permute-start(bf16[3,192,2048]{2,1,0:T(8,128)(2,1)S(1)} %get-tuple-element.17), channel_id=1, source_target_pairs={{0,1},{1,0},{2,5},{3,4},{4,3},{5,2},{6,7},{7,6},{8,9},{9,8},{10,13... | collective-permute-start | bytes 7077896 | tf_op jit(solution)/shard_map/ppermute | solution.py:359
  28.3 2.2 %collective-permute-start.2 = (bf16[3,192,2048]{2,1,0:T(8,128)(2,1)}, bf16[3,192,2048]{2,1,0:T(8,128)(2,1)}, u32[]{:S(2)}, u32[]{:S(2)}) collective-permute-start(bf16[3,192,2048]{2,1,0:T(8,128)(2,1)} %get-tuple-element.23), channel_id=1, source_target_pairs={{0,0},{1,1},{2,4},{3,5},{4,2},{5,3},{6,6},{7,7},{8,8},{9,9},{10,12... | collective-permute-start | bytes 7077896 | tf_op jit(solution)/shard_map/ppermute | solution.py:359
  30.6 19.2 %all_to_all.30.spread_ref = bf16[8,16,2176]{2,1,0:T(8,128)(2,1)S(1)} all-to-all(bf16[8,16,2176]{2,1,0:T(8,128)(2,1)S(1)} %get-tuple-element.16), channel_id=1, replica_groups=mesh['z'=8,'x'=4,'c'=2,'y'=4] {'z'}, dimensions={0} | all-to-all | bytes 1114112 | tf_op jit(solution)/shard_map/all_to_all | solution.py:411
  49.8 30.4 %collective-permute-done.after_ref.w0 = bf16[3,192,2048]{2,1,0:T(8,128)(2,1)S(1)} collective-permute-done((bf16[3,192,2048]{2,1,0:T(8,128)(2,1)S(1)}, bf16[3,192,2048]{2,1,0:T(8,128)(2,1)S(1)}, u32[]{:S(2)}, u32[]{:S(2)}) %collective-permute-start) | collective-permute-done | bytes 2359328 | tf_op jit(solution)/shard_map/ppermute | solution.py:359
  80.1 2.0 %gather_rows.1 = (bf16[16,80,512]{2,1,0:T(8,128)(2,1)}, f32[16,512]{1,0:T(8,128)S(1)}, f32[16,512]{1,0:T(8,128)S(1)}) custom-call(bf16[8,16,2176]{2,1,0:T(8,128)(2,1)S(1)} %all_to_all.30.spread_ref, bf16[3,192,2048]{2,1,0:T(8,128)(2,1)S(1)} %collective-permute-done.after_ref.w0), custom_call_target="tpu_custom_call" | custom-call | tf_op jit(solution)/shard_map/gather_rows/pallas_call | solution.py:275
  82.1 1.4 copy-done.1
  83.6 3.7 %all-to-all-start.2 = ((bf16[16,80,512]{2,1,0:T(8,128)(2,1)}), bf16[16,80,512]{2,1,0:T(8,128)(2,1)S(1)}, u32[]{:S(2)}, u32[]{:S(2)}) async-start(bf16[16,80,512]{2,1,0:T(8,128)(2,1)} %get-tuple-element.20), calls=%async_computation.2 | async-start | bytes 2621440 | tf_op jit(solution)/shard_map/all_to_all | solution.py:413
  87.4 20.9 %all-to-all-done.2.rows_ref.refs_0_ = bf16[16,80,512]{2,1,0:T(8,128)(2,1)S(1)} async-done(((bf16[16,80,512]{2,1,0:T(8,128)(2,1)}), bf16[16,80,512]{2,1,0:T(8,128)(2,1)S(1)}, u32[]{:S(2)}, u32[]{:S(2)}) %all-to-all-start.2) | async-done | bytes 1310752 | tf_op jit(solution)/shard_map/all_to_all | solution.py:413
  108.3 1.0 collective-permute-start.3
  110.0 3.8 %first_half.1 = (bf16[320,2048]{1,0:T(8,128)(2,1)S(1)}, f32[320,2048]{1,0:T(8,128)S(1)}) custom-call(bf16[16,80,512]{2,1,0:T(8,128)(2,1)S(1)} %all-to-all-done.2.rows_ref.refs_0_, f32[1,2048]{1,0:T(1,128)S(1)} %bitcast.53, bf16[3,192,2048]{2,1,0:T(8,128)(2,1)S(1)} %copy-done.2, bf16[3,192,2048]{2,1,0:T(8,128)(2,1)} %collective-permute-done.1.w1), custom_call_target="tpu_custom_call" | custom-call | tf_op jit(solution)/shard_map/first_half/pallas_call | solution.py:329
  113.8 3.8 %second_half.1 = bf16[16,80,512]{2,1,0:T(8,128)(2,1)S(1)} custom-call(bf16[320,2048]{1,0:T(8,128)(2,1)S(1)} %get-tuple-element.21.normed_ref, f32[320,2048]{1,0:T(8,128)S(1)} %get-tuple-element.22.part_ref, bf16[3,192,2048]{2,1,0:T(8,128)(2,1)} %hold.1.w2, bf16[3,192,2048]{2,1,0:T(8,128)(2,1)S(1)} %collective-permute-done.3.w3), custom_call_target="tpu_custom_call" | custom-call | tf_op jit(solution)/shard_map/second_half/pallas_call | solution.py:341
  117.6 22.8 %all_to_all.31.rows_ref = bf16[16,80,512]{2,1,0:T(8,128)(2,1)S(1)} all-to-all(bf16[16,80,512]{2,1,0:T(8,128)(2,1)S(1)} %second_half.1), channel_id=1, replica_groups=mesh['z'=8,'x'=4,'c'=2,'y'=4] {'x','y'}, dimensions={0} | all-to-all | bytes 2621440 | tf_op jit(solution)/shard_map/all_to_all | solution.py:419
  140.4 1.7 combine_rows.1
  142.1 5.2 %all-to-all-start.4 = ((bf16[8,64,512]{2,1,0:T(8,128)(2,1)}), bf16[8,64,512]{2,1,0:T(8,128)(2,1)S(1)}, u32[]{:S(2)}, u32[]{:S(2)}) async-start(bf16[8,64,512]{2,1,0:T(8,128)(2,1)} %combine_rows.1), calls=%async_computation.4 | async-start | bytes 1048576 | tf_op jit(solution)/shard_map/all_to_all | solution.py:421
  147.8 13.7 %all-to-all-done.4 = bf16[8,64,512]{2,1,0:T(8,128)(2,1)S(1)} async-done(((bf16[8,64,512]{2,1,0:T(8,128)(2,1)}), bf16[8,64,512]{2,1,0:T(8,128)(2,1)S(1)}, u32[]{:S(2)}, u32[]{:S(2)}) %all-to-all-start.4) | async-done | bytes 524320 | tf_op jit(solution)/shard_map/all_to_all | solution.py:421
  162.5 8.3 %all-to-all-start.5 = ((bf16[64,2,512]{2,1,0:T(2,128)(2,1)}), bf16[64,2,512]{2,1,0:T(2,128)(2,1)S(1)}, u32[]{:S(2)}, u32[]{:S(2)}) async-start(bf16[64,2,512]{2,1,0:T(2,128)(2,1)} %reshape.149), calls=%async_computation.5 | async-start | bytes 262144 | tf_op jit(solution)/shard_map/all_to_all | solution.py:427
  171.1 11.0 %all-to-all-done.5 = bf16[64,2,512]{2,1,0:T(2,128)(2,1)S(1)} async-done(((bf16[64,2,512]{2,1,0:T(2,128)(2,1)}), bf16[64,2,512]{2,1,0:T(2,128)(2,1)S(1)}, u32[]{:S(2)}, u32[]{:S(2)}) %all-to-all-start.5) | async-done | bytes 131104 | tf_op jit(solution)/shard_map/all_to_all | solution.py:427
  (58 shorter events, 10.5 us)
Async XLA Ops:
  0.6 19.9 %copy-start = (bf16[64,2048]{1,0:T(8,128)(2,1)S(1)}, bf16[64,2048]{1,0:T(8,128)(2,1)}, u32[]{:S(2)}) copy-start(bf16[64,2048]{1,0:T(8,128)(2,1)} %param.12) | copy-start | bytes 786436
  3.5 4.9 %copy-start.11 = (bf16[1024,2048]{1,0:T(8,128)(2,1)S(1)}, bf16[1024,2048]{1,0:T(8,128)(2,1)}, u32[]{:S(2)}) copy-start(bf16[1024,2048]{1,0:T(8,128)(2,1)} %param.17) | copy-start | bytes 12582916
  8.3 6.6 %copy-start.9 = (s32[64,8]{0,1:T(8,128)S(1)}, s32[64,8]{0,1:T(8,128)}, u32[]{:S(2)}) copy-start(s32[64,8]{0,1:T(8,128)} %param.19) | copy-start | bytes 6148
  8.3 6.6 %copy-start.10 = (f32[64,8]{0,1:T(8,128)S(1)}, f32[64,8]{0,1:T(8,128)}, u32[]{:S(2)}) copy-start(f32[64,8]{0,1:T(8,128)} %param.20) | copy-start | bytes 6148
  8.4 6.9 %copy-start.3 = (bf16[2,2,2048,192]{2,3,1,0:T(8,128)(2,1)S(1)}, bf16[2,2,2048,192]{2,3,1,0:T(8,128)(2,1)}, u32[]{:S(2)}) copy-start(bf16[2,2,2048,192]{2,3,1,0:T(8,128)(2,1)} %param.21) | copy-start | bytes 9437188
  9.9 10.6 %all-to-all-start = ((bf16[4,64,512]{2,1,0:T(8,128)(2,1)}), bf16[4,64,512]{2,1,0:T(8,128)(2,1)}, u32[]{:S(2)}, u32[]{:S(2)}) async-start(bf16[4,64,512]{2,1,0:T(8,128)(2,1)} %bitcast.51), calls=%async_computation | async-start | bytes 524288 | tf_op jit(solution)/shard_map/all_to_all | solution.py:405
  15.2 1.0 copy-start.6
  16.2 1.4 copy-start.7
  19.1 1.4 copy-start.4
  20.6 1.7 copy-start.5
  23.3 56.9 %collective-permute-start = (bf16[3,192,2048]{2,1,0:T(8,128)(2,1)S(1)}, bf16[3,192,2048]{2,1,0:T(8,128)(2,1)S(1)}, u32[]{:S(2)}, u32[]{:S(2)}) collective-permute-start(bf16[3,192,2048]{2,1,0:T(8,128)(2,1)S(1)} %get-tuple-element.17), channel_id=1, source_target_pairs={{0,1},{1,0},{2,5},{3,4},{4,3},{5,2},{6,7},{7,6},{8,9},{9,8},{10,13... | collective-permute-start | bytes 7077896 | tf_op jit(solution)/shard_map/ppermute | solution.py:359
  28.3 59.1 %collective-permute-start.2 = (bf16[3,192,2048]{2,1,0:T(8,128)(2,1)}, bf16[3,192,2048]{2,1,0:T(8,128)(2,1)}, u32[]{:S(2)}, u32[]{:S(2)}) collective-permute-start(bf16[3,192,2048]{2,1,0:T(8,128)(2,1)} %get-tuple-element.23), channel_id=1, source_target_pairs={{0,0},{1,1},{2,4},{3,5},{4,2},{5,3},{6,6},{7,7},{8,8},{9,9},{10,12... | collective-permute-start | bytes 7077896 | tf_op jit(solution)/shard_map/ppermute | solution.py:359
  82.1 1.4 copy-start.1
  83.6 24.7 %all-to-all-start.2 = ((bf16[16,80,512]{2,1,0:T(8,128)(2,1)}), bf16[16,80,512]{2,1,0:T(8,128)(2,1)S(1)}, u32[]{:S(2)}, u32[]{:S(2)}) async-start(bf16[16,80,512]{2,1,0:T(8,128)(2,1)} %get-tuple-element.20), calls=%async_computation.2 | async-start | bytes 2621440 | tf_op jit(solution)/shard_map/all_to_all | solution.py:413
  87.3 22.0 %copy-start.8 = (f32[2048]{0:T(1024)S(1)}, f32[2048]{0:T(1024)}, u32[]{:S(2)}) copy-start(f32[2048]{0:T(1024)} %param.18) | copy-start | bytes 24580
  87.3 22.0 %collective-permute-start.1 = (bf16[3,192,2048]{2,1,0:T(8,128)(2,1)}, bf16[3,192,2048]{2,1,0:T(8,128)(2,1)}, u32[]{:S(2)}, u32[]{:S(2)}) collective-permute-start(bf16[3,192,2048]{2,1,0:T(8,128)(2,1)} %copy-done.1), channel_id=1, source_target_pairs={{0,4},{4,0},{1,5},{5,1},{2,6},{6,2},{3,7},{7,3},{8,12},{12,8},{9,1... | collective-permute-start | bytes 7077896 | tf_op jit(solution)/shard_map/ppermute | solution.py:415
  108.3 1.7 copy-start.2
  108.3 5.5 %collective-permute-start.3 = (bf16[3,192,2048]{2,1,0:T(8,128)(2,1)}, bf16[3,192,2048]{2,1,0:T(8,128)(2,1)S(1)}, u32[]{:S(2)}, u32[]{:S(2)}) collective-permute-start(bf16[3,192,2048]{2,1,0:T(8,128)(2,1)} %hold.1.w2), channel_id=1, source_target_pairs={{0,4},{4,0},{1,5},{5,1},{2,6},{6,2},{3,7},{7,3},{8,12},{12,8},{9,1... | collective-permute-start | bytes 7077896 | tf_op jit(solution)/shard_map/ppermute | solution.py:416
  117.6 29.7 %copy-start.13 = (s32[4096]{0:T(1024)S(1)}, s32[4096]{0:T(1024)}, u32[]{:S(2)}) copy-start(s32[4096]{0:T(1024)} %param.23) | copy-start | bytes 49156
  142.1 19.5 %all-to-all-start.4 = ((bf16[8,64,512]{2,1,0:T(8,128)(2,1)}), bf16[8,64,512]{2,1,0:T(8,128)(2,1)S(1)}, u32[]{:S(2)}, u32[]{:S(2)}) async-start(bf16[8,64,512]{2,1,0:T(8,128)(2,1)} %combine_rows.1), calls=%async_computation.4 | async-start | bytes 1048576 | tf_op jit(solution)/shard_map/all_to_all | solution.py:421
  161.6 21.4 %copy-start.12 = (bf16[64,512]{1,0:T(8,128)(2,1)}, bf16[64,512]{1,0:T(8,128)(2,1)S(1)}, u32[]{:S(2)}) copy-start(bf16[64,512]{1,0:T(8,128)(2,1)S(1)} %add_convert_fusion) | copy-start | bytes 196612
  162.5 19.6 %all-to-all-start.5 = ((bf16[64,2,512]{2,1,0:T(2,128)(2,1)}), bf16[64,2,512]{2,1,0:T(2,128)(2,1)S(1)}, u32[]{:S(2)}, u32[]{:S(2)}) async-start(bf16[64,2,512]{2,1,0:T(2,128)(2,1)} %reshape.149), calls=%async_computation.5 | async-start | bytes 262144 | tf_op jit(solution)/shard_map/all_to_all | solution.py:427

commit v5 on v4

--- a/solution.py
+++ b/solution.py
@@ -110,7 +110,7 @@
         message_ref[z, :, WIDTH:] = plan_ref[z]
 
 
-def gather_kernel(spread_ref, after_ref, out_ref, target_ref, gate_ref, pick_ref, rows_ref):
+def gather_kernel(spread_ref, out_ref, target_ref, gate_ref, pick_ref, rows_ref):
     low = lax.broadcasted_iota(jnp.int32, (PLANE, 2 * REQ), 1) < REQ
     for pair in range(NZ // 2):
         left = spread_ref[2 * pair, :, WIDTH:].astype(jnp.float32)
@@ -271,7 +271,7 @@
     )(pieces, hidden, plan, *blocks)
 
 
-def gather_rows(spread, after):
+def gather_rows(spread):
     return pl.pallas_call(
         gather_kernel,
         out_shape=(
@@ -279,7 +279,7 @@
             shape(PLANE, TOKENS, dtype=jnp.float32),
             shape(PLANE, TOKENS, dtype=jnp.float32),
         ),
-        in_specs=[vmem(), anywhere()],
+        in_specs=[vmem()],
         out_specs=(vmem(), vmem(), vmem()),
         scratch_shapes=[
             pltpu.VMEM((PLANE * BLOCK, TOKENS), jnp.bfloat16),
@@ -287,7 +287,7 @@
         ],
         compiler_params=params(),
         name="gather_rows",
-    )(spread, after)
+    )(spread)
 
 
 def hold(after, block):
@@ -409,13 +409,13 @@
     swap = [(0, 1), (1, 0)]
 
     spread = lax.all_to_all(message, "z", 0, 0, tiled=True)
-    send, target, gate = gather_rows(spread, odd)
+    send, target, gate = gather_rows(spread)
     rows = lax.all_to_all(send, ("x", "y"), 0, 0, tiled=True)
-    even = hold(rows, even)
+    odd = hold(rows, odd)
+    even_swapped = lax.ppermute(even, "c", swap)
     odd_swapped = lax.ppermute(odd, "c", swap)
-    even_swapped = lax.ppermute(even, "c", swap)
-    normed, half = first_half(rows, moe_gain.reshape(1, WIDTH), (odd, odd_swapped))
-    done = second_half(normed, half, (even, even_swapped))
+    normed, half = first_half(rows, moe_gain.reshape(1, WIDTH), (even, even_swapped))
+    done = second_half(normed, half, (odd, odd_swapped))
     back = lax.all_to_all(done, ("x", "y"), 0, 0, tiled=True)
     part = combine_rows(target, gate, back)
     part = lax.all_to_all(part, "z", 0, 0, tiled=True)

time: 185 us -> 175 us (0.946)
  waiting for transfers between devices: 76.1 us -> 48.3 us
  starting transfers between devices: 30.6 us -> 51 us
  local copies, waits for them, and re-layouts: 10.4 us -> 5.17 us
    ppermute x2, waiting for transfers between devices: 30.4 us -> 0.01 us  [move_weights(): lax.ppermute(block, ('c', 'y'), to)]
    all_to_all x1, starting transfers between devices: 3.7 us -> 20.7 us  [local(): rows = lax.all_to_all(send, ('x', 'y'), 0, 0, tiled=True)]
    unnamed x30 -> x22, local copies, waits for them, and re-layouts: 8.55 us -> 3.38 us
    all_to_all x1, starting transfers between devices: 5.21 us -> 8.21 us  [local(): part = lax.all_to_all(part, 'z', 0, 0, tiled=True)]
  transfers between devices with their start and end apart: 8 -> 8, of which waited for: 5 -> 5; matrix products, arithmetic and copies ran while one was open for 0% -> 1% of each run, Pallas kernels for 4% -> 5%
where the time goes in v5:
time: 175 us; the launch traced here: 173 us
  starting transfers between devices  51 us (29%)
  waiting for transfers between devices  48.3 us (28%)
  blocking collectives  43.2 us (25%)
  Pallas kernels  14.9 us (9%)
  matrix products  6.6 us (4%)
  local copies, waits for them, and re-layouts  5.17 us (3%)
  other arithmetic  2.56 us (1%)
    all_to_all x1, blocking collectives, local(): back = lax.all_to_all(done, ('x', 'y'), 0, 0, tiled=True)  24 us
    all_to_all x1, waiting for transfers between devices, local(): rows = lax.all_to_all(send, ('x', 'y'), 0, 0, tiled=True)  21 us
    all_to_all x1, starting transfers between devices, local(): rows = lax.all_to_all(send, ('x', 'y'), 0, 0, tiled=True)  20.7 us
    all_to_all x1, blocking collectives, local(): spread = lax.all_to_all(message, 'z', 0, 0, tiled=True)  19.2 us
    all_to_all x1, waiting for transfers between devices, local(): part = lax.all_to_all(part, 'z', 0, 0, tiled=True)  15.2 us
    all_to_all x1, waiting for transfers between devices, local(): lax.all_to_all(leaving.reshape(SECTIONS, HCAP, QUARTER), ('z', 'x', 'c'),...  11 us
    all_to_all x1, starting transfers between devices, local(): part = lax.all_to_all(part, 'z', 0, 0, tiled=True)  8.21 us
    all_to_all x1, starting transfers between devices, local(): lax.all_to_all(leaving.reshape(SECTIONS, HCAP, QUARTER), ('z', 'x', 'c'),...  6.79 us
  transfers between devices with their start and end apart: 8, of which 5 were waited for; matrix products, arithmetic and copies ran while one was open for 1% of the time, Pallas kernels for 5%

profile of v5, /device:TPU:1, one launch (start us, length us, event | category | flops | bytes accessed | tf_op | source)
XLA Modules:
  0.0 172.7 jit_solution(3550003664144795228)
XLA Ops:
  0.6 1.0 copy.33
  2.4 0.9 fusion.30
  3.5 2.6 %fusion.31 = (f32[64,8]{1,0:T(8,128)S(1)}, f32[64,8,96]{2,1,0:T(8,128)S(1)}) fusion(bf16[64,8,128]{2,1,0:T(8,128)(2,1)S(1)} %bitcast.58, bf16[64,2,96,128]{3,2,1,0:T(8,128)(2,1)} %param.15, pred[64,96]{1,0:T(8,128)(4,1)S(1)} %iota_compare_fusion.7), kind=kOutput, calls=%fused_computation.48 | convolution fusion | flops 12729856 | bytes 1908736 | tf_op jit(solution)/shard_map/rkgd,rckd->rkgc/dot_general | solution.py:38
  6.3 2.0 %fusion.15 = bf16[64,8,128]{2,1,0:T(8,128)(2,1)S(1)} fusion(bf16[64,2,96,128]{3,2,1,0:T(8,128)(2,1)} %param.15, f32[64,8,96]{2,1,0:T(8,128)S(1)} %get-tuple-element.29, f32[64,128]{1,0:T(8,128)S(1)} %bitcast.63, f32[64,8]{1,0:T(8,128)S(1)} %get-tuple-element.25, f32[64,8]{1,0:T(8,128)S(1)} %get-tuple-element.24, f32[64,8]{1,0:T(8,128)S(1)} %multiply_maximum_fusion), kind=kOutput, calls=%fused_computation.11 | convolution fusion | flops 12926976 | bytes 1939456 | tf_op jit(solution)/shard_map/rkgc,rckd->rkgd/dot_general | solution.py:53
  9.9 5.0 %all-to-all-start = ((bf16[4,64,512]{2,1,0:T(8,128)(2,1)}), bf16[4,64,512]{2,1,0:T(8,128)(2,1)}, u32[]{:S(2)}, u32[]{:S(2)}) async-start(bf16[4,64,512]{2,1,0:T(8,128)(2,1)} %bitcast.51), calls=%async_computation | async-start | bytes 524288 | tf_op jit(solution)/shard_map/all_to_all | solution.py:405
  15.2 0.9 copy-done.2
  16.2 1.4 copy-done.3
  17.6 2.2 %pick_weights.1 = (bf16[3,192,2048]{2,1,0:T(8,128)(2,1)}, bf16[3,192,2048]{2,1,0:T(8,128)(2,1)}) custom-call(s32[1]{0:T(128)} %bitcast.10.first_ref, bf16[4,64,512]{2,1,0:T(8,128)(2,1)S(1)} %bitcast.52, bf16[2,2,192,2048]{3,2,1,0:T(8,128)(2,1)S(1)} %bitcast.50, bf16[2,192,2048]{2,1,0:T(8,128)(2,1)S(1)} %copy-done.3), custom_call_target="tpu_custom_call" | custom-call | tf_op jit(solution)/shard_map/pick_weights/pallas_call | solution.py:246
  20.6 1.0 sum_middle.1
  21.6 6.5 %collective-permute-start = (bf16[3,192,2048]{2,1,0:T(8,128)(2,1)}, bf16[3,192,2048]{2,1,0:T(8,128)(2,1)}, u32[]{:S(2)}, u32[]{:S(2)}) collective-permute-start(bf16[3,192,2048]{2,1,0:T(8,128)(2,1)} %get-tuple-element.20), channel_id=1, source_target_pairs={{0,0},{1,1},{2,4},{3,5},{4,2},{5,3},{6,6},{7,7},{8,8},{9,9},{10,12... | collective-permute-start | bytes 7077896 | tf_op jit(solution)/shard_map/ppermute | solution.py:359
  28.2 19.2 %all_to_all.30.spread_ref = bf16[8,16,2176]{2,1,0:T(8,128)(2,1)S(1)} all-to-all(bf16[8,16,2176]{2,1,0:T(8,128)(2,1)S(1)} %get-tuple-element.16), channel_id=1, replica_groups=mesh['z'=8,'x'=4,'c'=2,'y'=4] {'z'}, dimensions={0} | all-to-all | bytes 1114112 | tf_op jit(solution)/shard_map/all_to_all | solution.py:411
  47.5 2.0 %gather_rows.1 = (bf16[16,80,512]{2,1,0:T(8,128)(2,1)}, f32[16,512]{1,0:T(8,128)S(1)}, f32[16,512]{1,0:T(8,128)S(1)}) custom-call(bf16[8,16,2176]{2,1,0:T(8,128)(2,1)S(1)} %all_to_all.30.spread_ref), custom_call_target="tpu_custom_call" | custom-call | tf_op jit(solution)/shard_map/gather_rows/pallas_call | solution.py:275
  49.4 20.7 %all-to-all-start.2 = ((bf16[16,80,512]{2,1,0:T(8,128)(2,1)}), bf16[16,80,512]{2,1,0:T(8,128)(2,1)S(1)}, u32[]{:S(2)}, u32[]{:S(2)}) async-start(bf16[16,80,512]{2,1,0:T(8,128)(2,1)} %get-tuple-element.19), calls=%async_computation.2 | async-start | bytes 2621440 | tf_op jit(solution)/shard_map/all_to_all | solution.py:413
  70.2 2.5 %collective-permute-start.1 = (bf16[3,192,2048]{2,1,0:T(8,128)(2,1)}, bf16[3,192,2048]{2,1,0:T(8,128)(2,1)}, u32[]{:S(2)}, u32[]{:S(2)}) collective-permute-start(bf16[3,192,2048]{2,1,0:T(8,128)(2,1)} %collective-permute-done.w0), channel_id=1, source_target_pairs={{0,4},{4,0},{1,5},{5,1},{2,6},{6,2},{3,7},{7,3},{8,12},{12,8},{9,1... | collective-permute-start | bytes 7077896 | tf_op jit(solution)/shard_map/ppermute | solution.py:415
  72.7 21.0 %all-to-all-done.2.rows_ref.refs_0_ = bf16[16,80,512]{2,1,0:T(8,128)(2,1)S(1)} async-done(((bf16[16,80,512]{2,1,0:T(8,128)(2,1)}), bf16[16,80,512]{2,1,0:T(8,128)(2,1)S(1)}, u32[]{:S(2)}, u32[]{:S(2)}) %all-to-all-start.2) | async-done | bytes 1310752 | tf_op jit(solution)/shard_map/all_to_all | solution.py:413
  93.7 1.2 collective-permute-start.3
  94.9 4.0 %first_half.1 = (bf16[320,2048]{1,0:T(8,128)(2,1)S(1)}, f32[320,2048]{1,0:T(8,128)S(1)}) custom-call(bf16[16,80,512]{2,1,0:T(8,128)(2,1)S(1)} %all-to-all-done.2.rows_ref.refs_0_, f32[1,2048]{1,0:T(1,128)S(1)} %bitcast.53, bf16[3,192,2048]{2,1,0:T(8,128)(2,1)} %collective-permute-done.w0, bf16[3,192,2048]{2,1,0:T(8,128)(2,1)} %collective-permute-done.1.w1), custom_call_target="tpu_custom_call" | custom-call | tf_op jit(solution)/shard_map/first_half/pallas_call | solution.py:329
  99.2 3.8 %second_half.1 = bf16[16,80,512]{2,1,0:T(8,128)(2,1)S(1)} custom-call(bf16[320,2048]{1,0:T(8,128)(2,1)S(1)} %get-tuple-element.21.normed_ref, f32[320,2048]{1,0:T(8,128)S(1)} %get-tuple-element.22.part_ref, bf16[3,192,2048]{2,1,0:T(8,128)(2,1)} %hold.1.w2, bf16[3,192,2048]{2,1,0:T(8,128)(2,1)S(1)} %collective-permute-done.3.w3), custom_call_target="tpu_custom_call" | custom-call | tf_op jit(solution)/shard_map/second_half/pallas_call | solution.py:341
  103.1 24.0 %all_to_all.31.rows_ref = bf16[16,80,512]{2,1,0:T(8,128)(2,1)S(1)} all-to-all(bf16[16,80,512]{2,1,0:T(8,128)(2,1)S(1)} %second_half.1), channel_id=1, replica_groups=mesh['z'=8,'x'=4,'c'=2,'y'=4] {'x','y'}, dimensions={0} | all-to-all | bytes 2621440 | tf_op jit(solution)/shard_map/all_to_all | solution.py:419
  127.0 1.7 combine_rows.1
  128.7 8.2 %all-to-all-start.4 = ((bf16[8,64,512]{2,1,0:T(8,128)(2,1)}), bf16[8,64,512]{2,1,0:T(8,128)(2,1)S(1)}, u32[]{:S(2)}, u32[]{:S(2)}) async-start(bf16[8,64,512]{2,1,0:T(8,128)(2,1)} %combine_rows.1), calls=%async_computation.4 | async-start | bytes 1048576 | tf_op jit(solution)/shard_map/all_to_all | solution.py:421
  137.4 15.2 %all-to-all-done.4 = bf16[8,64,512]{2,1,0:T(8,128)(2,1)S(1)} async-done(((bf16[8,64,512]{2,1,0:T(8,128)(2,1)}), bf16[8,64,512]{2,1,0:T(8,128)(2,1)S(1)}, u32[]{:S(2)}, u32[]{:S(2)}) %all-to-all-start.4) | async-done | bytes 524320 | tf_op jit(solution)/shard_map/all_to_all | solution.py:421
  153.6 6.8 %all-to-all-start.5 = ((bf16[64,2,512]{2,1,0:T(2,128)(2,1)}), bf16[64,2,512]{2,1,0:T(2,128)(2,1)S(1)}, u32[]{:S(2)}, u32[]{:S(2)}) async-start(bf16[64,2,512]{2,1,0:T(2,128)(2,1)} %reshape.149), calls=%async_computation.5 | async-start | bytes 262144 | tf_op jit(solution)/shard_map/all_to_all | solution.py:427
  160.8 11.0 %all-to-all-done.5 = bf16[64,2,512]{2,1,0:T(2,128)(2,1)S(1)} async-done(((bf16[64,2,512]{2,1,0:T(2,128)(2,1)}), bf16[64,2,512]{2,1,0:T(2,128)(2,1)S(1)}, u32[]{:S(2)}, u32[]{:S(2)}) %all-to-all-start.5) | async-done | bytes 131104 | tf_op jit(solution)/shard_map/all_to_all | solution.py:427
  (50 shorter events, 7.0 us)
Async XLA Ops:
  0.6 19.2 %copy-start = (bf16[64,2048]{1,0:T(8,128)(2,1)S(1)}, bf16[64,2048]{1,0:T(8,128)(2,1)}, u32[]{:S(2)}) copy-start(bf16[64,2048]{1,0:T(8,128)(2,1)} %param.12) | copy-start | bytes 786436
  3.5 4.9 %copy-start.7 = (bf16[1024,2048]{1,0:T(8,128)(2,1)S(1)}, bf16[1024,2048]{1,0:T(8,128)(2,1)}, u32[]{:S(2)}) copy-start(bf16[1024,2048]{1,0:T(8,128)(2,1)} %param.17) | copy-start | bytes 12582916
  8.3 6.6 %copy-start.5 = (s32[64,8]{0,1:T(8,128)S(1)}, s32[64,8]{0,1:T(8,128)}, u32[]{:S(2)}) copy-start(s32[64,8]{0,1:T(8,128)} %param.19) | copy-start | bytes 6148
  8.3 6.6 %copy-start.6 = (f32[64,8]{0,1:T(8,128)S(1)}, f32[64,8]{0,1:T(8,128)}, u32[]{:S(2)}) copy-start(f32[64,8]{0,1:T(8,128)} %param.20) | copy-start | bytes 6148
  8.4 6.9 %copy-start.1 = (bf16[2,2,2048,192]{2,3,1,0:T(8,128)(2,1)S(1)}, bf16[2,2,2048,192]{2,3,1,0:T(8,128)(2,1)}, u32[]{:S(2)}) copy-start(bf16[2,2,2048,192]{2,3,1,0:T(8,128)(2,1)} %param.21) | copy-start | bytes 9437188
  9.9 10.6 %all-to-all-start = ((bf16[4,64,512]{2,1,0:T(8,128)(2,1)}), bf16[4,64,512]{2,1,0:T(8,128)(2,1)}, u32[]{:S(2)}, u32[]{:S(2)}) async-start(bf16[4,64,512]{2,1,0:T(8,128)(2,1)} %bitcast.51), calls=%async_computation | async-start | bytes 524288 | tf_op jit(solution)/shard_map/all_to_all | solution.py:405
  15.2 1.0 copy-start.2
  16.2 1.4 copy-start.3
  21.6 48.6 %collective-permute-start = (bf16[3,192,2048]{2,1,0:T(8,128)(2,1)}, bf16[3,192,2048]{2,1,0:T(8,128)(2,1)}, u32[]{:S(2)}, u32[]{:S(2)}) collective-permute-start(bf16[3,192,2048]{2,1,0:T(8,128)(2,1)} %get-tuple-element.20), channel_id=1, source_target_pairs={{0,0},{1,1},{2,4},{3,5},{4,2},{5,3},{6,6},{7,7},{8,8},{9,9},{10,12... | collective-permute-start | bytes 7077896 | tf_op jit(solution)/shard_map/ppermute | solution.py:359
  28.1 65.6 %collective-permute-start.2 = (bf16[3,192,2048]{2,1,0:T(8,128)(2,1)}, bf16[3,192,2048]{2,1,0:T(8,128)(2,1)}, u32[]{:S(2)}, u32[]{:S(2)}) collective-permute-start(bf16[3,192,2048]{2,1,0:T(8,128)(2,1)} %get-tuple-element.23), channel_id=1, source_target_pairs={{0,1},{1,0},{2,5},{3,4},{4,3},{5,2},{6,7},{7,6},{8,9},{9,8},{10,13... | collective-permute-start | bytes 7077896 | tf_op jit(solution)/shard_map/ppermute | solution.py:359
  49.4 44.3 %all-to-all-start.2 = ((bf16[16,80,512]{2,1,0:T(8,128)(2,1)}), bf16[16,80,512]{2,1,0:T(8,128)(2,1)S(1)}, u32[]{:S(2)}, u32[]{:S(2)}) async-start(bf16[16,80,512]{2,1,0:T(8,128)(2,1)} %get-tuple-element.19), calls=%async_computation.2 | async-start | bytes 2621440 | tf_op jit(solution)/shard_map/all_to_all | solution.py:413
  70.1 24.7 %copy-start.4 = (f32[2048]{0:T(1024)S(1)}, f32[2048]{0:T(1024)}, u32[]{:S(2)}) copy-start(f32[2048]{0:T(1024)} %param.18) | copy-start | bytes 24580
  70.2 24.7 %collective-permute-start.1 = (bf16[3,192,2048]{2,1,0:T(8,128)(2,1)}, bf16[3,192,2048]{2,1,0:T(8,128)(2,1)}, u32[]{:S(2)}, u32[]{:S(2)}) collective-permute-start(bf16[3,192,2048]{2,1,0:T(8,128)(2,1)} %collective-permute-done.w0), channel_id=1, source_target_pairs={{0,4},{4,0},{1,5},{5,1},{2,6},{6,2},{3,7},{7,3},{8,12},{12,8},{9,1... | collective-permute-start | bytes 7077896 | tf_op jit(solution)/shard_map/ppermute | solution.py:415
  93.7 5.5 %collective-permute-start.3 = (bf16[3,192,2048]{2,1,0:T(8,128)(2,1)}, bf16[3,192,2048]{2,1,0:T(8,128)(2,1)S(1)}, u32[]{:S(2)}, u32[]{:S(2)}) collective-permute-start(bf16[3,192,2048]{2,1,0:T(8,128)(2,1)} %hold.1.w2), channel_id=1, source_target_pairs={{0,4},{4,0},{1,5},{5,1},{2,6},{6,2},{3,7},{7,3},{8,12},{12,8},{9,1... | collective-permute-start | bytes 7077896 | tf_op jit(solution)/shard_map/ppermute | solution.py:416
  103.0 33.9 %copy-start.9 = (s32[4096]{0:T(1024)S(1)}, s32[4096]{0:T(1024)}, u32[]{:S(2)}) copy-start(s32[4096]{0:T(1024)} %param.23) | copy-start | bytes 49156
  128.7 23.9 %all-to-all-start.4 = ((bf16[8,64,512]{2,1,0:T(8,128)(2,1)}), bf16[8,64,512]{2,1,0:T(8,128)(2,1)S(1)}, u32[]{:S(2)}, u32[]{:S(2)}) async-start(bf16[8,64,512]{2,1,0:T(8,128)(2,1)} %combine_rows.1), calls=%async_computation.4 | async-start | bytes 1048576 | tf_op jit(solution)/shard_map/all_to_all | solution.py:421
  152.7 19.9 %copy-start.8 = (bf16[64,512]{1,0:T(8,128)(2,1)}, bf16[64,512]{1,0:T(8,128)(2,1)S(1)}, u32[]{:S(2)}) copy-start(bf16[64,512]{1,0:T(8,128)(2,1)S(1)} %add_convert_fusion) | copy-start | bytes 196612
  153.6 18.1 %all-to-all-start.5 = ((bf16[64,2,512]{2,1,0:T(2,128)(2,1)}), bf16[64,2,512]{2,1,0:T(2,128)(2,1)S(1)}, u32[]{:S(2)}, u32[]{:S(2)}) async-start(bf16[64,2,512]{2,1,0:T(2,128)(2,1)} %reshape.149), calls=%async_computation.5 | async-start | bytes 262144 | tf_op jit(solution)/shard_map/all_to_all | solution.py:427

commit v6 on v5

--- a/solution.py
+++ b/solution.py
@@ -19,46 +19,55 @@
 BLOCK = NZ * CAP
 ROWS = REQ // PLANE
 QUARTER = 512
+HEADS = 8
+CTX = 96
+CHUNK = 16
 WIDTH = 2048
 EHQ = 192
 
 
-def attend_local(queries, new_kv, cache, lengths):
-    req_count = queries.shape[0]
-    cached_count = cache.shape[2]
-    kv_local = new_kv.shape[2] // HD
-    group_size = queries.shape[1] // (kv_local * HD)
-    query_heads = queries.reshape(req_count, kv_local, group_size, HD)
-    cache_keys = cache[:, 0].reshape(req_count, cached_count, kv_local, HD)
-    cache_values = cache[:, 1].reshape(req_count, cached_count, kv_local, HD)
-    fresh_keys = new_kv[:, 0].reshape(req_count, kv_local, HD)
-    fresh_values = new_kv[:, 1].reshape(req_count, kv_local, HD)
-    scale_factor = 1.0 / math.sqrt(HD)
-    cache_scores = (
-        jnp.einsum("rkgd,rckd->rkgc", query_heads, cache_keys, preferred_element_type=jnp.float32)
-        * scale_factor
-    )
-    valid_cells = jnp.arange(cached_count)[None, :] < lengths[:, None]
-    cache_scores = jnp.where(valid_cells[:, None, None, :], cache_scores, -jnp.inf)
-    fresh_scores = (
-        jnp.einsum("rkgd,rkd->rkg", query_heads, fresh_keys, preferred_element_type=jnp.float32)
-        * scale_factor
-    )
-    top_score = jnp.maximum(jnp.max(cache_scores, axis=-1), fresh_scores)
-    cache_exp = jnp.exp(cache_scores - top_score[..., None])
-    fresh_exp = jnp.exp(fresh_scores - top_score)
-    total_mass = jnp.sum(cache_exp, axis=-1) + fresh_exp
-    cache_weights = (cache_exp / total_mass[..., None]).astype(jnp.bfloat16)
-    fresh_weights = (fresh_exp / total_mass).astype(jnp.bfloat16)
-    context = jnp.einsum(
-        "rkgc,rckd->rkgd", cache_weights, cache_values, preferred_element_type=jnp.float32
-    )
-    context = (
-        context
-        + fresh_weights.astype(jnp.float32)[..., None]
-        * fresh_values.astype(jnp.float32)[:, :, None, :]
-    )
-    return context.reshape(req_count, kv_local * group_size * HD).astype(jnp.bfloat16)
+def attention_kernel(lengths_ref, queries_ref, fresh_ref, cache, weight, out_ref, *scratch):
+    cache_ref, weight_ref, context_ref, cache_sem, weight_sem = scratch
+    loads = []
+    for i in range(REQ // CHUNK):
+        rows = pl.ds(i * CHUNK, CHUNK)
+        loads.append(pltpu.make_async_copy(cache.at[rows], cache_ref.at[rows], cache_sem.at[i]))
+    for copy in loads:
+        copy.start()
+    whole = pltpu.make_async_copy(weight, weight_ref, weight_sem)
+    whole.start()
+    scale = 1.0 / math.sqrt(HD)
+    cell = lax.broadcasted_iota(jnp.int32, (HEADS, CTX), 1)
+    for i in range(REQ // CHUNK):
+        rows = slice(i * CHUNK, (i + 1) * CHUNK)
+        heads = queries_ref[rows, :].astype(jnp.float32).reshape(CHUNK, HEADS, HD)
+        fresh = fresh_ref[rows].astype(jnp.float32)
+        loads[i].wait()
+        keys, values = cache_ref[rows, 0], cache_ref[rows, 1]
+        scores = lax.dot_general(
+            heads.astype(jnp.bfloat16), keys, (((2,), (2,)), ((0,), (0,))), preferred_element_type=jnp.float32
+        )
+        scores = scores * scale
+        scores = jnp.stack(
+            [jnp.where(cell < lengths_ref[i * CHUNK + r], scores[r], -jnp.inf) for r in range(CHUNK)]
+        )
+        new = jnp.sum(heads * fresh[:, 0:1, :], axis=-1, keepdims=True) * scale
+        top = jnp.maximum(jnp.max(scores, axis=-1, keepdims=True), new)
+        mass = jnp.exp(scores - top)
+        new = jnp.exp(new - top)
+        total = jnp.sum(mass, axis=-1, keepdims=True) + new
+        mass = (mass / total).astype(jnp.bfloat16)
+        new = (new / total).astype(jnp.bfloat16).astype(jnp.float32)
+        context = lax.dot_general(
+            mass, values, (((2,), (1,)), ((0,), (0,))), preferred_element_type=jnp.float32
+        ) + new * fresh[:, 1:2, :]
+        context_ref[rows, :] = context.reshape(CHUNK, HEADS * HD).astype(jnp.bfloat16)
+    whole.wait()
+    for y in range(NY):
+        out_ref[y] = jnp.dot(
+            context_ref[...], weight_ref[:, y * QUARTER : (y + 1) * QUARTER],
+            preferred_element_type=jnp.float32,
+        ).astype(jnp.bfloat16)
 
 
 def plan_kernel(ids_ref, gates_ref, out_ref):
@@ -230,6 +239,25 @@
     return jax.ShapeDtypeStruct(dims, dtype)
 
 
+def attend(lengths, queries, fresh, cache, weight):
+    hbm = pl.BlockSpec(memory_space=pltpu.HBM)
+    return pl.pallas_call(
+        attention_kernel,
+        out_shape=shape(NY, REQ, QUARTER),
+        in_specs=[pl.BlockSpec(memory_space=pltpu.SMEM), vmem(), vmem(), hbm, hbm],
+        out_specs=vmem(),
+        scratch_shapes=[
+            pltpu.VMEM((REQ, 2, CTX, HD), jnp.bfloat16),
+            pltpu.VMEM((HEADS * HD, WIDTH), jnp.bfloat16),
+            pltpu.VMEM((REQ, HEADS * HD), jnp.bfloat16),
+            pltpu.SemaphoreType.DMA((REQ // CHUNK,)),
+            pltpu.SemaphoreType.DMA,
+        ],
+        compiler_params=params(24),
+        name="attend",
+    )(lengths, queries, fresh, cache, weight)
+
+
 def make_plan(ids, gates):
     return pl.pallas_call(
         plan_kernel,
@@ -353,9 +381,8 @@
     even, odd = [], []
     for c in range(NC):
         for y in range(NY):
-            core = (y // 2) * NY
-            even.append((c * NY + y, core + 2 * c + y % 2))
-            odd.append((c * NY + y, core + 2 * c + 1 - y % 2))
+            even.append((c * NY + y, (1 - y // 2) * NY + 2 * c + y % 2))
+            odd.append((c * NY + y, (y // 2) * NY + 2 * c + 1 - y % 2))
     return [lax.ppermute(block, ("c", "y"), to) for block, to in zip(blocks, (even, odd))]
 
 
@@ -397,9 +424,7 @@
     z, x, c, y = (lax.axis_index(name) for name in ("z", "x", "c", "y"))
     section = (z * NX + x) * NC + c
     plan = make_plan(expert_ids.T, expert_gates.T)
-    context = attend_local(queries, new_kv, cache, lengths)
-    attention = jnp.dot(context, out_weight, preferred_element_type=jnp.float32)
-    pieces = attention.astype(jnp.bfloat16).reshape(REQ, NY, QUARTER).transpose(1, 0, 2)
+    pieces = attend(lengths, queries, new_kv, cache, out_weight)
     first = (y % 2).astype(jnp.int32).reshape(1)
     blocks = pick_weights(first, pieces, gate_up.transpose(0, 1, 3, 2), down)
     pieces = lax.all_to_all(pieces, "y", 0, 0, tiled=True)

time: 175 us -> 174 us (level); the launches traced: 173 us -> 173 us
  starting transfers between devices: 51 us -> 40.9 us
  waiting for transfers between devices: 48.3 us -> 54.8 us
  matrix products: 6.6 us -> 0.99 us
  local copies, waits for them, and re-layouts: 5.17 us -> 10.6 us
  Pallas kernels: 14.9 us -> 19.3 us
  blocking collectives: 43.2 us -> 45.4 us
  other arithmetic: 2.56 us -> 0.66 us
    ppermute x2, waiting for transfers between devices: 0.01 us -> 26.1 us  [move_weights(): lax.ppermute(block, ('c', 'y'), to)]
    all_to_all x1, waiting for transfers between devices: 21 us -> 0.01 us  [local(): rows = lax.all_to_all(send, ('x', 'y'), 0, 0, tiled=True)]
    all_to_all x1, starting transfers between devices: 20.7 us -> 5.29 us  [local(): rows = lax.all_to_all(send, ('x', 'y'), 0, 0, tiled=True)]
    unnamed x22 -> x30, local copies, waits for them, and re-layouts: 3.38 us -> 9.5 us
    ppermute x1, starting transfers between devices: 2.52 us -> 8.17 us  [local(): even_swapped = lax.ppermute(even, 'c', swap)]
    dot_general x4 -> x0, matrix products: 5.61 us -> none  [the longest x1 2.56 us: attend_local(): jnp.einsum('rkgd,rckd->rkgc', query_heads, cache_keys, preferred_element_...]
    all_to_all x1, blocking collectives: 19.2 us -> 23.7 us  [local(): spread = lax.all_to_all(message, 'z', 0, 0, tiled=True)]
    pallas_call x0 -> x1, Pallas kernels: none -> 4.38 us  [attend(): pl.pallas_call(attention_kernel, out_shape=shape(NY, REQ, QUARTER), in_sp...]
  transfers between devices with their start and end apart: 8 -> 8, of which waited for: 5 -> 6; matrix products, arithmetic and copies ran while one was open for 1% -> 1% of each run, Pallas kernels for 5% -> 5%
where the time goes in v6:
time: 174 us; the launch traced here: 173 us
  waiting for transfers between devices  54.8 us (31%)
  blocking collectives  45.4 us (26%)
  starting transfers between devices  40.9 us (24%)
  Pallas kernels  19.3 us (11%)
  local copies, waits for them, and re-layouts  10.6 us (6%)
    ppermute x2, waiting for transfers between devices, move_weights(): lax.ppermute(block, ('c', 'y'), to)  26.1 us
    all_to_all x1, blocking collectives, local(): spread = lax.all_to_all(message, 'z', 0, 0, tiled=True)  23.7 us
    all_to_all x1, blocking collectives, local(): back = lax.all_to_all(done, ('x', 'y'), 0, 0, tiled=True)  21.6 us
    all_to_all x1, waiting for transfers between devices, local(): part = lax.all_to_all(part, 'z', 0, 0, tiled=True)  15.2 us
    all_to_all x1, waiting for transfers between devices, local(): lax.all_to_all(leaving.reshape(SECTIONS, HCAP, QUARTER), ('z', 'x', 'c'),...  11 us
    unnamed x30, local copies, waits for them, and re-layouts  9.5 us
    ppermute x1, starting transfers between devices, local(): even_swapped = lax.ppermute(even, 'c', swap)  8.17 us
    all_to_all x1, starting transfers between devices, local(): part = lax.all_to_all(part, 'z', 0, 0, tiled=True)  7.83 us
  transfers between devices with their start and end apart: 8, of which 6 were waited for; matrix products, arithmetic and copies ran while one was open for 1% of the time, Pallas kernels for 5%

profile of v6, /device:TPU:1, one launch (start us, length us, event | category | flops | bytes accessed | tf_op | source)
XLA Modules:
  0.0 173.4 jit_solution(15423172634144517203)
XLA Ops:
  0.7 2.2 %copy-done.1 = bf16[1024,2048]{1,0:T(8,128)(2,1)S(1)} copy-done((bf16[1024,2048]{1,0:T(8,128)(2,1)S(1)}, bf16[1024,2048]{1,0:T(8,128)(2,1)}, u32[]{:S(2)}) %copy-start.1) | copy-done | bytes 4194328
  2.9 1.9 %copy-done.3 = bf16[64,2,96,128]{3,2,1,0:T(8,128)(2,1)S(1)} copy-done((bf16[64,2,96,128]{3,2,1,0:T(8,128)(2,1)S(1)}, bf16[64,2,96,128]{3,2,1,0:T(8,128)(2,1)}, u32[]{:S(2)}) %copy-start.3) | copy-done | bytes 3145752
  7.1 4.4 %attend.1.after_ref = bf16[4,64,512]{2,1,0:T(8,128)(2,1)S(1)} custom-call(s32[64]{0:T(128)S(1)} %copy-done.12, bf16[64,1024]{1,0:T(8,128)(2,1)S(1)} %copy-done.7, bf16[64,2,128]{2,1,0:T(2,128)(2,1)S(1)} %copy-done.8, bf16[64,2,96,128]{3,2,1,0:T(8,128)(2,1)S(1)} %copy-done.3, bf16[1024,2048]{1,0:T(8,128)(2,1)S(1)} %copy-done.1), custom_call_target="tpu_custom_call" | custom-call | tf_op jit(solution)/shard_map/attend/pallas_call | solution.py:244
  12.2 5.0 %all-to-all-start = ((bf16[4,64,512]{2,1,0:T(8,128)(2,1)}), bf16[4,64,512]{2,1,0:T(8,128)(2,1)}, u32[]{:S(2)}, u32[]{:S(2)}) async-start(bf16[4,64,512]{2,1,0:T(8,128)(2,1)} %copy-done.4), calls=%async_computation | async-start | bytes 524288 | tf_op jit(solution)/shard_map/all_to_all | solution.py:430
  18.4 1.4 copy-done.6
  19.8 2.2 %pick_weights.1 = (bf16[3,192,2048]{2,1,0:T(8,128)(2,1)}, bf16[3,192,2048]{2,1,0:T(8,128)(2,1)}) custom-call(s32[1]{0:T(128)} %bitcast.2.first_ref, bf16[4,64,512]{2,1,0:T(8,128)(2,1)S(1)} %copy-done.5, bf16[2,2,192,2048]{3,2,1,0:T(8,128)(2,1)S(1)} %bitcast.7, bf16[2,192,2048]{2,1,0:T(8,128)(2,1)S(1)} %copy-done.6), custom_call_target="tpu_custom_call" | custom-call | tf_op jit(solution)/shard_map/pick_weights/pallas_call | solution.py:274
  23.8 2.3 %collective-permute-start = (bf16[3,192,2048]{2,1,0:T(8,128)(2,1)}, bf16[3,192,2048]{2,1,0:T(8,128)(2,1)}, u32[]{:S(2)}, u32[]{:S(2)}) collective-permute-start(bf16[3,192,2048]{2,1,0:T(8,128)(2,1)} %get-tuple-element.20), channel_id=1, source_target_pairs={{0,4},{1,5},{2,0},{3,1},{4,6},{5,7},{6,2},{7,3},{8,12},{9,13},{10,... | collective-permute-start | bytes 7077896 | tf_op jit(solution)/shard_map/ppermute | solution.py:386
  26.1 4.0 %collective-permute-start.2 = (bf16[3,192,2048]{2,1,0:T(8,128)(2,1)}, bf16[3,192,2048]{2,1,0:T(8,128)(2,1)}, u32[]{:S(2)}, u32[]{:S(2)}) collective-permute-start(bf16[3,192,2048]{2,1,0:T(8,128)(2,1)} %get-tuple-element.23), channel_id=1, source_target_pairs={{0,1},{1,0},{2,5},{3,4},{4,3},{5,2},{6,7},{7,6},{8,9},{9,8},{10,13... | collective-permute-start | bytes 7077896 | tf_op jit(solution)/shard_map/ppermute | solution.py:386
  30.1 23.7 %all_to_all.30.spread_ref = bf16[8,16,2176]{2,1,0:T(8,128)(2,1)S(1)} all-to-all(bf16[8,16,2176]{2,1,0:T(8,128)(2,1)S(1)} %get-tuple-element.16), channel_id=1, replica_groups=mesh['z'=8,'x'=4,'c'=2,'y'=4] {'z'}, dimensions={0} | all-to-all | bytes 1114112 | tf_op jit(solution)/shard_map/all_to_all | solution.py:436
  53.9 2.0 %gather_rows.1 = (bf16[16,80,512]{2,1,0:T(8,128)(2,1)}, f32[16,512]{1,0:T(8,128)S(1)}, f32[16,512]{1,0:T(8,128)S(1)}) custom-call(bf16[8,16,2176]{2,1,0:T(8,128)(2,1)S(1)} %all_to_all.30.spread_ref), custom_call_target="tpu_custom_call" | custom-call | tf_op jit(solution)/shard_map/gather_rows/pallas_call | solution.py:303
  55.8 5.3 %all-to-all-start.2 = ((bf16[16,80,512]{2,1,0:T(8,128)(2,1)}), bf16[16,80,512]{2,1,0:T(8,128)(2,1)S(1)}, u32[]{:S(2)}, u32[]{:S(2)}) async-start(bf16[16,80,512]{2,1,0:T(8,128)(2,1)} %get-tuple-element.19), calls=%async_computation.2 | async-start | bytes 2621440 | tf_op jit(solution)/shard_map/all_to_all | solution.py:438
  61.2 24.8 %collective-permute-done.w0 = bf16[3,192,2048]{2,1,0:T(8,128)(2,1)} collective-permute-done((bf16[3,192,2048]{2,1,0:T(8,128)(2,1)}, bf16[3,192,2048]{2,1,0:T(8,128)(2,1)}, u32[]{:S(2)}, u32[]{:S(2)}) %collective-permute-start) | collective-permute-done | bytes 2359328 | tf_op jit(solution)/shard_map/ppermute | solution.py:386
  86.0 8.2 %collective-permute-start.1 = (bf16[3,192,2048]{2,1,0:T(8,128)(2,1)}, bf16[3,192,2048]{2,1,0:T(8,128)(2,1)}, u32[]{:S(2)}, u32[]{:S(2)}) collective-permute-start(bf16[3,192,2048]{2,1,0:T(8,128)(2,1)} %collective-permute-done.w0), channel_id=1, source_target_pairs={{0,4},{4,0},{1,5},{5,1},{2,6},{6,2},{3,7},{7,3},{8,12},{12,8},{9,1... | collective-permute-start | bytes 7077896 | tf_op jit(solution)/shard_map/ppermute | solution.py:440
  94.2 1.3 collective-permute-done.2.refs_1_
  95.4 1.5 collective-permute-start.3
  96.9 1.8 %collective-permute-done.1.w1 = bf16[3,192,2048]{2,1,0:T(8,128)(2,1)} collective-permute-done((bf16[3,192,2048]{2,1,0:T(8,128)(2,1)}, bf16[3,192,2048]{2,1,0:T(8,128)(2,1)}, u32[]{:S(2)}, u32[]{:S(2)}) %collective-permute-start.1) | collective-permute-done | bytes 2359328 | tf_op jit(solution)/shard_map/ppermute | solution.py:440
  98.7 4.0 %first_half.1 = (bf16[320,2048]{1,0:T(8,128)(2,1)S(1)}, f32[320,2048]{1,0:T(8,128)S(1)}) custom-call(bf16[16,80,512]{2,1,0:T(8,128)(2,1)S(1)} %all-to-all-done.2.rows_ref.refs_0_, f32[1,2048]{1,0:T(1,128)S(1)} %bitcast.8, bf16[3,192,2048]{2,1,0:T(8,128)(2,1)} %collective-permute-done.w0, bf16[3,192,2048]{2,1,0:T(8,128)(2,1)} %collective-permute-done.1.w1), custom_call_target="tpu_custom_call" | custom-call | tf_op jit(solution)/shard_map/first_half/pallas_call | solution.py:357
  102.7 3.8 %second_half.1 = bf16[16,80,512]{2,1,0:T(8,128)(2,1)S(1)} custom-call(bf16[320,2048]{1,0:T(8,128)(2,1)S(1)} %get-tuple-element.21.normed_ref, f32[320,2048]{1,0:T(8,128)S(1)} %get-tuple-element.22.part_ref, bf16[3,192,2048]{2,1,0:T(8,128)(2,1)} %hold.1.w2, bf16[3,192,2048]{2,1,0:T(8,128)(2,1)S(1)} %collective-permute-done.3.w3), custom_call_target="tpu_custom_call" | custom-call | tf_op jit(solution)/shard_map/second_half/pallas_call | solution.py:369
  106.5 21.6 %all_to_all.31.rows_ref = bf16[16,80,512]{2,1,0:T(8,128)(2,1)S(1)} all-to-all(bf16[16,80,512]{2,1,0:T(8,128)(2,1)S(1)} %second_half.1), channel_id=1, replica_groups=mesh['z'=8,'x'=4,'c'=2,'y'=4] {'x','y'}, dimensions={0} | all-to-all | bytes 2621440 | tf_op jit(solution)/shard_map/all_to_all | solution.py:444
  128.2 1.7 combine_rows.1
  129.8 7.8 %all-to-all-start.4 = ((bf16[8,64,512]{2,1,0:T(8,128)(2,1)}), bf16[8,64,512]{2,1,0:T(8,128)(2,1)S(1)}, u32[]{:S(2)}, u32[]{:S(2)}) async-start(bf16[8,64,512]{2,1,0:T(8,128)(2,1)} %combine_rows.1), calls=%async_computation.4 | async-start | bytes 1048576 | tf_op jit(solution)/shard_map/all_to_all | solution.py:446
  138.2 15.2 %all-to-all-done.4 = bf16[8,64,512]{2,1,0:T(8,128)(2,1)S(1)} async-done(((bf16[8,64,512]{2,1,0:T(8,128)(2,1)}), bf16[8,64,512]{2,1,0:T(8,128)(2,1)S(1)}, u32[]{:S(2)}, u32[]{:S(2)}) %all-to-all-start.4) | async-done | bytes 524320 | tf_op jit(solution)/shard_map/all_to_all | solution.py:446
  154.4 6.8 %all-to-all-start.5 = ((bf16[64,2,512]{2,1,0:T(2,128)(2,1)}), bf16[64,2,512]{2,1,0:T(2,128)(2,1)S(1)}, u32[]{:S(2)}, u32[]{:S(2)}) async-start(bf16[64,2,512]{2,1,0:T(2,128)(2,1)} %reshape.58), calls=%async_computation.5 | async-start | bytes 262144 | tf_op jit(solution)/shard_map/all_to_all | solution.py:452
  161.5 11.0 %all-to-all-done.5 = bf16[64,2,512]{2,1,0:T(2,128)(2,1)S(1)} async-done(((bf16[64,2,512]{2,1,0:T(2,128)(2,1)}), bf16[64,2,512]{2,1,0:T(2,128)(2,1)S(1)}, u32[]{:S(2)}, u32[]{:S(2)}) %all-to-all-start.5) | async-done | bytes 131104 | tf_op jit(solution)/shard_map/all_to_all | solution.py:452
  (49 shorter events, 8.7 us)
Async XLA Ops:
  0.6 21.4 %copy-start = (bf16[64,2048]{1,0:T(8,128)(2,1)S(1)}, bf16[64,2048]{1,0:T(8,128)(2,1)}, u32[]{:S(2)}) copy-start(bf16[64,2048]{1,0:T(8,128)(2,1)} %param.12) | copy-start | bytes 786436
  0.6 2.2 %copy-start.1 = (bf16[1024,2048]{1,0:T(8,128)(2,1)S(1)}, bf16[1024,2048]{1,0:T(8,128)(2,1)}, u32[]{:S(2)}) copy-start(bf16[1024,2048]{1,0:T(8,128)(2,1)} %weight.1) | copy-start | bytes 12582916
  2.9 1.9 %copy-start.3 = (bf16[64,2,96,128]{3,2,1,0:T(8,128)(2,1)S(1)}, bf16[64,2,96,128]{3,2,1,0:T(8,128)(2,1)}, u32[]{:S(2)}) copy-start(bf16[64,2,96,128]{3,2,1,0:T(8,128)(2,1)} %cache.1) | copy-start | bytes 9437188
  4.8 0.9 copy-start.7
  5.7 0.8 copy-start.8
  6.4 0.7 copy-start.12
  7.1 10.1 %copy-start.10 = (s32[64,8]{0,1:T(8,128)S(1)}, s32[64,8]{0,1:T(8,128)}, u32[]{:S(2)}) copy-start(s32[64,8]{0,1:T(8,128)} %param.19) | copy-start | bytes 6148
  7.1 10.1 %copy-start.11 = (f32[64,8]{0,1:T(8,128)S(1)}, f32[64,8]{0,1:T(8,128)}, u32[]{:S(2)}) copy-start(f32[64,8]{0,1:T(8,128)} %param.20) | copy-start | bytes 6148
  7.1 10.4 %copy-start.2 = (bf16[2,2,2048,192]{2,3,1,0:T(8,128)(2,1)S(1)}, bf16[2,2,2048,192]{2,3,1,0:T(8,128)(2,1)}, u32[]{:S(2)}) copy-start(bf16[2,2,2048,192]{2,3,1,0:T(8,128)(2,1)} %param.21) | copy-start | bytes 9437188
  11.5 0.7 copy-start.4
  12.2 10.6 %all-to-all-start = ((bf16[4,64,512]{2,1,0:T(8,128)(2,1)}), bf16[4,64,512]{2,1,0:T(8,128)(2,1)}, u32[]{:S(2)}, u32[]{:S(2)}) async-start(bf16[4,64,512]{2,1,0:T(8,128)(2,1)} %copy-done.4), calls=%async_computation | async-start | bytes 524288 | tf_op jit(solution)/shard_map/all_to_all | solution.py:430
  17.5 1.0 copy-start.5
  18.4 1.4 copy-start.6
  23.8 62.2 %collective-permute-start = (bf16[3,192,2048]{2,1,0:T(8,128)(2,1)}, bf16[3,192,2048]{2,1,0:T(8,128)(2,1)}, u32[]{:S(2)}, u32[]{:S(2)}) collective-permute-start(bf16[3,192,2048]{2,1,0:T(8,128)(2,1)} %get-tuple-element.20), channel_id=1, source_target_pairs={{0,4},{1,5},{2,0},{3,1},{4,6},{5,7},{6,2},{7,3},{8,12},{9,13},{10,... | collective-permute-start | bytes 7077896 | tf_op jit(solution)/shard_map/ppermute | solution.py:386
  26.1 69.3 %collective-permute-start.2 = (bf16[3,192,2048]{2,1,0:T(8,128)(2,1)}, bf16[3,192,2048]{2,1,0:T(8,128)(2,1)}, u32[]{:S(2)}, u32[]{:S(2)}) collective-permute-start(bf16[3,192,2048]{2,1,0:T(8,128)(2,1)} %get-tuple-element.23), channel_id=1, source_target_pairs={{0,1},{1,0},{2,5},{3,4},{4,3},{5,2},{6,7},{7,6},{8,9},{9,8},{10,13... | collective-permute-start | bytes 7077896 | tf_op jit(solution)/shard_map/ppermute | solution.py:386
  55.8 38.3 %all-to-all-start.2 = ((bf16[16,80,512]{2,1,0:T(8,128)(2,1)}), bf16[16,80,512]{2,1,0:T(8,128)(2,1)S(1)}, u32[]{:S(2)}, u32[]{:S(2)}) async-start(bf16[16,80,512]{2,1,0:T(8,128)(2,1)} %get-tuple-element.19), calls=%async_computation.2 | async-start | bytes 2621440 | tf_op jit(solution)/shard_map/all_to_all | solution.py:438
  61.1 37.5 %copy-start.9 = (f32[2048]{0:T(1024)S(1)}, f32[2048]{0:T(1024)}, u32[]{:S(2)}) copy-start(f32[2048]{0:T(1024)} %param.18) | copy-start | bytes 24580
  86.0 12.7 %collective-permute-start.1 = (bf16[3,192,2048]{2,1,0:T(8,128)(2,1)}, bf16[3,192,2048]{2,1,0:T(8,128)(2,1)}, u32[]{:S(2)}, u32[]{:S(2)}) collective-permute-start(bf16[3,192,2048]{2,1,0:T(8,128)(2,1)} %collective-permute-done.w0), channel_id=1, source_target_pairs={{0,4},{4,0},{1,5},{5,1},{2,6},{6,2},{3,7},{7,3},{8,12},{12,8},{9,1... | collective-permute-start | bytes 7077896 | tf_op jit(solution)/shard_map/ppermute | solution.py:440
  95.4 7.3 %collective-permute-start.3 = (bf16[3,192,2048]{2,1,0:T(8,128)(2,1)}, bf16[3,192,2048]{2,1,0:T(8,128)(2,1)S(1)}, u32[]{:S(2)}, u32[]{:S(2)}) collective-permute-start(bf16[3,192,2048]{2,1,0:T(8,128)(2,1)} %hold.1.w2), channel_id=1, source_target_pairs={{0,4},{4,0},{1,5},{5,1},{2,6},{6,2},{3,7},{7,3},{8,12},{12,8},{9,1... | collective-permute-start | bytes 7077896 | tf_op jit(solution)/shard_map/ppermute | solution.py:441
  106.5 31.2 %copy-start.14 = (s32[4096]{0:T(1024)S(1)}, s32[4096]{0:T(1024)}, u32[]{:S(2)}) copy-start(s32[4096]{0:T(1024)} %param.23) | copy-start | bytes 49156
  129.8 23.5 %all-to-all-start.4 = ((bf16[8,64,512]{2,1,0:T(8,128)(2,1)}), bf16[8,64,512]{2,1,0:T(8,128)(2,1)S(1)}, u32[]{:S(2)}, u32[]{:S(2)}) async-start(bf16[8,64,512]{2,1,0:T(8,128)(2,1)} %combine_rows.1), calls=%async_computation.4 | async-start | bytes 1048576 | tf_op jit(solution)/shard_map/all_to_all | solution.py:446
  153.5 19.9 %copy-start.13 = (bf16[64,512]{1,0:T(8,128)(2,1)}, bf16[64,512]{1,0:T(8,128)(2,1)S(1)}, u32[]{:S(2)}) copy-start(bf16[64,512]{1,0:T(8,128)(2,1)S(1)} %add_convert_fusion) | copy-start | bytes 196612
  154.4 18.2 %all-to-all-start.5 = ((bf16[64,2,512]{2,1,0:T(2,128)(2,1)}), bf16[64,2,512]{2,1,0:T(2,128)(2,1)S(1)}, u32[]{:S(2)}, u32[]{:S(2)}) async-start(bf16[64,2,512]{2,1,0:T(2,128)(2,1)} %reshape.58), calls=%async_computation.5 | async-start | bytes 262144 | tf_op jit(solution)/shard_map/all_to_all | solution.py:452

commit v7 on v6

--- a/solution.py
+++ b/solution.py
@@ -107,7 +107,7 @@
         copy.wait()
 
 
-def middle_kernel(pieces_ref, hidden_ref, plan_ref, even, odd, message_ref, middle_ref, *same):
+def middle_kernel(pieces_ref, hidden_ref, plan_ref, message_ref, middle_ref):
     total = hidden_ref[...].astype(jnp.float32)
     for y in range(NY):
         total = total + pieces_ref[y].astype(jnp.float32)
@@ -253,7 +253,7 @@
             pltpu.SemaphoreType.DMA((REQ // CHUNK,)),
             pltpu.SemaphoreType.DMA,
         ],
-        compiler_params=params(24),
+        compiler_params=params(60),
         name="attend",
     )(lengths, queries, fresh, cache, weight)
 
@@ -278,25 +278,20 @@
         + [pl.BlockSpec(memory_space=pltpu.HBM)] * 2,
         out_specs=(anywhere(), anywhere()),
         scratch_shapes=[pltpu.SemaphoreType.DMA((4,))],
-        compiler_params=params(),
+        compiler_params=params(60),
         name="pick_weights",
     )(first, after, gate_up, down)
 
 
-def sum_middle(pieces, hidden, plan, blocks):
+def sum_middle(pieces, hidden, plan):
     return pl.pallas_call(
         middle_kernel,
-        out_shape=(
-            shape(NZ, PLANE, WIDTH + 2 * REQ),
-            shape(REQ, QUARTER),
-            *[shape(*block.shape) for block in blocks],
-        ),
-        in_specs=[vmem()] * 3 + [anywhere()] * 2,
-        out_specs=(vmem(), vmem()) + (anywhere(),) * 2,
-        input_output_aliases={3: 2, 4: 3},
+        out_shape=(shape(NZ, PLANE, WIDTH + 2 * REQ), shape(REQ, QUARTER)),
+        in_specs=[vmem()] * 3,
+        out_specs=(vmem(), vmem()),
         compiler_params=params(),
         name="sum_middle",
-    )(pieces, hidden, plan, *blocks)
+    )(pieces, hidden, plan)
 
 
 def gather_rows(spread):
@@ -429,7 +424,7 @@
     blocks = pick_weights(first, pieces, gate_up.transpose(0, 1, 3, 2), down)
     pieces = lax.all_to_all(pieces, "y", 0, 0, tiled=True)
     hidden = lax.dynamic_slice_in_dim(hidden_in, y * QUARTER, QUARTER, 1)
-    message, middle, *blocks = sum_middle(pieces, hidden, plan, blocks)
+    message, middle = sum_middle(pieces, hidden, plan)
     even, odd = move_weights(blocks)
     swap = [(0, 1), (1, 0)]
 

time: 174 us -> 306 us (1.76)
  Pallas kernels: 19.3 us -> 162 us
  local copies, waits for them, and re-layouts: 10.6 us -> 1.11 us
  starting transfers between devices: 40.9 us -> 35.9 us
    pallas_call x1, Pallas kernels: 2.21 us -> 144 us  [pick_weights(): pl.pallas_call(pick_kernel, out_shape=(block, block), in_specs=[pl.BlockS...]
    unnamed x30 -> x12, local copies, waits for them, and re-layouts: 9.5 us -> 0.04 us
    ppermute x1, starting transfers between devices: 8.17 us -> 3.98 us  [local(): even_swapped = lax.ppermute(even, 'c', swap)]
    ppermute x2, waiting for transfers between devices: 26.1 us -> 29.3 us  [move_weights(): lax.ppermute(block, ('c', 'y'), to)]
  transfers between devices with their start and end apart: 8 -> 8, of which waited for: 6 -> 5; matrix products, arithmetic and copies ran while one was open for 1% -> 0% of each run, Pallas kernels for 5% -> 49%
where the time goes in v7:
time: 306 us
  Pallas kernels  162 us (53%)
  waiting for transfers between devices  56.1 us (18%)
  blocking collectives  48.2 us (16%)
  starting transfers between devices  35.9 us (12%)
    pallas_call x1, Pallas kernels, pick_weights(): pl.pallas_call(pick_kernel, out_shape=(block, block), in_specs=[pl.BlockS...  144 us
    ppermute x2, waiting for transfers between devices, move_weights(): lax.ppermute(block, ('c', 'y'), to)  29.3 us
    all_to_all x1, blocking collectives, local(): spread = lax.all_to_all(message, 'z', 0, 0, tiled=True)  24.4 us
    all_to_all x1, blocking collectives, local(): back = lax.all_to_all(done, ('x', 'y'), 0, 0, tiled=True)  23.8 us
    all_to_all x1, waiting for transfers between devices, local(): part = lax.all_to_all(part, 'z', 0, 0, tiled=True)  15.2 us
    all_to_all x1, waiting for transfers between devices, local(): lax.all_to_all(leaving.reshape(SECTIONS, HCAP, QUARTER), ('z', 'x', 'c'),...  11 us
    all_to_all x1, starting transfers between devices, local(): part = lax.all_to_all(part, 'z', 0, 0, tiled=True)  8.2 us
    all_to_all x1, starting transfers between devices, local(): lax.all_to_all(leaving.reshape(SECTIONS, HCAP, QUARTER), ('z', 'x', 'c'),...  6.79 us
  transfers between devices with their start and end apart: 8, of which 5 were waited for; matrix products, arithmetic and copies ran while one was open for 0% of the time, Pallas kernels for 49%

profile of v7, /device:TPU:1, one launch (start us, length us, event | category | flops | bytes accessed | tf_op | source)
XLA Modules:
  0.0 305.7 jit_solution(6814876901233554751)
XLA Ops:
  0.6 6.1 %attend.1.after_ref = bf16[4,64,512]{2,1,0:T(8,128)(2,1)} custom-call(s32[64]{0:T(128)} %lengths_ref.1, bf16[64,1024]{1,0:T(8,128)(2,1)} %queries_ref.1, bf16[64,2,128]{2,1,0:T(2,128)(2,1)} %fresh_ref.1, bf16[64,2,96,128]{3,2,1,0:T(8,128)(2,1)} %cache.1, bf16[1024,2048]{1,0:T(8,128)(2,1)} %weight.1), custom_call_target="tpu_custom_call" | custom-call | tf_op jit(solution)/shard_map/attend/pallas_call | solution.py:244
  6.8 5.0 %all-to-all-start = ((bf16[4,64,512]{2,1,0:T(8,128)(2,1)}), bf16[4,64,512]{2,1,0:T(8,128)(2,1)S(1)}, u32[]{:S(2)}, u32[]{:S(2)}) async-start(bf16[4,64,512]{2,1,0:T(8,128)(2,1)} %attend.1.after_ref), calls=%async_computation | async-start | bytes 524288 | tf_op jit(solution)/shard_map/all_to_all | solution.py:425
  11.8 144.1 %pick_weights.1 = (bf16[3,192,2048]{2,1,0:T(8,128)(2,1)}, bf16[3,192,2048]{2,1,0:T(8,128)(2,1)}) custom-call(s32[1]{0:T(128)} %bitcast.3.first_ref, bf16[4,64,512]{2,1,0:T(8,128)(2,1)} %attend.1.after_ref, bf16[2,2,192,2048]{3,2,1,0:T(8,128)(2,1)} %bitcast.10, bf16[2,192,2048]{2,1,0:T(8,128)(2,1)} %down.1), custom_call_target="tpu_custom_call" | custom-call | tf_op jit(solution)/shard_map/pick_weights/pallas_call | solution.py:274
  155.9 3.1 collective-permute-start
  158.9 2.9 collective-permute-start.2
  161.9 0.3 plan.1.plan_ref
  162.2 24.4 %all_to_all.30.spread_ref = bf16[8,16,2176]{2,1,0:T(8,128)(2,1)S(1)} all-to-all(bf16[8,16,2176]{2,1,0:T(8,128)(2,1)S(1)} %get-tuple-element.12), channel_id=1, replica_groups=mesh['z'=8,'x'=4,'c'=2,'y'=4] {'z'}, dimensions={0} | all-to-all | bytes 1114112 | tf_op jit(solution)/shard_map/all_to_all | solution.py:431
  186.6 2.0 gather_rows.1
  188.6 4.4 %all-to-all-start.2 = ((bf16[16,80,512]{2,1,0:T(8,128)(2,1)}), bf16[16,80,512]{2,1,0:T(8,128)(2,1)S(1)}, u32[]{:S(2)}, u32[]{:S(2)}) async-start(bf16[16,80,512]{2,1,0:T(8,128)(2,1)} %get-tuple-element.15), calls=%async_computation.2 | async-start | bytes 2621440 | tf_op jit(solution)/shard_map/all_to_all | solution.py:433
  193.0 26.9 %collective-permute-done.w0 = bf16[3,192,2048]{2,1,0:T(8,128)(2,1)} collective-permute-done((bf16[3,192,2048]{2,1,0:T(8,128)(2,1)}, bf16[3,192,2048]{2,1,0:T(8,128)(2,1)}, u32[]{:S(2)}, u32[]{:S(2)}) %collective-permute-start) | collective-permute-done | bytes 2359328 | tf_op jit(solution)/shard_map/ppermute | solution.py:381
  219.9 4.0 %collective-permute-start.1 = (bf16[3,192,2048]{2,1,0:T(8,128)(2,1)}, bf16[3,192,2048]{2,1,0:T(8,128)(2,1)}, u32[]{:S(2)}, u32[]{:S(2)}) collective-permute-start(bf16[3,192,2048]{2,1,0:T(8,128)(2,1)} %collective-permute-done.w0), channel_id=1, source_target_pairs={{0,4},{4,0},{1,5},{5,1},{2,6},{6,2},{3,7},{7,3},{8,12},{12,8},{9,1... | collective-permute-start | bytes 7077896 | tf_op jit(solution)/shard_map/ppermute | solution.py:435
  223.9 2.4 collective-permute-done.2.refs_1_
  226.3 1.5 collective-permute-start.3
  227.8 0.6 collective-permute-done.1.w1
  228.4 4.0 %first_half.1 = (bf16[320,2048]{1,0:T(8,128)(2,1)S(1)}, f32[320,2048]{1,0:T(8,128)S(1)}) custom-call(bf16[16,80,512]{2,1,0:T(8,128)(2,1)S(1)} %all-to-all-done.2.rows_ref.refs_0_, f32[1,2048]{1,0:T(1,128)S(1)} %bitcast.7, bf16[3,192,2048]{2,1,0:T(8,128)(2,1)} %collective-permute-done.w0, bf16[3,192,2048]{2,1,0:T(8,128)(2,1)} %collective-permute-done.1.w1), custom_call_target="tpu_custom_call" | custom-call | tf_op jit(solution)/shard_map/first_half/pallas_call | solution.py:352
  232.4 3.8 %second_half.1 = bf16[16,80,512]{2,1,0:T(8,128)(2,1)S(1)} custom-call(bf16[320,2048]{1,0:T(8,128)(2,1)S(1)} %get-tuple-element.17.normed_ref, f32[320,2048]{1,0:T(8,128)S(1)} %get-tuple-element.18.part_ref, bf16[3,192,2048]{2,1,0:T(8,128)(2,1)} %hold.1.w2, bf16[3,192,2048]{2,1,0:T(8,128)(2,1)S(1)} %collective-permute-done.3.w3), custom_call_target="tpu_custom_call" | custom-call | tf_op jit(solution)/shard_map/second_half/pallas_call | solution.py:364
  236.3 23.8 %all_to_all.31.rows_ref = bf16[16,80,512]{2,1,0:T(8,128)(2,1)S(1)} all-to-all(bf16[16,80,512]{2,1,0:T(8,128)(2,1)S(1)} %second_half.1), channel_id=1, replica_groups=mesh['z'=8,'x'=4,'c'=2,'y'=4] {'x','y'}, dimensions={0} | all-to-all | bytes 2621440 | tf_op jit(solution)/shard_map/all_to_all | solution.py:439
  260.1 1.7 combine_rows.1
  261.8 8.2 %all-to-all-start.4 = ((bf16[8,64,512]{2,1,0:T(8,128)(2,1)}), bf16[8,64,512]{2,1,0:T(8,128)(2,1)S(1)}, u32[]{:S(2)}, u32[]{:S(2)}) async-start(bf16[8,64,512]{2,1,0:T(8,128)(2,1)} %combine_rows.1), calls=%async_computation.4 | async-start | bytes 1048576 | tf_op jit(solution)/shard_map/all_to_all | solution.py:441
  270.5 15.2 %all-to-all-done.4 = bf16[8,64,512]{2,1,0:T(8,128)(2,1)S(1)} async-done(((bf16[8,64,512]{2,1,0:T(8,128)(2,1)}), bf16[8,64,512]{2,1,0:T(8,128)(2,1)S(1)}, u32[]{:S(2)}, u32[]{:S(2)}) %all-to-all-start.4) | async-done | bytes 524320 | tf_op jit(solution)/shard_map/all_to_all | solution.py:441
  286.0 0.7 reshape.58
  286.7 6.8 %all-to-all-start.5 = ((bf16[64,2,512]{2,1,0:T(2,128)(2,1)}), bf16[64,2,512]{2,1,0:T(2,128)(2,1)S(1)}, u32[]{:S(2)}, u32[]{:S(2)}) async-start(bf16[64,2,512]{2,1,0:T(2,128)(2,1)} %reshape.58), calls=%async_computation.5 | async-start | bytes 262144 | tf_op jit(solution)/shard_map/all_to_all | solution.py:447
  293.8 11.0 %all-to-all-done.5 = bf16[64,2,512]{2,1,0:T(2,128)(2,1)S(1)} async-done(((bf16[64,2,512]{2,1,0:T(2,128)(2,1)}), bf16[64,2,512]{2,1,0:T(2,128)(2,1)S(1)}, u32[]{:S(2)}, u32[]{:S(2)}) %all-to-all-start.5) | async-done | bytes 131104 | tf_op jit(solution)/shard_map/all_to_all | solution.py:447
  304.9 0.8 convolution_convert_fusion
  (31 shorter events, 1.3 us)
Async XLA Ops:
  0.6 161.5 %copy-start = (bf16[64,2048]{1,0:T(8,128)(2,1)S(1)}, bf16[64,2048]{1,0:T(8,128)(2,1)}, u32[]{:S(2)}) copy-start(bf16[64,2048]{1,0:T(8,128)(2,1)} %param.12) | copy-start | bytes 786436
  6.8 155.4 %all-to-all-start = ((bf16[4,64,512]{2,1,0:T(8,128)(2,1)}), bf16[4,64,512]{2,1,0:T(8,128)(2,1)S(1)}, u32[]{:S(2)}, u32[]{:S(2)}) async-start(bf16[4,64,512]{2,1,0:T(8,128)(2,1)} %attend.1.after_ref), calls=%async_computation | async-start | bytes 524288 | tf_op jit(solution)/shard_map/all_to_all | solution.py:425
  11.8 150.1 %copy-start.2 = (s32[64,8]{0,1:T(8,128)S(1)}, s32[64,8]{0,1:T(8,128)}, u32[]{:S(2)}) copy-start(s32[64,8]{0,1:T(8,128)} %param.19) | copy-start | bytes 6148
  11.8 150.1 %copy-start.3 = (f32[64,8]{0,1:T(8,128)S(1)}, f32[64,8]{0,1:T(8,128)}, u32[]{:S(2)}) copy-start(f32[64,8]{0,1:T(8,128)} %param.20) | copy-start | bytes 6148
  155.9 64.0 %collective-permute-start = (bf16[3,192,2048]{2,1,0:T(8,128)(2,1)}, bf16[3,192,2048]{2,1,0:T(8,128)(2,1)}, u32[]{:S(2)}, u32[]{:S(2)}) collective-permute-start(bf16[3,192,2048]{2,1,0:T(8,128)(2,1)} %get-tuple-element.16), channel_id=1, source_target_pairs={{0,4},{1,5},{2,0},{3,1},{4,6},{5,7},{6,2},{7,3},{8,12},{9,13},{10,... | collective-permute-start | bytes 7077896 | tf_op jit(solution)/shard_map/ppermute | solution.py:381
  158.9 67.4 %collective-permute-start.2 = (bf16[3,192,2048]{2,1,0:T(8,128)(2,1)}, bf16[3,192,2048]{2,1,0:T(8,128)(2,1)}, u32[]{:S(2)}, u32[]{:S(2)}) collective-permute-start(bf16[3,192,2048]{2,1,0:T(8,128)(2,1)} %get-tuple-element.19), channel_id=1, source_target_pairs={{0,1},{1,0},{2,5},{3,4},{4,3},{5,2},{6,7},{7,6},{8,9},{9,8},{10,13... | collective-permute-start | bytes 7077896 | tf_op jit(solution)/shard_map/ppermute | solution.py:381
  188.6 37.8 %all-to-all-start.2 = ((bf16[16,80,512]{2,1,0:T(8,128)(2,1)}), bf16[16,80,512]{2,1,0:T(8,128)(2,1)S(1)}, u32[]{:S(2)}, u32[]{:S(2)}) async-start(bf16[16,80,512]{2,1,0:T(8,128)(2,1)} %get-tuple-element.15), calls=%async_computation.2 | async-start | bytes 2621440 | tf_op jit(solution)/shard_map/all_to_all | solution.py:433
  193.0 35.4 %copy-start.1 = (f32[2048]{0:T(1024)S(1)}, f32[2048]{0:T(1024)}, u32[]{:S(2)}) copy-start(f32[2048]{0:T(1024)} %param.18) | copy-start | bytes 24580
  219.9 8.5 %collective-permute-start.1 = (bf16[3,192,2048]{2,1,0:T(8,128)(2,1)}, bf16[3,192,2048]{2,1,0:T(8,128)(2,1)}, u32[]{:S(2)}, u32[]{:S(2)}) collective-permute-start(bf16[3,192,2048]{2,1,0:T(8,128)(2,1)} %collective-permute-done.w0), channel_id=1, source_target_pairs={{0,4},{4,0},{1,5},{5,1},{2,6},{6,2},{3,7},{7,3},{8,12},{12,8},{9,1... | collective-permute-start | bytes 7077896 | tf_op jit(solution)/shard_map/ppermute | solution.py:435
  226.3 6.1 %collective-permute-start.3 = (bf16[3,192,2048]{2,1,0:T(8,128)(2,1)}, bf16[3,192,2048]{2,1,0:T(8,128)(2,1)S(1)}, u32[]{:S(2)}, u32[]{:S(2)}) collective-permute-start(bf16[3,192,2048]{2,1,0:T(8,128)(2,1)} %hold.1.w2), channel_id=1, source_target_pairs={{0,4},{4,0},{1,5},{5,1},{2,6},{6,2},{3,7},{7,3},{8,12},{12,8},{9,1... | collective-permute-start | bytes 7077896 | tf_op jit(solution)/shard_map/ppermute | solution.py:436
  236.2 33.7 %copy-start.5 = (s32[4096]{0:T(1024)S(1)}, s32[4096]{0:T(1024)}, u32[]{:S(2)}) copy-start(s32[4096]{0:T(1024)} %param.23) | copy-start | bytes 49156
  261.8 23.9 %all-to-all-start.4 = ((bf16[8,64,512]{2,1,0:T(8,128)(2,1)}), bf16[8,64,512]{2,1,0:T(8,128)(2,1)S(1)}, u32[]{:S(2)}, u32[]{:S(2)}) async-start(bf16[8,64,512]{2,1,0:T(8,128)(2,1)} %combine_rows.1), calls=%async_computation.4 | async-start | bytes 1048576 | tf_op jit(solution)/shard_map/all_to_all | solution.py:441
  285.8 19.9 %copy-start.4 = (bf16[64,512]{1,0:T(8,128)(2,1)}, bf16[64,512]{1,0:T(8,128)(2,1)S(1)}, u32[]{:S(2)}) copy-start(bf16[64,512]{1,0:T(8,128)(2,1)S(1)} %add_convert_fusion) | copy-start | bytes 196612
  286.7 18.1 %all-to-all-start.5 = ((bf16[64,2,512]{2,1,0:T(2,128)(2,1)}), bf16[64,2,512]{2,1,0:T(2,128)(2,1)S(1)}, u32[]{:S(2)}, u32[]{:S(2)}) async-start(bf16[64,2,512]{2,1,0:T(2,128)(2,1)} %reshape.58), calls=%async_computation.5 | async-start | bytes 262144 | tf_op jit(solution)/shard_map/all_to_all | solution.py:447

commit v8 on v7

--- a/solution.py
+++ b/solution.py
@@ -94,16 +94,25 @@
         out_ref[z] = both[z * PLANE : (z + 1) * PLANE, :]
 
 
-def pick_kernel(first_ref, after_ref, gate_up, down, even_ref, odd_ref, sems):
+def pick_kernel(first_ref, after_ref, gate_up, down, even_ref, odd_ref, hold_ref, in_sems, out_sems):
     first = first_ref[0]
-    copies = []
+    loads, stores = [], []
     for k, out in ((0, even_ref), (1, odd_ref)):
         index = first if k == 0 else 1 - first
-        copies.append(pltpu.make_async_copy(gate_up.at[index], out.at[pl.ds(0, 2)], sems.at[2 * k]))
-        copies.append(pltpu.make_async_copy(down.at[index], out.at[2], sems.at[2 * k + 1]))
-    for copy in copies:
+        for part in range(3):
+            source = gate_up.at[index, part] if part < 2 else down.at[index]
+            loads.append(
+                pltpu.make_async_copy(source, hold_ref.at[k, part], in_sems.at[k, part])
+            )
+            stores.append(
+                pltpu.make_async_copy(hold_ref.at[k, part], out.at[part], out_sems.at[k, part])
+            )
+    for copy in loads:
         copy.start()
-    for copy in copies:
+    for load, store in zip(loads, stores):
+        load.wait()
+        store.start()
+    for copy in stores:
         copy.wait()
 
 
@@ -277,7 +286,11 @@
         in_specs=[pl.BlockSpec(memory_space=pltpu.SMEM), anywhere()]
         + [pl.BlockSpec(memory_space=pltpu.HBM)] * 2,
         out_specs=(anywhere(), anywhere()),
-        scratch_shapes=[pltpu.SemaphoreType.DMA((4,))],
+        scratch_shapes=[
+            pltpu.VMEM((2, 3, EHQ, WIDTH), jnp.bfloat16),
+            pltpu.SemaphoreType.DMA((2, 3)),
+            pltpu.SemaphoreType.DMA((2, 3)),
+        ],
         compiler_params=params(60),
         name="pick_weights",
     )(first, after, gate_up, down)

time: 306 us -> 166 us (0.54)
  Pallas kernels: 162 us -> 21.9 us
    pallas_call x1, Pallas kernels: 144 us -> 4.02 us  [pick_weights(): pl.pallas_call(pick_kernel, out_shape=(block, block), in_specs=[pl.BlockS...]
  transfers between devices with their start and end apart: 8 -> 8, of which waited for: 5 -> 5; matrix products, arithmetic and copies ran while one was open for 0% -> 1% of each run, Pallas kernels for 49% -> 6%
where the time goes in v8:
time: 166 us
  waiting for transfers between devices  56.1 us (34%)
  blocking collectives  48.4 us (29%)
  starting transfers between devices  35.7 us (22%)
  Pallas kernels  21.9 us (13%)
    ppermute x2, waiting for transfers between devices, move_weights(): lax.ppermute(block, ('c', 'y'), to)  29.4 us
    all_to_all x1, blocking collectives, local(): spread = lax.all_to_all(message, 'z', 0, 0, tiled=True)  24.5 us
    all_to_all x1, blocking collectives, local(): back = lax.all_to_all(done, ('x', 'y'), 0, 0, tiled=True)  23.9 us
    all_to_all x1, waiting for transfers between devices, local(): part = lax.all_to_all(part, 'z', 0, 0, tiled=True)  15.1 us
    all_to_all x1, waiting for transfers between devices, local(): lax.all_to_all(leaving.reshape(SECTIONS, HCAP, QUARTER), ('z', 'x', 'c'),...  11 us
    all_to_all x1, starting transfers between devices, local(): part = lax.all_to_all(part, 'z', 0, 0, tiled=True)  8.17 us
    all_to_all x1, starting transfers between devices, local(): lax.all_to_all(leaving.reshape(SECTIONS, HCAP, QUARTER), ('z', 'x', 'c'),...  6.81 us
    pallas_call x1, Pallas kernels, attend(): pl.pallas_call(attention_kernel, out_shape=shape(NY, REQ, QUARTER), in_sp...  6.12 us
  transfers between devices with their start and end apart: 8, of which 5 were waited for; matrix products, arithmetic and copies ran while one was open for 1% of the time, Pallas kernels for 6%

profile of v8, /device:TPU:1, one launch (start us, length us, event | category | flops | bytes accessed | tf_op | source)
XLA Modules:
  0.0 165.6 jit_solution(10710964569732601172)
XLA Ops:
  0.6 6.1 %attend.1.after_ref = bf16[4,64,512]{2,1,0:T(8,128)(2,1)} custom-call(s32[64]{0:T(128)} %lengths_ref.1, bf16[64,1024]{1,0:T(8,128)(2,1)} %queries_ref.1, bf16[64,2,128]{2,1,0:T(2,128)(2,1)} %fresh_ref.1, bf16[64,2,96,128]{3,2,1,0:T(8,128)(2,1)} %cache.1, bf16[1024,2048]{1,0:T(8,128)(2,1)} %weight.1), custom_call_target="tpu_custom_call" | custom-call | tf_op jit(solution)/shard_map/attend/pallas_call | solution.py:253
  6.8 5.0 %all-to-all-start = ((bf16[4,64,512]{2,1,0:T(8,128)(2,1)}), bf16[4,64,512]{2,1,0:T(8,128)(2,1)S(1)}, u32[]{:S(2)}, u32[]{:S(2)}) async-start(bf16[4,64,512]{2,1,0:T(8,128)(2,1)} %attend.1.after_ref), calls=%async_computation | async-start | bytes 524288 | tf_op jit(solution)/shard_map/all_to_all | solution.py:438
  11.8 4.0 %pick_weights.1 = (bf16[3,192,2048]{2,1,0:T(8,128)(2,1)}, bf16[3,192,2048]{2,1,0:T(8,128)(2,1)}) custom-call(s32[1]{0:T(128)} %bitcast.3.first_ref, bf16[4,64,512]{2,1,0:T(8,128)(2,1)} %attend.1.after_ref, bf16[2,2,192,2048]{3,2,1,0:T(8,128)(2,1)} %bitcast.10, bf16[2,192,2048]{2,1,0:T(8,128)(2,1)} %down.1), custom_call_target="tpu_custom_call" | custom-call | tf_op jit(solution)/shard_map/pick_weights/pallas_call | solution.py:283
  15.8 3.1 %collective-permute-start = (bf16[3,192,2048]{2,1,0:T(8,128)(2,1)}, bf16[3,192,2048]{2,1,0:T(8,128)(2,1)}, u32[]{:S(2)}, u32[]{:S(2)}) collective-permute-start(bf16[3,192,2048]{2,1,0:T(8,128)(2,1)} %get-tuple-element.16), channel_id=1, source_target_pairs={{0,4},{1,5},{2,0},{3,1},{4,6},{5,7},{6,2},{7,3},{8,12},{9,13},{10,... | collective-permute-start | bytes 7077896 | tf_op jit(solution)/shard_map/ppermute | solution.py:394
  18.9 2.9 %collective-permute-start.2 = (bf16[3,192,2048]{2,1,0:T(8,128)(2,1)}, bf16[3,192,2048]{2,1,0:T(8,128)(2,1)}, u32[]{:S(2)}, u32[]{:S(2)}) collective-permute-start(bf16[3,192,2048]{2,1,0:T(8,128)(2,1)} %get-tuple-element.19), channel_id=1, source_target_pairs={{0,1},{1,0},{2,5},{3,4},{4,3},{5,2},{6,7},{7,6},{8,9},{9,8},{10,13... | collective-permute-start | bytes 7077896 | tf_op jit(solution)/shard_map/ppermute | solution.py:394
  21.8 0.3 plan.1.plan_ref
  22.2 24.5 %all_to_all.30.spread_ref = bf16[8,16,2176]{2,1,0:T(8,128)(2,1)S(1)} all-to-all(bf16[8,16,2176]{2,1,0:T(8,128)(2,1)S(1)} %get-tuple-element.12), channel_id=1, replica_groups=mesh['z'=8,'x'=4,'c'=2,'y'=4] {'z'}, dimensions={0} | all-to-all | bytes 1114112 | tf_op jit(solution)/shard_map/all_to_all | solution.py:444
  46.7 2.0 %gather_rows.1 = (bf16[16,80,512]{2,1,0:T(8,128)(2,1)}, f32[16,512]{1,0:T(8,128)S(1)}, f32[16,512]{1,0:T(8,128)S(1)}) custom-call(bf16[8,16,2176]{2,1,0:T(8,128)(2,1)S(1)} %all_to_all.30.spread_ref), custom_call_target="tpu_custom_call" | custom-call | tf_op jit(solution)/shard_map/gather_rows/pallas_call | solution.py:311
  48.7 4.3 %all-to-all-start.2 = ((bf16[16,80,512]{2,1,0:T(8,128)(2,1)}), bf16[16,80,512]{2,1,0:T(8,128)(2,1)S(1)}, u32[]{:S(2)}, u32[]{:S(2)}) async-start(bf16[16,80,512]{2,1,0:T(8,128)(2,1)} %get-tuple-element.15), calls=%async_computation.2 | async-start | bytes 2621440 | tf_op jit(solution)/shard_map/all_to_all | solution.py:446
  53.0 26.9 %collective-permute-done.w0 = bf16[3,192,2048]{2,1,0:T(8,128)(2,1)} collective-permute-done((bf16[3,192,2048]{2,1,0:T(8,128)(2,1)}, bf16[3,192,2048]{2,1,0:T(8,128)(2,1)}, u32[]{:S(2)}, u32[]{:S(2)}) %collective-permute-start) | collective-permute-done | bytes 2359328 | tf_op jit(solution)/shard_map/ppermute | solution.py:394
  79.9 3.9 %collective-permute-start.1 = (bf16[3,192,2048]{2,1,0:T(8,128)(2,1)}, bf16[3,192,2048]{2,1,0:T(8,128)(2,1)}, u32[]{:S(2)}, u32[]{:S(2)}) collective-permute-start(bf16[3,192,2048]{2,1,0:T(8,128)(2,1)} %collective-permute-done.w0), channel_id=1, source_target_pairs={{0,4},{4,0},{1,5},{5,1},{2,6},{6,2},{3,7},{7,3},{8,12},{12,8},{9,1... | collective-permute-start | bytes 7077896 | tf_op jit(solution)/shard_map/ppermute | solution.py:448
  83.8 2.5 %collective-permute-done.2.refs_1_ = bf16[3,192,2048]{2,1,0:T(8,128)(2,1)} collective-permute-done((bf16[3,192,2048]{2,1,0:T(8,128)(2,1)}, bf16[3,192,2048]{2,1,0:T(8,128)(2,1)}, u32[]{:S(2)}, u32[]{:S(2)}) %collective-permute-start.2) | collective-permute-done | bytes 2359328 | tf_op jit(solution)/shard_map/ppermute | solution.py:394
  86.3 1.5 collective-permute-start.3
  87.7 0.6 collective-permute-done.1.w1
  88.3 4.0 %first_half.1 = (bf16[320,2048]{1,0:T(8,128)(2,1)S(1)}, f32[320,2048]{1,0:T(8,128)S(1)}) custom-call(bf16[16,80,512]{2,1,0:T(8,128)(2,1)S(1)} %all-to-all-done.2.rows_ref.refs_0_, f32[1,2048]{1,0:T(1,128)S(1)} %bitcast.7, bf16[3,192,2048]{2,1,0:T(8,128)(2,1)} %collective-permute-done.w0, bf16[3,192,2048]{2,1,0:T(8,128)(2,1)} %collective-permute-done.1.w1), custom_call_target="tpu_custom_call" | custom-call | tf_op jit(solution)/shard_map/first_half/pallas_call | solution.py:365
  92.4 3.8 %second_half.1 = bf16[16,80,512]{2,1,0:T(8,128)(2,1)S(1)} custom-call(bf16[320,2048]{1,0:T(8,128)(2,1)S(1)} %get-tuple-element.17.normed_ref, f32[320,2048]{1,0:T(8,128)S(1)} %get-tuple-element.18.part_ref, bf16[3,192,2048]{2,1,0:T(8,128)(2,1)} %hold.1.w2, bf16[3,192,2048]{2,1,0:T(8,128)(2,1)S(1)} %collective-permute-done.3.w3), custom_call_target="tpu_custom_call" | custom-call | tf_op jit(solution)/shard_map/second_half/pallas_call | solution.py:377
  96.2 23.9 %all_to_all.31.rows_ref = bf16[16,80,512]{2,1,0:T(8,128)(2,1)S(1)} all-to-all(bf16[16,80,512]{2,1,0:T(8,128)(2,1)S(1)} %second_half.1), channel_id=1, replica_groups=mesh['z'=8,'x'=4,'c'=2,'y'=4] {'x','y'}, dimensions={0} | all-to-all | bytes 2621440 | tf_op jit(solution)/shard_map/all_to_all | solution.py:452
  120.1 1.7 %combine_rows.1 = bf16[8,64,512]{2,1,0:T(8,128)(2,1)} custom-call(f32[16,512]{1,0:T(8,128)S(1)} %get-tuple-element.13.target_ref, f32[16,512]{1,0:T(8,128)S(1)} %get-tuple-element.14.gate_ref, bf16[16,80,512]{2,1,0:T(8,128)(2,1)S(1)} %all_to_all.31.rows_ref), custom_call_target="tpu_custom_call" | custom-call | tf_op jit(solution)/shard_map/combine_rows/pallas_call | solution.py:342
  121.7 8.2 %all-to-all-start.4 = ((bf16[8,64,512]{2,1,0:T(8,128)(2,1)}), bf16[8,64,512]{2,1,0:T(8,128)(2,1)S(1)}, u32[]{:S(2)}, u32[]{:S(2)}) async-start(bf16[8,64,512]{2,1,0:T(8,128)(2,1)} %combine_rows.1), calls=%async_computation.4 | async-start | bytes 1048576 | tf_op jit(solution)/shard_map/all_to_all | solution.py:454
  130.4 15.1 %all-to-all-done.4 = bf16[8,64,512]{2,1,0:T(8,128)(2,1)S(1)} async-done(((bf16[8,64,512]{2,1,0:T(8,128)(2,1)}), bf16[8,64,512]{2,1,0:T(8,128)(2,1)S(1)}, u32[]{:S(2)}, u32[]{:S(2)}) %all-to-all-start.4) | async-done | bytes 524320 | tf_op jit(solution)/shard_map/all_to_all | solution.py:454
  145.9 0.7 reshape.58
  146.6 6.8 %all-to-all-start.5 = ((bf16[64,2,512]{2,1,0:T(2,128)(2,1)}), bf16[64,2,512]{2,1,0:T(2,128)(2,1)S(1)}, u32[]{:S(2)}, u32[]{:S(2)}) async-start(bf16[64,2,512]{2,1,0:T(2,128)(2,1)} %reshape.58), calls=%async_computation.5 | async-start | bytes 262144 | tf_op jit(solution)/shard_map/all_to_all | solution.py:460
  153.7 11.0 %all-to-all-done.5 = bf16[64,2,512]{2,1,0:T(2,128)(2,1)S(1)} async-done(((bf16[64,2,512]{2,1,0:T(2,128)(2,1)}), bf16[64,2,512]{2,1,0:T(2,128)(2,1)S(1)}, u32[]{:S(2)}, u32[]{:S(2)}) %all-to-all-start.5) | async-done | bytes 131104 | tf_op jit(solution)/shard_map/all_to_all | solution.py:460
  164.8 0.8 convolution_convert_fusion
  (31 shorter events, 1.3 us)
Async XLA Ops:
  0.6 21.5 %copy-start = (bf16[64,2048]{1,0:T(8,128)(2,1)S(1)}, bf16[64,2048]{1,0:T(8,128)(2,1)}, u32[]{:S(2)}) copy-start(bf16[64,2048]{1,0:T(8,128)(2,1)} %param.12) | copy-start | bytes 786436
  6.8 15.3 %all-to-all-start = ((bf16[4,64,512]{2,1,0:T(8,128)(2,1)}), bf16[4,64,512]{2,1,0:T(8,128)(2,1)S(1)}, u32[]{:S(2)}, u32[]{:S(2)}) async-start(bf16[4,64,512]{2,1,0:T(8,128)(2,1)} %attend.1.after_ref), calls=%async_computation | async-start | bytes 524288 | tf_op jit(solution)/shard_map/all_to_all | solution.py:438
  11.8 10.0 %copy-start.2 = (s32[64,8]{0,1:T(8,128)S(1)}, s32[64,8]{0,1:T(8,128)}, u32[]{:S(2)}) copy-start(s32[64,8]{0,1:T(8,128)} %param.19) | copy-start | bytes 6148
  11.8 10.0 %copy-start.3 = (f32[64,8]{0,1:T(8,128)S(1)}, f32[64,8]{0,1:T(8,128)}, u32[]{:S(2)}) copy-start(f32[64,8]{0,1:T(8,128)} %param.20) | copy-start | bytes 6148
  15.8 64.0 %collective-permute-start = (bf16[3,192,2048]{2,1,0:T(8,128)(2,1)}, bf16[3,192,2048]{2,1,0:T(8,128)(2,1)}, u32[]{:S(2)}, u32[]{:S(2)}) collective-permute-start(bf16[3,192,2048]{2,1,0:T(8,128)(2,1)} %get-tuple-element.16), channel_id=1, source_target_pairs={{0,4},{1,5},{2,0},{3,1},{4,6},{5,7},{6,2},{7,3},{8,12},{9,13},{10,... | collective-permute-start | bytes 7077896 | tf_op jit(solution)/shard_map/ppermute | solution.py:394
  18.9 67.4 %collective-permute-start.2 = (bf16[3,192,2048]{2,1,0:T(8,128)(2,1)}, bf16[3,192,2048]{2,1,0:T(8,128)(2,1)}, u32[]{:S(2)}, u32[]{:S(2)}) collective-permute-start(bf16[3,192,2048]{2,1,0:T(8,128)(2,1)} %get-tuple-element.19), channel_id=1, source_target_pairs={{0,1},{1,0},{2,5},{3,4},{4,3},{5,2},{6,7},{7,6},{8,9},{9,8},{10,13... | collective-permute-start | bytes 7077896 | tf_op jit(solution)/shard_map/ppermute | solution.py:394
  48.7 37.6 %all-to-all-start.2 = ((bf16[16,80,512]{2,1,0:T(8,128)(2,1)}), bf16[16,80,512]{2,1,0:T(8,128)(2,1)S(1)}, u32[]{:S(2)}, u32[]{:S(2)}) async-start(bf16[16,80,512]{2,1,0:T(8,128)(2,1)} %get-tuple-element.15), calls=%async_computation.2 | async-start | bytes 2621440 | tf_op jit(solution)/shard_map/all_to_all | solution.py:446
  52.9 35.4 %copy-start.1 = (f32[2048]{0:T(1024)S(1)}, f32[2048]{0:T(1024)}, u32[]{:S(2)}) copy-start(f32[2048]{0:T(1024)} %param.18) | copy-start | bytes 24580
  79.9 8.4 %collective-permute-start.1 = (bf16[3,192,2048]{2,1,0:T(8,128)(2,1)}, bf16[3,192,2048]{2,1,0:T(8,128)(2,1)}, u32[]{:S(2)}, u32[]{:S(2)}) collective-permute-start(bf16[3,192,2048]{2,1,0:T(8,128)(2,1)} %collective-permute-done.w0), channel_id=1, source_target_pairs={{0,4},{4,0},{1,5},{5,1},{2,6},{6,2},{3,7},{7,3},{8,12},{12,8},{9,1... | collective-permute-start | bytes 7077896 | tf_op jit(solution)/shard_map/ppermute | solution.py:448
  86.3 6.1 %collective-permute-start.3 = (bf16[3,192,2048]{2,1,0:T(8,128)(2,1)}, bf16[3,192,2048]{2,1,0:T(8,128)(2,1)S(1)}, u32[]{:S(2)}, u32[]{:S(2)}) collective-permute-start(bf16[3,192,2048]{2,1,0:T(8,128)(2,1)} %hold.1.w2), channel_id=1, source_target_pairs={{0,4},{4,0},{1,5},{5,1},{2,6},{6,2},{3,7},{7,3},{8,12},{12,8},{9,1... | collective-permute-start | bytes 7077896 | tf_op jit(solution)/shard_map/ppermute | solution.py:449
  96.2 33.8 %copy-start.5 = (s32[4096]{0:T(1024)S(1)}, s32[4096]{0:T(1024)}, u32[]{:S(2)}) copy-start(s32[4096]{0:T(1024)} %param.23) | copy-start | bytes 49156
  121.7 23.9 %all-to-all-start.4 = ((bf16[8,64,512]{2,1,0:T(8,128)(2,1)}), bf16[8,64,512]{2,1,0:T(8,128)(2,1)S(1)}, u32[]{:S(2)}, u32[]{:S(2)}) async-start(bf16[8,64,512]{2,1,0:T(8,128)(2,1)} %combine_rows.1), calls=%async_computation.4 | async-start | bytes 1048576 | tf_op jit(solution)/shard_map/all_to_all | solution.py:454
  145.7 20.0 %copy-start.4 = (bf16[64,512]{1,0:T(8,128)(2,1)}, bf16[64,512]{1,0:T(8,128)(2,1)S(1)}, u32[]{:S(2)}) copy-start(bf16[64,512]{1,0:T(8,128)(2,1)S(1)} %add_convert_fusion) | copy-start | bytes 196612
  146.6 18.2 %all-to-all-start.5 = ((bf16[64,2,512]{2,1,0:T(2,128)(2,1)}), bf16[64,2,512]{2,1,0:T(2,128)(2,1)S(1)}, u32[]{:S(2)}, u32[]{:S(2)}) async-start(bf16[64,2,512]{2,1,0:T(2,128)(2,1)} %reshape.58), calls=%async_computation.5 | async-start | bytes 262144 | tf_op jit(solution)/shard_map/all_to_all | solution.py:460

commit v9 on v7

--- a/solution.py
+++ b/solution.py
@@ -26,8 +26,24 @@
 EHQ = 192
 
 
-def attention_kernel(lengths_ref, queries_ref, fresh_ref, cache, weight, out_ref, *scratch):
-    cache_ref, weight_ref, context_ref, cache_sem, weight_sem = scratch
+def select_blocks(first, gate_up, down, blocks, hold_ref, in_sems, out_sems):
+    loads, stores = [], []
+    for k, out in enumerate(blocks):
+        index = first if k == 0 else 1 - first
+        for part in range(3):
+            source = gate_up.at[index, part] if part < 2 else down.at[index]
+            loads.append(pltpu.make_async_copy(source, hold_ref.at[k, part], in_sems.at[k, part]))
+            stores.append(
+                pltpu.make_async_copy(hold_ref.at[k, part], out.at[part], out_sems.at[k, part])
+            )
+    return loads, stores
+
+
+def attention_kernel(first_ref, lengths_ref, queries_ref, fresh_ref, cache, weight, *refs):
+    gate_up, down, out_ref, even_ref, odd_ref, cache_ref, weight_ref, context_ref = refs[:8]
+    hold_ref, cache_sem, weight_sem, in_sems, out_sems = refs[8:]
+    blocks = (even_ref, odd_ref)
+    picks, stores = select_blocks(first_ref[0], gate_up, down, blocks, hold_ref, in_sems, out_sems)
     loads = []
     for i in range(REQ // CHUNK):
         rows = pl.ds(i * CHUNK, CHUNK)
@@ -36,6 +52,8 @@
         copy.start()
     whole = pltpu.make_async_copy(weight, weight_ref, weight_sem)
     whole.start()
+    for copy in picks:
+        copy.start()
     scale = 1.0 / math.sqrt(HD)
     cell = lax.broadcasted_iota(jnp.int32, (HEADS, CTX), 1)
     for i in range(REQ // CHUNK):
@@ -62,15 +80,20 @@
             mass, values, (((2,), (1,)), ((0,), (0,))), preferred_element_type=jnp.float32
         ) + new * fresh[:, 1:2, :]
         context_ref[rows, :] = context.reshape(CHUNK, HEADS * HD).astype(jnp.bfloat16)
+    for load, store in zip(picks, stores):
+        load.wait()
+        store.start()
     whole.wait()
     for y in range(NY):
         out_ref[y] = jnp.dot(
             context_ref[...], weight_ref[:, y * QUARTER : (y + 1) * QUARTER],
             preferred_element_type=jnp.float32,
         ).astype(jnp.bfloat16)
-
-
-def plan_kernel(ids_ref, gates_ref, out_ref):
+    for copy in stores:
+        copy.wait()
+
+
+def plan_kernel(ids_ref, gates_ref, even, odd, out_ref, *same):
     ids = jnp.concatenate([ids_ref[...], ids_ref[...]], axis=1)
     gates = jnp.concatenate([gates_ref[...], gates_ref[...]], axis=1)
     gates = gates / jnp.sum(gates, axis=0, keepdims=True)
@@ -92,19 +115,6 @@
     both = jnp.where(first, slot, gate).astype(jnp.bfloat16)
     for z in range(NZ):
         out_ref[z] = both[z * PLANE : (z + 1) * PLANE, :]
-
-
-def pick_kernel(first_ref, after_ref, gate_up, down, even_ref, odd_ref, sems):
-    first = first_ref[0]
-    copies = []
-    for k, out in ((0, even_ref), (1, odd_ref)):
-        index = first if k == 0 else 1 - first
-        copies.append(pltpu.make_async_copy(gate_up.at[index], out.at[pl.ds(0, 2)], sems.at[2 * k]))
-        copies.append(pltpu.make_async_copy(down.at[index], out.at[2], sems.at[2 * k + 1]))
-    for copy in copies:
-        copy.start()
-    for copy in copies:
-        copy.wait()
 
 
 def middle_kernel(pieces_ref, hidden_ref, plan_ref, message_ref, middle_ref):
@@ -166,37 +176,27 @@
         out_ref[z] = total[z * REQ : (z + 1) * REQ, :]
 
 
-def load_weights(blocks, weight_ref, sems):
-    copies = []
-    for part in range(3):
-        for q, block in enumerate(blocks):
-            copies.append(
-                pltpu.make_async_copy(
-                    block.at[part], weight_ref.at[part, pl.ds(q * EHQ, EHQ)], sems.at[part, q]
-                )
-            )
+def load_block(block, weight_ref, sems):
+    copies = [
+        pltpu.make_async_copy(block.at[part], weight_ref.at[part], sems.at[part])
+        for part in range(3)
+    ]
     for copy in copies:
         copy.start()
     return copies
 
 
-def activate(normed_ref, weight_ref, act_ref, copies):
+def activate(normed_ref, block_ref):
     dims = (((1,), (1,)), ((), ()))
-    for copy in copies[:2]:
-        copy.wait()
-    gate = lax.dot_general(
-        normed_ref[...], weight_ref[0], dims, preferred_element_type=jnp.float32
-    )
-    for copy in copies[2:4]:
-        copy.wait()
-    up = lax.dot_general(normed_ref[...], weight_ref[1], dims, preferred_element_type=jnp.float32)
-    act_ref[...] = (gate / (1.0 + jnp.exp(-gate)) * up).astype(jnp.bfloat16)
-    for copy in copies[4:]:
-        copy.wait()
-
-
-def first_half_kernel(rows_ref, gain_ref, w0, w1, normed_ref, part_ref, weight_ref, act_ref, sems):
-    copies = load_weights((w0, w1), weight_ref, sems)
+    gate, up = (
+        lax.dot_general(normed_ref[...], block_ref[k], dims, preferred_element_type=jnp.float32)
+        for k in range(2)
+    )
+    return (gate / (1.0 + jnp.exp(-gate)) * up).astype(jnp.bfloat16)
+
+
+def first_half_kernel(rows_ref, gain_ref, w0, w1, normed_ref, part_ref, w0_ref, w1_ref, sems):
+    copies = load_block(w0, w0_ref, sems.at[0]), load_block(w1, w1_ref, sems.at[1])
     for x in range(NX):
         parts = [rows_ref[x * NY + y].astype(jnp.float32) for y in range(NY)]
         square = sum(jnp.sum(part * part, axis=-1, keepdims=True) for part in parts)
@@ -206,18 +206,29 @@
             normed_ref[x * BLOCK : (x + 1) * BLOCK, columns] = (
                 parts[y] * scale * gain_ref[:, columns]
             ).astype(jnp.bfloat16)
-    activate(normed_ref, weight_ref, act_ref, copies)
-    part_ref[...] = jnp.dot(act_ref[...], weight_ref[2], preferred_element_type=jnp.float32)
-
-
-def second_half_kernel(normed_ref, part_ref, w2, w3, out_ref, weight_ref, act_ref, sems):
-    copies = load_weights((w2, w3), weight_ref, sems)
-    activate(normed_ref, weight_ref, act_ref, copies)
+    for copy in copies[0]:
+        copy.wait()
+    first = activate(normed_ref, w0_ref)
+    for copy in copies[1]:
+        copy.wait()
+    second = activate(normed_ref, w1_ref)
+    part_ref[...] = jnp.dot(first, w0_ref[2], preferred_element_type=jnp.float32) + jnp.dot(
+        second, w1_ref[2], preferred_element_type=jnp.float32
+    )
+
+
+def second_half_kernel(normed_ref, part_ref, w2, w3_ref, out_ref, w2_ref, sems):
+    copies = load_block(w2, w2_ref, sems)
+    second = activate(normed_ref, w3_ref)
+    for copy in copies:
+        copy.wait()
+    first = activate(normed_ref, w2_ref)
     for y in range(NY):
         columns = slice(y * QUARTER, (y + 1) * QUARTER)
         part = part_ref[:, columns] + jnp.dot(
-            act_ref[...], weight_ref[2, :, columns], preferred_element_type=jnp.float32
+            first, w2_ref[2, :, columns], preferred_element_type=jnp.float32
         )
+        part = part + jnp.dot(second, w3_ref[2, :, columns], preferred_element_type=jnp.float32)
         part = part.astype(jnp.bfloat16)
         for x in range(NX):
             out_ref[x * NY + y] = part[x * BLOCK : (x + 1) * BLOCK, :]
@@ -239,48 +250,40 @@
     return jax.ShapeDtypeStruct(dims, dtype)
 
 
-def attend(lengths, queries, fresh, cache, weight):
+def attend(first, lengths, queries, fresh, cache, weight, gate_up, down):
     hbm = pl.BlockSpec(memory_space=pltpu.HBM)
+    smem = pl.BlockSpec(memory_space=pltpu.SMEM)
+    block = shape(3, EHQ, WIDTH)
     return pl.pallas_call(
         attention_kernel,
-        out_shape=shape(NY, REQ, QUARTER),
-        in_specs=[pl.BlockSpec(memory_space=pltpu.SMEM), vmem(), vmem(), hbm, hbm],
-        out_specs=vmem(),
+        out_shape=(shape(NY, REQ, QUARTER), block, block),
+        in_specs=[smem, smem, vmem(), vmem(), hbm, hbm, hbm, hbm],
+        out_specs=(vmem(), hbm, hbm),
         scratch_shapes=[
             pltpu.VMEM((REQ, 2, CTX, HD), jnp.bfloat16),
             pltpu.VMEM((HEADS * HD, WIDTH), jnp.bfloat16),
             pltpu.VMEM((REQ, HEADS * HD), jnp.bfloat16),
+            pltpu.VMEM((2, 3, EHQ, WIDTH), jnp.bfloat16),
             pltpu.SemaphoreType.DMA((REQ // CHUNK,)),
             pltpu.SemaphoreType.DMA,
+            pltpu.SemaphoreType.DMA((2, 3)),
+            pltpu.SemaphoreType.DMA((2, 3)),
         ],
         compiler_params=params(60),
         name="attend",
-    )(lengths, queries, fresh, cache, weight)
-
-
-def make_plan(ids, gates):
+    )(first, lengths, queries, fresh, cache, weight, gate_up, down)
+
+
+def make_plan(ids, gates, blocks):
     return pl.pallas_call(
         plan_kernel,
-        out_shape=shape(NZ, PLANE, 2 * REQ),
-        in_specs=[vmem(), vmem()],
-        out_specs=vmem(),
+        out_shape=(shape(NZ, PLANE, 2 * REQ), *[shape(*block.shape) for block in blocks]),
+        in_specs=[vmem(), vmem()] + [anywhere()] * 2,
+        out_specs=(vmem(), anywhere(), anywhere()),
+        input_output_aliases={2: 1, 3: 2},
         compiler_params=params(),
         name="plan",
-    )(ids, gates)
-
-
-def pick_weights(first, after, gate_up, down):
-    block = shape(3, EHQ, WIDTH)
-    return pl.pallas_call(
-        pick_kernel,
-        out_shape=(block, block),
-        in_specs=[pl.BlockSpec(memory_space=pltpu.SMEM), anywhere()]
-        + [pl.BlockSpec(memory_space=pltpu.HBM)] * 2,
-        out_specs=(anywhere(), anywhere()),
-        scratch_shapes=[pltpu.SemaphoreType.DMA((4,))],
-        compiler_params=params(60),
-        name="pick_weights",
-    )(first, after, gate_up, down)
+    )(ids, gates, *blocks)
 
 
 def sum_middle(pieces, hidden, plan):
@@ -340,21 +343,17 @@
     )(target, gate, rows)
 
 
-def half_scratch():
-    return [
-        pltpu.VMEM((3, 2 * EHQ, WIDTH), jnp.bfloat16),
-        pltpu.VMEM((NX * BLOCK, 2 * EHQ), jnp.bfloat16),
-        pltpu.SemaphoreType.DMA((3, 2)),
-    ]
-
-
 def first_half(rows, gain, blocks):
     return pl.pallas_call(
         first_half_kernel,
         out_shape=(shape(NX * BLOCK, WIDTH), shape(NX * BLOCK, WIDTH, dtype=jnp.float32)),
-        in_specs=[vmem(), vmem()] + [anywhere()] * 2,
+        in_specs=[vmem(), vmem(), anywhere(), anywhere()],
         out_specs=(vmem(), vmem()),
-        scratch_shapes=half_scratch(),
+        scratch_shapes=[
+            pltpu.VMEM((3, EHQ, WIDTH), jnp.bfloat16),
+            pltpu.VMEM((3, EHQ, WIDTH), jnp.bfloat16),
+            pltpu.SemaphoreType.DMA((2, 3)),
+        ],
         compiler_params=params(24),
         name="first_half",
     )(rows, gain, *blocks)
@@ -364,9 +363,12 @@
     return pl.pallas_call(
         second_half_kernel,
         out_shape=shape(PLANE, BLOCK, QUARTER),
-        in_specs=[vmem(), vmem()] + [anywhere()] * 2,
+        in_specs=[vmem(), vmem(), anywhere(), vmem()],
         out_specs=vmem(),
-        scratch_shapes=half_scratch(),
+        scratch_shapes=[
+            pltpu.VMEM((3, EHQ, WIDTH), jnp.bfloat16),
+            pltpu.SemaphoreType.DMA((3,)),
+        ],
         compiler_params=params(24),
         name="second_half",
     )(normed, part, *blocks)
@@ -418,10 +420,18 @@
 ):
     z, x, c, y = (lax.axis_index(name) for name in ("z", "x", "c", "y"))
     section = (z * NX + x) * NC + c
-    plan = make_plan(expert_ids.T, expert_gates.T)
-    pieces = attend(lengths, queries, new_kv, cache, out_weight)
     first = (y % 2).astype(jnp.int32).reshape(1)
-    blocks = pick_weights(first, pieces, gate_up.transpose(0, 1, 3, 2), down)
+    pieces, *blocks = attend(
+        first,
+        lengths,
+        queries,
+        new_kv,
+        cache,
+        out_weight,
+        gate_up.transpose(0, 1, 3, 2),
+        down,
+    )
+    plan, *blocks = make_plan(expert_ids.T, expert_gates.T, blocks)
     pieces = lax.all_to_all(pieces, "y", 0, 0, tiled=True)
     hidden = lax.dynamic_slice_in_dim(hidden_in, y * QUARTER, QUARTER, 1)
     message, middle = sum_middle(pieces, hidden, plan)

time: 306 us -> 164 us (0.54)
  Pallas kernels: 162 us -> 19.4 us
  blocking collectives: 48.2 us -> 44.9 us
    pallas_call x3 -> x2, Pallas kernels: 150 us -> 8.29 us  [the longest x1 8.03 us: attend(): pl.pallas_call(attention_kernel, out_shape=(shape(NY, REQ, QUARTER), bloc...]
  transfers between devices with their start and end apart: 8 -> 8, of which waited for: 5 -> 5; matrix products, arithmetic and copies ran while one was open for 0% -> 1% of each run, Pallas kernels for 49% -> 4%
where the time goes in v9:
time: 164 us
  waiting for transfers between devices  58.6 us (36%)
  blocking collectives  44.9 us (27%)
  starting transfers between devices  37.3 us (23%)
  Pallas kernels  19.4 us (12%)
    ppermute x2, waiting for transfers between devices, move_weights(): lax.ppermute(block, ('c', 'y'), to)  30.8 us
    all_to_all x1, blocking collectives, local(): spread = lax.all_to_all(message, 'z', 0, 0, tiled=True)  22.6 us
    all_to_all x1, blocking collectives, local(): back = lax.all_to_all(done, ('x', 'y'), 0, 0, tiled=True)  22.3 us
    all_to_all x1, waiting for transfers between devices, local(): part = lax.all_to_all(part, 'z', 0, 0, tiled=True)  15.1 us
    all_to_all x1, waiting for transfers between devices, local(): lax.all_to_all(leaving.reshape(SECTIONS, HCAP, QUARTER), ('z', 'x', 'c'),...  11 us
    all_to_all x1, starting transfers between devices, local(): part = lax.all_to_all(part, 'z', 0, 0, tiled=True)  8.15 us
    pallas_call x1, Pallas kernels, attend(): pl.pallas_call(attention_kernel, out_shape=(shape(NY, REQ, QUARTER), bloc...  8.03 us
    all_to_all x1, starting transfers between devices, local(): lax.all_to_all(leaving.reshape(SECTIONS, HCAP, QUARTER), ('z', 'x', 'c'),...  6.81 us
  transfers between devices with their start and end apart: 8, of which 5 were waited for; matrix products, arithmetic and copies ran while one was open for 1% of the time, Pallas kernels for 4%

profile of v9, /device:TPU:1, one launch (start us, length us, event | category | flops | bytes accessed | tf_op | source)
XLA Modules:
  0.0 163.8 jit_solution(3335606544119258320)
XLA Ops:
  0.7 8.0 %attend.1 = (bf16[4,64,512]{2,1,0:T(8,128)(2,1)}, bf16[3,192,2048]{2,1,0:T(8,128)(2,1)}, bf16[3,192,2048]{2,1,0:T(8,128)(2,1)}) custom-call(s32[1]{0:T(128)} %bitcast.first_ref, s32[64]{0:T(128)} %lengths_ref.1, bf16[64,1024]{1,0:T(8,128)(2,1)} %queries_ref.1, bf16[64,2,128]{2,1,0:T(2,128)(2,1)} %fresh_ref.1, bf16[64,2,96,128]{3,2,1,0:T(8,128)(2,1)} %cache.1, ...), custom_call_target="tpu_custom_call" | custom-call | tf_op jit(solution)/shard_map/attend/pallas_call | solution.py:257
  8.7 5.0 %all-to-all-start = ((bf16[4,64,512]{2,1,0:T(8,128)(2,1)}), bf16[4,64,512]{2,1,0:T(8,128)(2,1)S(1)}, u32[]{:S(2)}, u32[]{:S(2)}) async-start(bf16[4,64,512]{2,1,0:T(8,128)(2,1)} %get-tuple-element.15), calls=%async_computation | async-start | bytes 524288 | tf_op jit(solution)/shard_map/all_to_all | solution.py:435
  13.7 0.3 plan.1
  14.0 3.0 %collective-permute-start = (bf16[3,192,2048]{2,1,0:T(8,128)(2,1)}, bf16[3,192,2048]{2,1,0:T(8,128)(2,1)}, u32[]{:S(2)}, u32[]{:S(2)}) collective-permute-start(bf16[3,192,2048]{2,1,0:T(8,128)(2,1)} %get-tuple-element.24), channel_id=1, source_target_pairs={{0,4},{1,5},{2,0},{3,1},{4,6},{5,7},{6,2},{7,3},{8,12},{9,13},{10,... | collective-permute-start | bytes 7077896 | tf_op jit(solution)/shard_map/ppermute | solution.py:383
  17.1 2.9 %collective-permute-start.2 = (bf16[3,192,2048]{2,1,0:T(8,128)(2,1)}, bf16[3,192,2048]{2,1,0:T(8,128)(2,1)}, u32[]{:S(2)}, u32[]{:S(2)}) collective-permute-start(bf16[3,192,2048]{2,1,0:T(8,128)(2,1)} %get-tuple-element.27), channel_id=1, source_target_pairs={{0,1},{1,0},{2,5},{3,4},{4,3},{5,2},{6,7},{7,6},{8,9},{9,8},{10,13... | collective-permute-start | bytes 7077896 | tf_op jit(solution)/shard_map/ppermute | solution.py:383
  20.1 22.6 %all_to_all.30.spread_ref = bf16[8,16,2176]{2,1,0:T(8,128)(2,1)S(1)} all-to-all(bf16[8,16,2176]{2,1,0:T(8,128)(2,1)S(1)} %get-tuple-element.20), channel_id=1, replica_groups=mesh['z'=8,'x'=4,'c'=2,'y'=4] {'z'}, dimensions={0} | all-to-all | bytes 1114112 | tf_op jit(solution)/shard_map/all_to_all | solution.py:441
  42.7 2.0 %gather_rows.1 = (bf16[16,80,512]{2,1,0:T(8,128)(2,1)}, f32[16,512]{1,0:T(8,128)S(1)}, f32[16,512]{1,0:T(8,128)S(1)}) custom-call(bf16[8,16,2176]{2,1,0:T(8,128)(2,1)S(1)} %all_to_all.30.spread_ref), custom_call_target="tpu_custom_call" | custom-call | tf_op jit(solution)/shard_map/gather_rows/pallas_call | solution.py:301
  44.7 4.1 %all-to-all-start.2 = ((bf16[16,80,512]{2,1,0:T(8,128)(2,1)}), bf16[16,80,512]{2,1,0:T(8,128)(2,1)S(1)}, u32[]{:S(2)}, u32[]{:S(2)}) async-start(bf16[16,80,512]{2,1,0:T(8,128)(2,1)} %get-tuple-element.23), calls=%async_computation.2 | async-start | bytes 2621440 | tf_op jit(solution)/shard_map/all_to_all | solution.py:443
  48.8 29.4 %collective-permute-done.w0 = bf16[3,192,2048]{2,1,0:T(8,128)(2,1)} collective-permute-done((bf16[3,192,2048]{2,1,0:T(8,128)(2,1)}, bf16[3,192,2048]{2,1,0:T(8,128)(2,1)}, u32[]{:S(2)}, u32[]{:S(2)}) %collective-permute-start) | collective-permute-done | bytes 2359328 | tf_op jit(solution)/shard_map/ppermute | solution.py:383
  78.2 5.8 %collective-permute-start.1 = (bf16[3,192,2048]{2,1,0:T(8,128)(2,1)}, bf16[3,192,2048]{2,1,0:T(8,128)(2,1)}, u32[]{:S(2)}, u32[]{:S(2)}) collective-permute-start(bf16[3,192,2048]{2,1,0:T(8,128)(2,1)} %collective-permute-done.w0), channel_id=1, source_target_pairs={{0,4},{4,0},{1,5},{5,1},{2,6},{6,2},{3,7},{7,3},{8,12},{12,8},{9,1... | collective-permute-start | bytes 7077896 | tf_op jit(solution)/shard_map/ppermute | solution.py:445
  84.0 1.4 collective-permute-done.2.refs_1_
  85.4 1.5 collective-permute-start.3
  86.9 1.6 collective-permute-done.1.w1
  88.5 4.2 %first_half.1 = (bf16[320,2048]{1,0:T(8,128)(2,1)S(1)}, f32[320,2048]{1,0:T(8,128)S(1)}) custom-call(bf16[16,80,512]{2,1,0:T(8,128)(2,1)S(1)} %all-to-all-done.2.rows_ref.refs_0_, f32[1,2048]{1,0:T(1,128)S(1)} %bitcast.7, bf16[3,192,2048]{2,1,0:T(8,128)(2,1)} %collective-permute-done.w0, bf16[3,192,2048]{2,1,0:T(8,128)(2,1)} %collective-permute-done.1.w1), custom_call_target="tpu_custom_call" | custom-call | tf_op jit(solution)/shard_map/first_half/pallas_call | solution.py:347
  92.7 3.3 %second_half.1 = bf16[16,80,512]{2,1,0:T(8,128)(2,1)S(1)} custom-call(bf16[320,2048]{1,0:T(8,128)(2,1)S(1)} %get-tuple-element.25.normed_ref, f32[320,2048]{1,0:T(8,128)S(1)} %get-tuple-element.26.part_ref, bf16[3,192,2048]{2,1,0:T(8,128)(2,1)} %hold.1.w2, bf16[3,192,2048]{2,1,0:T(8,128)(2,1)S(1)} %collective-permute-done.3.w3_ref), custom_call_target="tpu_custom_call" | custom-call | tf_op jit(solution)/shard_map/second_half/pallas_call | solution.py:363
  96.0 22.3 %all_to_all.31.rows_ref = bf16[16,80,512]{2,1,0:T(8,128)(2,1)S(1)} all-to-all(bf16[16,80,512]{2,1,0:T(8,128)(2,1)S(1)} %second_half.1), channel_id=1, replica_groups=mesh['z'=8,'x'=4,'c'=2,'y'=4] {'x','y'}, dimensions={0} | all-to-all | bytes 2621440 | tf_op jit(solution)/shard_map/all_to_all | solution.py:449
  118.2 1.7 %combine_rows.1 = bf16[8,64,512]{2,1,0:T(8,128)(2,1)} custom-call(f32[16,512]{1,0:T(8,128)S(1)} %get-tuple-element.21.target_ref, f32[16,512]{1,0:T(8,128)S(1)} %get-tuple-element.22.gate_ref, bf16[16,80,512]{2,1,0:T(8,128)(2,1)S(1)} %all_to_all.31.rows_ref), custom_call_target="tpu_custom_call" | custom-call | tf_op jit(solution)/shard_map/combine_rows/pallas_call | solution.py:332
  119.9 8.1 %all-to-all-start.4 = ((bf16[8,64,512]{2,1,0:T(8,128)(2,1)}), bf16[8,64,512]{2,1,0:T(8,128)(2,1)S(1)}, u32[]{:S(2)}, u32[]{:S(2)}) async-start(bf16[8,64,512]{2,1,0:T(8,128)(2,1)} %combine_rows.1), calls=%async_computation.4 | async-start | bytes 1048576 | tf_op jit(solution)/shard_map/all_to_all | solution.py:451
  128.3 0.2 convert_reduce_fusion.1
  128.6 15.1 %all-to-all-done.4 = bf16[8,64,512]{2,1,0:T(8,128)(2,1)S(1)} async-done(((bf16[8,64,512]{2,1,0:T(8,128)(2,1)}), bf16[8,64,512]{2,1,0:T(8,128)(2,1)S(1)}, u32[]{:S(2)}, u32[]{:S(2)}) %all-to-all-start.4) | async-done | bytes 524320 | tf_op jit(solution)/shard_map/all_to_all | solution.py:451
  144.0 0.7 reshape.58
  144.7 6.8 %all-to-all-start.5 = ((bf16[64,2,512]{2,1,0:T(2,128)(2,1)}), bf16[64,2,512]{2,1,0:T(2,128)(2,1)S(1)}, u32[]{:S(2)}, u32[]{:S(2)}) async-start(bf16[64,2,512]{2,1,0:T(2,128)(2,1)} %reshape.58), calls=%async_computation.5 | async-start | bytes 262144 | tf_op jit(solution)/shard_map/all_to_all | solution.py:457
  151.9 11.0 %all-to-all-done.5 = bf16[64,2,512]{2,1,0:T(2,128)(2,1)S(1)} async-done(((bf16[64,2,512]{2,1,0:T(2,128)(2,1)}), bf16[64,2,512]{2,1,0:T(2,128)(2,1)S(1)}, u32[]{:S(2)}, u32[]{:S(2)}) %all-to-all-start.5) | async-done | bytes 131104 | tf_op jit(solution)/shard_map/all_to_all | solution.py:457
  162.9 0.8 convolution_convert_fusion
  (30 shorter events, 1.1 us)
Async XLA Ops:
  0.6 19.4 %copy-start = (bf16[64,2048]{1,0:T(8,128)(2,1)S(1)}, bf16[64,2048]{1,0:T(8,128)(2,1)}, u32[]{:S(2)}) copy-start(bf16[64,2048]{1,0:T(8,128)(2,1)} %param.12) | copy-start | bytes 786436
  0.7 13.1 %copy-start.2 = (s32[64,8]{0,1:T(8,128)S(1)}, s32[64,8]{0,1:T(8,128)}, u32[]{:S(2)}) copy-start(s32[64,8]{0,1:T(8,128)} %param.19) | copy-start | bytes 6148
  0.7 13.1 %copy-start.3 = (f32[64,8]{0,1:T(8,128)S(1)}, f32[64,8]{0,1:T(8,128)}, u32[]{:S(2)}) copy-start(f32[64,8]{0,1:T(8,128)} %param.20) | copy-start | bytes 6148
  8.7 11.3 %all-to-all-start = ((bf16[4,64,512]{2,1,0:T(8,128)(2,1)}), bf16[4,64,512]{2,1,0:T(8,128)(2,1)S(1)}, u32[]{:S(2)}, u32[]{:S(2)}) async-start(bf16[4,64,512]{2,1,0:T(8,128)(2,1)} %get-tuple-element.15), calls=%async_computation | async-start | bytes 524288 | tf_op jit(solution)/shard_map/all_to_all | solution.py:435
  14.0 64.2 %collective-permute-start = (bf16[3,192,2048]{2,1,0:T(8,128)(2,1)}, bf16[3,192,2048]{2,1,0:T(8,128)(2,1)}, u32[]{:S(2)}, u32[]{:S(2)}) collective-permute-start(bf16[3,192,2048]{2,1,0:T(8,128)(2,1)} %get-tuple-element.24), channel_id=1, source_target_pairs={{0,4},{1,5},{2,0},{3,1},{4,6},{5,7},{6,2},{7,3},{8,12},{9,13},{10,... | collective-permute-start | bytes 7077896 | tf_op jit(solution)/shard_map/ppermute | solution.py:383
  17.1 68.3 %collective-permute-start.2 = (bf16[3,192,2048]{2,1,0:T(8,128)(2,1)}, bf16[3,192,2048]{2,1,0:T(8,128)(2,1)}, u32[]{:S(2)}, u32[]{:S(2)}) collective-permute-start(bf16[3,192,2048]{2,1,0:T(8,128)(2,1)} %get-tuple-element.27), channel_id=1, source_target_pairs={{0,1},{1,0},{2,5},{3,4},{4,3},{5,2},{6,7},{7,6},{8,9},{9,8},{10,13... | collective-permute-start | bytes 7077896 | tf_op jit(solution)/shard_map/ppermute | solution.py:383
  44.7 40.7 %all-to-all-start.2 = ((bf16[16,80,512]{2,1,0:T(8,128)(2,1)}), bf16[16,80,512]{2,1,0:T(8,128)(2,1)S(1)}, u32[]{:S(2)}, u32[]{:S(2)}) async-start(bf16[16,80,512]{2,1,0:T(8,128)(2,1)} %get-tuple-element.23), calls=%async_computation.2 | async-start | bytes 2621440 | tf_op jit(solution)/shard_map/all_to_all | solution.py:443
  48.8 39.7 %copy-start.1 = (f32[2048]{0:T(1024)S(1)}, f32[2048]{0:T(1024)}, u32[]{:S(2)}) copy-start(f32[2048]{0:T(1024)} %param.18) | copy-start | bytes 24580
  78.2 10.3 %collective-permute-start.1 = (bf16[3,192,2048]{2,1,0:T(8,128)(2,1)}, bf16[3,192,2048]{2,1,0:T(8,128)(2,1)}, u32[]{:S(2)}, u32[]{:S(2)}) collective-permute-start(bf16[3,192,2048]{2,1,0:T(8,128)(2,1)} %collective-permute-done.w0), channel_id=1, source_target_pairs={{0,4},{4,0},{1,5},{5,1},{2,6},{6,2},{3,7},{7,3},{8,12},{12,8},{9,1... | collective-permute-start | bytes 7077896 | tf_op jit(solution)/shard_map/ppermute | solution.py:445
  85.4 7.3 %collective-permute-start.3 = (bf16[3,192,2048]{2,1,0:T(8,128)(2,1)}, bf16[3,192,2048]{2,1,0:T(8,128)(2,1)S(1)}, u32[]{:S(2)}, u32[]{:S(2)}) collective-permute-start(bf16[3,192,2048]{2,1,0:T(8,128)(2,1)} %hold.1.w2), channel_id=1, source_target_pairs={{0,4},{4,0},{1,5},{5,1},{2,6},{6,2},{3,7},{7,3},{8,12},{12,8},{9,1... | collective-permute-start | bytes 7077896 | tf_op jit(solution)/shard_map/ppermute | solution.py:446
  96.0 32.1 %copy-start.5 = (s32[4096]{0:T(1024)S(1)}, s32[4096]{0:T(1024)}, u32[]{:S(2)}) copy-start(s32[4096]{0:T(1024)} %param.23) | copy-start | bytes 49156
  119.9 23.8 %all-to-all-start.4 = ((bf16[8,64,512]{2,1,0:T(8,128)(2,1)}), bf16[8,64,512]{2,1,0:T(8,128)(2,1)S(1)}, u32[]{:S(2)}, u32[]{:S(2)}) async-start(bf16[8,64,512]{2,1,0:T(8,128)(2,1)} %combine_rows.1), calls=%async_computation.4 | async-start | bytes 1048576 | tf_op jit(solution)/shard_map/all_to_all | solution.py:451
  143.8 20.0 %copy-start.4 = (bf16[64,512]{1,0:T(8,128)(2,1)}, bf16[64,512]{1,0:T(8,128)(2,1)S(1)}, u32[]{:S(2)}) copy-start(bf16[64,512]{1,0:T(8,128)(2,1)S(1)} %add_convert_fusion) | copy-start | bytes 196612
  144.7 18.2 %all-to-all-start.5 = ((bf16[64,2,512]{2,1,0:T(2,128)(2,1)}), bf16[64,2,512]{2,1,0:T(2,128)(2,1)S(1)}, u32[]{:S(2)}, u32[]{:S(2)}) async-start(bf16[64,2,512]{2,1,0:T(2,128)(2,1)} %reshape.58), calls=%async_computation.5 | async-start | bytes 262144 | tf_op jit(solution)/shard_map/all_to_all | solution.py:457

commit v10 on v9

--- a/solution.py
+++ b/solution.py
@@ -80,9 +80,10 @@
             mass, values, (((2,), (1,)), ((0,), (0,))), preferred_element_type=jnp.float32
         ) + new * fresh[:, 1:2, :]
         context_ref[rows, :] = context.reshape(CHUNK, HEADS * HD).astype(jnp.bfloat16)
-    for load, store in zip(picks, stores):
-        load.wait()
-        store.start()
+        if i > 0:
+            for k in (2 * i - 2, 2 * i - 1):
+                picks[k].wait()
+                stores[k].start()
     whole.wait()
     for y in range(NY):
         out_ref[y] = jnp.dot(
@@ -444,8 +445,8 @@
     odd = hold(rows, odd)
     even_swapped = lax.ppermute(even, "c", swap)
     odd_swapped = lax.ppermute(odd, "c", swap)
-    normed, half = first_half(rows, moe_gain.reshape(1, WIDTH), (even, even_swapped))
-    done = second_half(normed, half, (odd, odd_swapped))
+    normed, half = first_half(rows, moe_gain.reshape(1, WIDTH), (even, odd))
+    done = second_half(normed, half, (odd_swapped, even_swapped))
     back = lax.all_to_all(done, ("x", "y"), 0, 0, tiled=True)
     part = combine_rows(target, gate, back)
     part = lax.all_to_all(part, "z", 0, 0, tiled=True)

time: 164 us -> 165 us (level)
  Pallas kernels: 19.4 us -> 21.1 us
where the time goes in v10:
time: 165 us
  waiting for transfers between devices  57.7 us (35%)
  blocking collectives  45 us (27%)
  starting transfers between devices  37.5 us (23%)
  Pallas kernels  21.1 us (13%)
    ppermute x2, waiting for transfers between devices, move_weights(): lax.ppermute(block, ('c', 'y'), to)  30.8 us
    all_to_all x1, blocking collectives, local(): spread = lax.all_to_all(message, 'z', 0, 0, tiled=True)  22.6 us
    all_to_all x1, blocking collectives, local(): back = lax.all_to_all(done, ('x', 'y'), 0, 0, tiled=True)  22.4 us
    all_to_all x1, waiting for transfers between devices, local(): part = lax.all_to_all(part, 'z', 0, 0, tiled=True)  15.2 us
    all_to_all x1, waiting for transfers between devices, local(): lax.all_to_all(leaving.reshape(SECTIONS, HCAP, QUARTER), ('z', 'x', 'c'),...  11 us
    pallas_call x1, Pallas kernels, attend(): pl.pallas_call(attention_kernel, out_shape=(shape(NY, REQ, QUARTER), bloc...  8.63 us
    all_to_all x1, starting transfers between devices, local(): part = lax.all_to_all(part, 'z', 0, 0, tiled=True)  8.35 us
    all_to_all x1, starting transfers between devices, local(): lax.all_to_all(leaving.reshape(SECTIONS, HCAP, QUARTER), ('z', 'x', 'c'),...  6.79 us
  transfers between devices with their start and end apart: 8, of which 5 were waited for; matrix products, arithmetic and copies ran while one was open for 1% of the time, Pallas kernels for 4%

profile of v10, /device:TPU:1, one launch (start us, length us, event | category | flops | bytes accessed | tf_op | source)
XLA Modules:
  0.0 164.8 jit_solution(13500548802911872051)
XLA Ops:
  0.7 8.6 %attend.1 = (bf16[4,64,512]{2,1,0:T(8,128)(2,1)}, bf16[3,192,2048]{2,1,0:T(8,128)(2,1)}, bf16[3,192,2048]{2,1,0:T(8,128)(2,1)}) custom-call(s32[1]{0:T(128)} %bitcast.first_ref, s32[64]{0:T(128)} %lengths_ref.1, bf16[64,1024]{1,0:T(8,128)(2,1)} %queries_ref.1, bf16[64,2,128]{2,1,0:T(2,128)(2,1)} %fresh_ref.1, bf16[64,2,96,128]{3,2,1,0:T(8,128)(2,1)} %cache.1, ...), custom_call_target="tpu_custom_call" | custom-call | tf_op jit(solution)/shard_map/attend/pallas_call | solution.py:258
  9.3 5.0 %all-to-all-start = ((bf16[4,64,512]{2,1,0:T(8,128)(2,1)}), bf16[4,64,512]{2,1,0:T(8,128)(2,1)S(1)}, u32[]{:S(2)}, u32[]{:S(2)}) async-start(bf16[4,64,512]{2,1,0:T(8,128)(2,1)} %get-tuple-element.15), calls=%async_computation | async-start | bytes 524288 | tf_op jit(solution)/shard_map/all_to_all | solution.py:436
  14.3 0.3 plan.1
  14.6 3.0 %collective-permute-start = (bf16[3,192,2048]{2,1,0:T(8,128)(2,1)}, bf16[3,192,2048]{2,1,0:T(8,128)(2,1)}, u32[]{:S(2)}, u32[]{:S(2)}) collective-permute-start(bf16[3,192,2048]{2,1,0:T(8,128)(2,1)} %get-tuple-element.24), channel_id=1, source_target_pairs={{0,4},{1,5},{2,0},{3,1},{4,6},{5,7},{6,2},{7,3},{8,12},{9,13},{10,... | collective-permute-start | bytes 7077896 | tf_op jit(solution)/shard_map/ppermute | solution.py:384
  17.7 2.9 %collective-permute-start.1 = (bf16[3,192,2048]{2,1,0:T(8,128)(2,1)}, bf16[3,192,2048]{2,1,0:T(8,128)(2,1)}, u32[]{:S(2)}, u32[]{:S(2)}) collective-permute-start(bf16[3,192,2048]{2,1,0:T(8,128)(2,1)} %get-tuple-element.25), channel_id=1, source_target_pairs={{0,1},{1,0},{2,5},{3,4},{4,3},{5,2},{6,7},{7,6},{8,9},{9,8},{10,13... | collective-permute-start | bytes 7077896 | tf_op jit(solution)/shard_map/ppermute | solution.py:384
  20.7 22.6 %all_to_all.30.spread_ref = bf16[8,16,2176]{2,1,0:T(8,128)(2,1)S(1)} all-to-all(bf16[8,16,2176]{2,1,0:T(8,128)(2,1)S(1)} %get-tuple-element.20), channel_id=1, replica_groups=mesh['z'=8,'x'=4,'c'=2,'y'=4] {'z'}, dimensions={0} | all-to-all | bytes 1114112 | tf_op jit(solution)/shard_map/all_to_all | solution.py:442
  43.3 2.0 %gather_rows.1 = (bf16[16,80,512]{2,1,0:T(8,128)(2,1)}, f32[16,512]{1,0:T(8,128)S(1)}, f32[16,512]{1,0:T(8,128)S(1)}) custom-call(bf16[8,16,2176]{2,1,0:T(8,128)(2,1)S(1)} %all_to_all.30.spread_ref), custom_call_target="tpu_custom_call" | custom-call | tf_op jit(solution)/shard_map/gather_rows/pallas_call | solution.py:302
  45.3 4.1 %all-to-all-start.2 = ((bf16[16,80,512]{2,1,0:T(8,128)(2,1)}), bf16[16,80,512]{2,1,0:T(8,128)(2,1)S(1)}, u32[]{:S(2)}, u32[]{:S(2)}) async-start(bf16[16,80,512]{2,1,0:T(8,128)(2,1)} %get-tuple-element.23), calls=%async_computation.2 | async-start | bytes 2621440 | tf_op jit(solution)/shard_map/all_to_all | solution.py:444
  49.4 29.4 %collective-permute-done.w0 = bf16[3,192,2048]{2,1,0:T(8,128)(2,1)} collective-permute-done((bf16[3,192,2048]{2,1,0:T(8,128)(2,1)}, bf16[3,192,2048]{2,1,0:T(8,128)(2,1)}, u32[]{:S(2)}, u32[]{:S(2)}) %collective-permute-start) | collective-permute-done | bytes 2359328 | tf_op jit(solution)/shard_map/ppermute | solution.py:384
  78.8 5.8 %collective-permute-start.3 = (bf16[3,192,2048]{2,1,0:T(8,128)(2,1)}, bf16[3,192,2048]{2,1,0:T(8,128)(2,1)}, u32[]{:S(2)}, u32[]{:S(2)}) collective-permute-start(bf16[3,192,2048]{2,1,0:T(8,128)(2,1)} %collective-permute-done.w0), channel_id=1, source_target_pairs={{0,4},{4,0},{1,5},{5,1},{2,6},{6,2},{3,7},{7,3},{8,12},{12,8},{9,1... | collective-permute-start | bytes 7077896 | tf_op jit(solution)/shard_map/ppermute | solution.py:446
  84.6 1.4 collective-permute-done.1.refs_1_
  86.0 1.5 collective-permute-start.2
  87.5 4.2 %first_half.1 = (bf16[320,2048]{1,0:T(8,128)(2,1)S(1)}, f32[320,2048]{1,0:T(8,128)S(1)}) custom-call(bf16[16,80,512]{2,1,0:T(8,128)(2,1)S(1)} %all-to-all-done.2.refs_0_.rows_ref, f32[1,2048]{1,0:T(1,128)S(1)} %bitcast.7, bf16[3,192,2048]{2,1,0:T(8,128)(2,1)} %collective-permute-done.w0, bf16[3,192,2048]{2,1,0:T(8,128)(2,1)} %hold.1.w1), custom_call_target="tpu_custom_call" | custom-call | tf_op jit(solution)/shard_map/first_half/pallas_call | solution.py:348
  91.7 0.7 collective-permute-done.2.w2
  92.3 4.4 %second_half.1 = bf16[16,80,512]{2,1,0:T(8,128)(2,1)S(1)} custom-call(bf16[320,2048]{1,0:T(8,128)(2,1)S(1)} %get-tuple-element.26.normed_ref, f32[320,2048]{1,0:T(8,128)S(1)} %get-tuple-element.27.part_ref, bf16[3,192,2048]{2,1,0:T(8,128)(2,1)S(1)} %collective-permute-done.2.w2, bf16[3,192,2048]{2,1,0:T(8,128)(2,1)} %collective-permute-done.3.w3_ref), custom_call_target="tpu_custom_call" | custom-call | tf_op jit(solution)/shard_map/second_half/pallas_call | solution.py:364
  96.7 22.4 %all_to_all.31.rows_ref = bf16[16,80,512]{2,1,0:T(8,128)(2,1)S(1)} all-to-all(bf16[16,80,512]{2,1,0:T(8,128)(2,1)S(1)} %second_half.1), channel_id=1, replica_groups=mesh['z'=8,'x'=4,'c'=2,'y'=4] {'x','y'}, dimensions={0} | all-to-all | bytes 2621440 | tf_op jit(solution)/shard_map/all_to_all | solution.py:450
  119.1 1.7 %combine_rows.1 = bf16[8,64,512]{2,1,0:T(8,128)(2,1)} custom-call(f32[16,512]{1,0:T(8,128)S(1)} %get-tuple-element.21.target_ref, f32[16,512]{1,0:T(8,128)S(1)} %get-tuple-element.22.gate_ref, bf16[16,80,512]{2,1,0:T(8,128)(2,1)S(1)} %all_to_all.31.rows_ref), custom_call_target="tpu_custom_call" | custom-call | tf_op jit(solution)/shard_map/combine_rows/pallas_call | solution.py:333
  120.7 8.4 %all-to-all-start.4 = ((bf16[8,64,512]{2,1,0:T(8,128)(2,1)}), bf16[8,64,512]{2,1,0:T(8,128)(2,1)S(1)}, u32[]{:S(2)}, u32[]{:S(2)}) async-start(bf16[8,64,512]{2,1,0:T(8,128)(2,1)} %combine_rows.1), calls=%async_computation.4 | async-start | bytes 1048576 | tf_op jit(solution)/shard_map/all_to_all | solution.py:452
  129.4 0.2 convert_reduce_fusion.1
  129.6 15.2 %all-to-all-done.4 = bf16[8,64,512]{2,1,0:T(8,128)(2,1)S(1)} async-done(((bf16[8,64,512]{2,1,0:T(8,128)(2,1)}), bf16[8,64,512]{2,1,0:T(8,128)(2,1)S(1)}, u32[]{:S(2)}, u32[]{:S(2)}) %all-to-all-start.4) | async-done | bytes 524320 | tf_op jit(solution)/shard_map/all_to_all | solution.py:452
  145.1 0.7 reshape.58
  145.8 6.8 %all-to-all-start.5 = ((bf16[64,2,512]{2,1,0:T(2,128)(2,1)}), bf16[64,2,512]{2,1,0:T(2,128)(2,1)S(1)}, u32[]{:S(2)}, u32[]{:S(2)}) async-start(bf16[64,2,512]{2,1,0:T(2,128)(2,1)} %reshape.58), calls=%async_computation.5 | async-start | bytes 262144 | tf_op jit(solution)/shard_map/all_to_all | solution.py:458
  152.9 11.0 %all-to-all-done.5 = bf16[64,2,512]{2,1,0:T(2,128)(2,1)S(1)} async-done(((bf16[64,2,512]{2,1,0:T(2,128)(2,1)}), bf16[64,2,512]{2,1,0:T(2,128)(2,1)S(1)}, u32[]{:S(2)}, u32[]{:S(2)}) %all-to-all-start.5) | async-done | bytes 131104 | tf_op jit(solution)/shard_map/all_to_all | solution.py:458
  164.0 0.8 convolution_convert_fusion
  (30 shorter events, 1.1 us)
Async XLA Ops:
  0.6 20.0 %copy-start = (bf16[64,2048]{1,0:T(8,128)(2,1)S(1)}, bf16[64,2048]{1,0:T(8,128)(2,1)}, u32[]{:S(2)}) copy-start(bf16[64,2048]{1,0:T(8,128)(2,1)} %param.12) | copy-start | bytes 786436
  0.7 13.7 %copy-start.2 = (s32[64,8]{0,1:T(8,128)S(1)}, s32[64,8]{0,1:T(8,128)}, u32[]{:S(2)}) copy-start(s32[64,8]{0,1:T(8,128)} %param.19) | copy-start | bytes 6148
  0.7 13.7 %copy-start.3 = (f32[64,8]{0,1:T(8,128)S(1)}, f32[64,8]{0,1:T(8,128)}, u32[]{:S(2)}) copy-start(f32[64,8]{0,1:T(8,128)} %param.20) | copy-start | bytes 6148
  9.3 11.3 %all-to-all-start = ((bf16[4,64,512]{2,1,0:T(8,128)(2,1)}), bf16[4,64,512]{2,1,0:T(8,128)(2,1)S(1)}, u32[]{:S(2)}, u32[]{:S(2)}) async-start(bf16[4,64,512]{2,1,0:T(8,128)(2,1)} %get-tuple-element.15), calls=%async_computation | async-start | bytes 524288 | tf_op jit(solution)/shard_map/all_to_all | solution.py:436
  14.6 64.2 %collective-permute-start = (bf16[3,192,2048]{2,1,0:T(8,128)(2,1)}, bf16[3,192,2048]{2,1,0:T(8,128)(2,1)}, u32[]{:S(2)}, u32[]{:S(2)}) collective-permute-start(bf16[3,192,2048]{2,1,0:T(8,128)(2,1)} %get-tuple-element.24), channel_id=1, source_target_pairs={{0,4},{1,5},{2,0},{3,1},{4,6},{5,7},{6,2},{7,3},{8,12},{9,13},{10,... | collective-permute-start | bytes 7077896 | tf_op jit(solution)/shard_map/ppermute | solution.py:384
  17.7 68.3 %collective-permute-start.1 = (bf16[3,192,2048]{2,1,0:T(8,128)(2,1)}, bf16[3,192,2048]{2,1,0:T(8,128)(2,1)}, u32[]{:S(2)}, u32[]{:S(2)}) collective-permute-start(bf16[3,192,2048]{2,1,0:T(8,128)(2,1)} %get-tuple-element.25), channel_id=1, source_target_pairs={{0,1},{1,0},{2,5},{3,4},{4,3},{5,2},{6,7},{7,6},{8,9},{9,8},{10,13... | collective-permute-start | bytes 7077896 | tf_op jit(solution)/shard_map/ppermute | solution.py:384
  45.3 40.7 %all-to-all-start.2 = ((bf16[16,80,512]{2,1,0:T(8,128)(2,1)}), bf16[16,80,512]{2,1,0:T(8,128)(2,1)S(1)}, u32[]{:S(2)}, u32[]{:S(2)}) async-start(bf16[16,80,512]{2,1,0:T(8,128)(2,1)} %get-tuple-element.23), calls=%async_computation.2 | async-start | bytes 2621440 | tf_op jit(solution)/shard_map/all_to_all | solution.py:444
  49.4 38.1 %copy-start.1 = (f32[2048]{0:T(1024)S(1)}, f32[2048]{0:T(1024)}, u32[]{:S(2)}) copy-start(f32[2048]{0:T(1024)} %param.18) | copy-start | bytes 24580
  78.8 12.8 %collective-permute-start.3 = (bf16[3,192,2048]{2,1,0:T(8,128)(2,1)}, bf16[3,192,2048]{2,1,0:T(8,128)(2,1)}, u32[]{:S(2)}, u32[]{:S(2)}) collective-permute-start(bf16[3,192,2048]{2,1,0:T(8,128)(2,1)} %collective-permute-done.w0), channel_id=1, source_target_pairs={{0,4},{4,0},{1,5},{5,1},{2,6},{6,2},{3,7},{7,3},{8,12},{12,8},{9,1... | collective-permute-start | bytes 7077896 | tf_op jit(solution)/shard_map/ppermute | solution.py:446
  86.0 6.3 %collective-permute-start.2 = (bf16[3,192,2048]{2,1,0:T(8,128)(2,1)}, bf16[3,192,2048]{2,1,0:T(8,128)(2,1)S(1)}, u32[]{:S(2)}, u32[]{:S(2)}) collective-permute-start(bf16[3,192,2048]{2,1,0:T(8,128)(2,1)} %hold.1.w1), channel_id=1, source_target_pairs={{0,4},{4,0},{1,5},{5,1},{2,6},{6,2},{3,7},{7,3},{8,12},{12,8},{9,1... | collective-permute-start | bytes 7077896 | tf_op jit(solution)/shard_map/ppermute | solution.py:447
  96.7 32.4 %copy-start.5 = (s32[4096]{0:T(1024)S(1)}, s32[4096]{0:T(1024)}, u32[]{:S(2)}) copy-start(s32[4096]{0:T(1024)} %param.23) | copy-start | bytes 49156
  120.7 24.1 %all-to-all-start.4 = ((bf16[8,64,512]{2,1,0:T(8,128)(2,1)}), bf16[8,64,512]{2,1,0:T(8,128)(2,1)S(1)}, u32[]{:S(2)}, u32[]{:S(2)}) async-start(bf16[8,64,512]{2,1,0:T(8,128)(2,1)} %combine_rows.1), calls=%async_computation.4 | async-start | bytes 1048576 | tf_op jit(solution)/shard_map/all_to_all | solution.py:452
  144.9 19.9 %copy-start.4 = (bf16[64,512]{1,0:T(8,128)(2,1)}, bf16[64,512]{1,0:T(8,128)(2,1)S(1)}, u32[]{:S(2)}) copy-start(bf16[64,512]{1,0:T(8,128)(2,1)S(1)} %add_convert_fusion) | copy-start | bytes 196612
  145.8 18.1 %all-to-all-start.5 = ((bf16[64,2,512]{2,1,0:T(2,128)(2,1)}), bf16[64,2,512]{2,1,0:T(2,128)(2,1)S(1)}, u32[]{:S(2)}, u32[]{:S(2)}) async-start(bf16[64,2,512]{2,1,0:T(2,128)(2,1)} %reshape.58), calls=%async_computation.5 | async-start | bytes 262144 | tf_op jit(solution)/shard_map/all_to_all | solution.py:458

commit v11 on v9

--- a/solution.py
+++ b/solution.py
@@ -51,9 +51,9 @@
     for copy in loads:
         copy.start()
     whole = pltpu.make_async_copy(weight, weight_ref, weight_sem)
-    whole.start()
     for copy in picks:
         copy.start()
+    whole.start()
     scale = 1.0 / math.sqrt(HD)
     cell = lax.broadcasted_iota(jnp.int32, (HEADS, CTX), 1)
     for i in range(REQ // CHUNK):
@@ -80,9 +80,10 @@
             mass, values, (((2,), (1,)), ((0,), (0,))), preferred_element_type=jnp.float32
         ) + new * fresh[:, 1:2, :]
         context_ref[rows, :] = context.reshape(CHUNK, HEADS * HD).astype(jnp.bfloat16)
-    for load, store in zip(picks, stores):
-        load.wait()
-        store.start()
+        if i == 2:
+            for load, store in zip(picks, stores):
+                load.wait()
+                store.start()
     whole.wait()
     for y in range(NY):
         out_ref[y] = jnp.dot(

time: 164 us -> 164 us (level)
  no operation moved by 1% of the time
where the time goes in v11:
time: 164 us; the launch traced here: 163 us
  waiting for transfers between devices  58.6 us (36%)
  blocking collectives  44.9 us (27%)
  starting transfers between devices  37.3 us (23%)
  Pallas kernels  18.8 us (11%)
    ppermute x2, waiting for transfers between devices, move_weights(): lax.ppermute(block, ('c', 'y'), to)  30.8 us
    all_to_all x1, blocking collectives, local(): spread = lax.all_to_all(message, 'z', 0, 0, tiled=True)  22.6 us
    all_to_all x1, blocking collectives, local(): back = lax.all_to_all(done, ('x', 'y'), 0, 0, tiled=True)  22.3 us
    all_to_all x1, waiting for transfers between devices, local(): part = lax.all_to_all(part, 'z', 0, 0, tiled=True)  15.2 us
    all_to_all x1, waiting for transfers between devices, local(): lax.all_to_all(leaving.reshape(SECTIONS, HCAP, QUARTER), ('z', 'x', 'c'),...  11 us
    all_to_all x1, starting transfers between devices, local(): part = lax.all_to_all(part, 'z', 0, 0, tiled=True)  8.18 us
    pallas_call x1, Pallas kernels, attend(): pl.pallas_call(attention_kernel, out_shape=(shape(NY, REQ, QUARTER), bloc...  7.42 us
    all_to_all x1, starting transfers between devices, local(): lax.all_to_all(leaving.reshape(SECTIONS, HCAP, QUARTER), ('z', 'x', 'c'),...  6.79 us
  transfers between devices with their start and end apart: 8, of which 5 were waited for; matrix products, arithmetic and copies ran while one was open for 1% of the time, Pallas kernels for 4%

profile of v11, /device:TPU:1, one launch (start us, length us, event | category | flops | bytes accessed | tf_op | source)
XLA Modules:
  0.0 163.2 jit_solution(13753741511910723784)
XLA Ops:
  0.7 7.4 %attend.1 = (bf16[4,64,512]{2,1,0:T(8,128)(2,1)}, bf16[3,192,2048]{2,1,0:T(8,128)(2,1)}, bf16[3,192,2048]{2,1,0:T(8,128)(2,1)}) custom-call(s32[1]{0:T(128)} %bitcast.first_ref, s32[64]{0:T(128)} %lengths_ref.1, bf16[64,1024]{1,0:T(8,128)(2,1)} %queries_ref.1, bf16[64,2,128]{2,1,0:T(2,128)(2,1)} %fresh_ref.1, bf16[64,2,96,128]{3,2,1,0:T(8,128)(2,1)} %cache.1, ...), custom_call_target="tpu_custom_call" | custom-call | tf_op jit(solution)/shard_map/attend/pallas_call | solution.py:258
  8.1 5.0 %all-to-all-start = ((bf16[4,64,512]{2,1,0:T(8,128)(2,1)}), bf16[4,64,512]{2,1,0:T(8,128)(2,1)S(1)}, u32[]{:S(2)}, u32[]{:S(2)}) async-start(bf16[4,64,512]{2,1,0:T(8,128)(2,1)} %get-tuple-element.15), calls=%async_computation | async-start | bytes 524288 | tf_op jit(solution)/shard_map/all_to_all | solution.py:436
  13.1 0.3 plan.1
  13.4 3.0 %collective-permute-start = (bf16[3,192,2048]{2,1,0:T(8,128)(2,1)}, bf16[3,192,2048]{2,1,0:T(8,128)(2,1)}, u32[]{:S(2)}, u32[]{:S(2)}) collective-permute-start(bf16[3,192,2048]{2,1,0:T(8,128)(2,1)} %get-tuple-element.24), channel_id=1, source_target_pairs={{0,4},{1,5},{2,0},{3,1},{4,6},{5,7},{6,2},{7,3},{8,12},{9,13},{10,... | collective-permute-start | bytes 7077896 | tf_op jit(solution)/shard_map/ppermute | solution.py:384
  16.5 2.9 %collective-permute-start.2 = (bf16[3,192,2048]{2,1,0:T(8,128)(2,1)}, bf16[3,192,2048]{2,1,0:T(8,128)(2,1)}, u32[]{:S(2)}, u32[]{:S(2)}) collective-permute-start(bf16[3,192,2048]{2,1,0:T(8,128)(2,1)} %get-tuple-element.27), channel_id=1, source_target_pairs={{0,1},{1,0},{2,5},{3,4},{4,3},{5,2},{6,7},{7,6},{8,9},{9,8},{10,13... | collective-permute-start | bytes 7077896 | tf_op jit(solution)/shard_map/ppermute | solution.py:384
  19.5 22.6 %all_to_all.30.spread_ref = bf16[8,16,2176]{2,1,0:T(8,128)(2,1)S(1)} all-to-all(bf16[8,16,2176]{2,1,0:T(8,128)(2,1)S(1)} %get-tuple-element.20), channel_id=1, replica_groups=mesh['z'=8,'x'=4,'c'=2,'y'=4] {'z'}, dimensions={0} | all-to-all | bytes 1114112 | tf_op jit(solution)/shard_map/all_to_all | solution.py:442
  42.1 2.0 %gather_rows.1 = (bf16[16,80,512]{2,1,0:T(8,128)(2,1)}, f32[16,512]{1,0:T(8,128)S(1)}, f32[16,512]{1,0:T(8,128)S(1)}) custom-call(bf16[8,16,2176]{2,1,0:T(8,128)(2,1)S(1)} %all_to_all.30.spread_ref), custom_call_target="tpu_custom_call" | custom-call | tf_op jit(solution)/shard_map/gather_rows/pallas_call | solution.py:302
  44.1 4.1 %all-to-all-start.2 = ((bf16[16,80,512]{2,1,0:T(8,128)(2,1)}), bf16[16,80,512]{2,1,0:T(8,128)(2,1)S(1)}, u32[]{:S(2)}, u32[]{:S(2)}) async-start(bf16[16,80,512]{2,1,0:T(8,128)(2,1)} %get-tuple-element.23), calls=%async_computation.2 | async-start | bytes 2621440 | tf_op jit(solution)/shard_map/all_to_all | solution.py:444
  48.2 29.4 %collective-permute-done.w0 = bf16[3,192,2048]{2,1,0:T(8,128)(2,1)} collective-permute-done((bf16[3,192,2048]{2,1,0:T(8,128)(2,1)}, bf16[3,192,2048]{2,1,0:T(8,128)(2,1)}, u32[]{:S(2)}, u32[]{:S(2)}) %collective-permute-start) | collective-permute-done | bytes 2359328 | tf_op jit(solution)/shard_map/ppermute | solution.py:384
  77.6 5.8 %collective-permute-start.1 = (bf16[3,192,2048]{2,1,0:T(8,128)(2,1)}, bf16[3,192,2048]{2,1,0:T(8,128)(2,1)}, u32[]{:S(2)}, u32[]{:S(2)}) collective-permute-start(bf16[3,192,2048]{2,1,0:T(8,128)(2,1)} %collective-permute-done.w0), channel_id=1, source_target_pairs={{0,4},{4,0},{1,5},{5,1},{2,6},{6,2},{3,7},{7,3},{8,12},{12,8},{9,1... | collective-permute-start | bytes 7077896 | tf_op jit(solution)/shard_map/ppermute | solution.py:446
  83.4 1.4 collective-permute-done.2.refs_1_
  84.8 1.5 collective-permute-start.3
  86.3 1.6 collective-permute-done.1.w1
  87.9 4.2 %first_half.1 = (bf16[320,2048]{1,0:T(8,128)(2,1)S(1)}, f32[320,2048]{1,0:T(8,128)S(1)}) custom-call(bf16[16,80,512]{2,1,0:T(8,128)(2,1)S(1)} %all-to-all-done.2.rows_ref.refs_0_, f32[1,2048]{1,0:T(1,128)S(1)} %bitcast.7, bf16[3,192,2048]{2,1,0:T(8,128)(2,1)} %collective-permute-done.w0, bf16[3,192,2048]{2,1,0:T(8,128)(2,1)} %collective-permute-done.1.w1), custom_call_target="tpu_custom_call" | custom-call | tf_op jit(solution)/shard_map/first_half/pallas_call | solution.py:348
  92.1 3.3 %second_half.1 = bf16[16,80,512]{2,1,0:T(8,128)(2,1)S(1)} custom-call(bf16[320,2048]{1,0:T(8,128)(2,1)S(1)} %get-tuple-element.25.normed_ref, f32[320,2048]{1,0:T(8,128)S(1)} %get-tuple-element.26.part_ref, bf16[3,192,2048]{2,1,0:T(8,128)(2,1)} %hold.1.w2, bf16[3,192,2048]{2,1,0:T(8,128)(2,1)S(1)} %collective-permute-done.3.w3_ref), custom_call_target="tpu_custom_call" | custom-call | tf_op jit(solution)/shard_map/second_half/pallas_call | solution.py:364
  95.3 22.3 %all_to_all.31.rows_ref = bf16[16,80,512]{2,1,0:T(8,128)(2,1)S(1)} all-to-all(bf16[16,80,512]{2,1,0:T(8,128)(2,1)S(1)} %second_half.1), channel_id=1, replica_groups=mesh['z'=8,'x'=4,'c'=2,'y'=4] {'x','y'}, dimensions={0} | all-to-all | bytes 2621440 | tf_op jit(solution)/shard_map/all_to_all | solution.py:450
  117.6 1.7 %combine_rows.1 = bf16[8,64,512]{2,1,0:T(8,128)(2,1)} custom-call(f32[16,512]{1,0:T(8,128)S(1)} %get-tuple-element.21.target_ref, f32[16,512]{1,0:T(8,128)S(1)} %get-tuple-element.22.gate_ref, bf16[16,80,512]{2,1,0:T(8,128)(2,1)S(1)} %all_to_all.31.rows_ref), custom_call_target="tpu_custom_call" | custom-call | tf_op jit(solution)/shard_map/combine_rows/pallas_call | solution.py:333
  119.3 8.2 %all-to-all-start.4 = ((bf16[8,64,512]{2,1,0:T(8,128)(2,1)}), bf16[8,64,512]{2,1,0:T(8,128)(2,1)S(1)}, u32[]{:S(2)}, u32[]{:S(2)}) async-start(bf16[8,64,512]{2,1,0:T(8,128)(2,1)} %combine_rows.1), calls=%async_computation.4 | async-start | bytes 1048576 | tf_op jit(solution)/shard_map/all_to_all | solution.py:452
  127.7 0.2 convert_reduce_fusion.1
  128.0 15.2 %all-to-all-done.4 = bf16[8,64,512]{2,1,0:T(8,128)(2,1)S(1)} async-done(((bf16[8,64,512]{2,1,0:T(8,128)(2,1)}), bf16[8,64,512]{2,1,0:T(8,128)(2,1)S(1)}, u32[]{:S(2)}, u32[]{:S(2)}) %all-to-all-start.4) | async-done | bytes 524320 | tf_op jit(solution)/shard_map/all_to_all | solution.py:452
  143.4 0.7 reshape.58
  144.2 6.8 %all-to-all-start.5 = ((bf16[64,2,512]{2,1,0:T(2,128)(2,1)}), bf16[64,2,512]{2,1,0:T(2,128)(2,1)S(1)}, u32[]{:S(2)}, u32[]{:S(2)}) async-start(bf16[64,2,512]{2,1,0:T(2,128)(2,1)} %reshape.58), calls=%async_computation.5 | async-start | bytes 262144 | tf_op jit(solution)/shard_map/all_to_all | solution.py:458
  151.3 11.0 %all-to-all-done.5 = bf16[64,2,512]{2,1,0:T(2,128)(2,1)S(1)} async-done(((bf16[64,2,512]{2,1,0:T(2,128)(2,1)}), bf16[64,2,512]{2,1,0:T(2,128)(2,1)S(1)}, u32[]{:S(2)}, u32[]{:S(2)}) %all-to-all-start.5) | async-done | bytes 131104 | tf_op jit(solution)/shard_map/all_to_all | solution.py:458
  162.4 0.8 convolution_convert_fusion
  (30 shorter events, 1.1 us)
Async XLA Ops:
  0.6 18.8 %copy-start = (bf16[64,2048]{1,0:T(8,128)(2,1)S(1)}, bf16[64,2048]{1,0:T(8,128)(2,1)}, u32[]{:S(2)}) copy-start(bf16[64,2048]{1,0:T(8,128)(2,1)} %param.12) | copy-start | bytes 786436
  0.7 12.5 %copy-start.2 = (s32[64,8]{0,1:T(8,128)S(1)}, s32[64,8]{0,1:T(8,128)}, u32[]{:S(2)}) copy-start(s32[64,8]{0,1:T(8,128)} %param.19) | copy-start | bytes 6148
  0.7 12.5 %copy-start.3 = (f32[64,8]{0,1:T(8,128)S(1)}, f32[64,8]{0,1:T(8,128)}, u32[]{:S(2)}) copy-start(f32[64,8]{0,1:T(8,128)} %param.20) | copy-start | bytes 6148
  8.1 11.3 %all-to-all-start = ((bf16[4,64,512]{2,1,0:T(8,128)(2,1)}), bf16[4,64,512]{2,1,0:T(8,128)(2,1)S(1)}, u32[]{:S(2)}, u32[]{:S(2)}) async-start(bf16[4,64,512]{2,1,0:T(8,128)(2,1)} %get-tuple-element.15), calls=%async_computation | async-start | bytes 524288 | tf_op jit(solution)/shard_map/all_to_all | solution.py:436
  13.4 64.2 %collective-permute-start = (bf16[3,192,2048]{2,1,0:T(8,128)(2,1)}, bf16[3,192,2048]{2,1,0:T(8,128)(2,1)}, u32[]{:S(2)}, u32[]{:S(2)}) collective-permute-start(bf16[3,192,2048]{2,1,0:T(8,128)(2,1)} %get-tuple-element.24), channel_id=1, source_target_pairs={{0,4},{1,5},{2,0},{3,1},{4,6},{5,7},{6,2},{7,3},{8,12},{9,13},{10,... | collective-permute-start | bytes 7077896 | tf_op jit(solution)/shard_map/ppermute | solution.py:384
  16.5 68.3 %collective-permute-start.2 = (bf16[3,192,2048]{2,1,0:T(8,128)(2,1)}, bf16[3,192,2048]{2,1,0:T(8,128)(2,1)}, u32[]{:S(2)}, u32[]{:S(2)}) collective-permute-start(bf16[3,192,2048]{2,1,0:T(8,128)(2,1)} %get-tuple-element.27), channel_id=1, source_target_pairs={{0,1},{1,0},{2,5},{3,4},{4,3},{5,2},{6,7},{7,6},{8,9},{9,8},{10,13... | collective-permute-start | bytes 7077896 | tf_op jit(solution)/shard_map/ppermute | solution.py:384
  44.1 40.7 %all-to-all-start.2 = ((bf16[16,80,512]{2,1,0:T(8,128)(2,1)}), bf16[16,80,512]{2,1,0:T(8,128)(2,1)S(1)}, u32[]{:S(2)}, u32[]{:S(2)}) async-start(bf16[16,80,512]{2,1,0:T(8,128)(2,1)} %get-tuple-element.23), calls=%async_computation.2 | async-start | bytes 2621440 | tf_op jit(solution)/shard_map/all_to_all | solution.py:444
  48.2 39.7 %copy-start.1 = (f32[2048]{0:T(1024)S(1)}, f32[2048]{0:T(1024)}, u32[]{:S(2)}) copy-start(f32[2048]{0:T(1024)} %param.18) | copy-start | bytes 24580
  77.6 10.3 %collective-permute-start.1 = (bf16[3,192,2048]{2,1,0:T(8,128)(2,1)}, bf16[3,192,2048]{2,1,0:T(8,128)(2,1)}, u32[]{:S(2)}, u32[]{:S(2)}) collective-permute-start(bf16[3,192,2048]{2,1,0:T(8,128)(2,1)} %collective-permute-done.w0), channel_id=1, source_target_pairs={{0,4},{4,0},{1,5},{5,1},{2,6},{6,2},{3,7},{7,3},{8,12},{12,8},{9,1... | collective-permute-start | bytes 7077896 | tf_op jit(solution)/shard_map/ppermute | solution.py:446
  84.8 7.3 %collective-permute-start.3 = (bf16[3,192,2048]{2,1,0:T(8,128)(2,1)}, bf16[3,192,2048]{2,1,0:T(8,128)(2,1)S(1)}, u32[]{:S(2)}, u32[]{:S(2)}) collective-permute-start(bf16[3,192,2048]{2,1,0:T(8,128)(2,1)} %hold.1.w2), channel_id=1, source_target_pairs={{0,4},{4,0},{1,5},{5,1},{2,6},{6,2},{3,7},{7,3},{8,12},{12,8},{9,1... | collective-permute-start | bytes 7077896 | tf_op jit(solution)/shard_map/ppermute | solution.py:447
  95.3 32.1 %copy-start.5 = (s32[4096]{0:T(1024)S(1)}, s32[4096]{0:T(1024)}, u32[]{:S(2)}) copy-start(s32[4096]{0:T(1024)} %param.23) | copy-start | bytes 49156
  119.3 23.9 %all-to-all-start.4 = ((bf16[8,64,512]{2,1,0:T(8,128)(2,1)}), bf16[8,64,512]{2,1,0:T(8,128)(2,1)S(1)}, u32[]{:S(2)}, u32[]{:S(2)}) async-start(bf16[8,64,512]{2,1,0:T(8,128)(2,1)} %combine_rows.1), calls=%async_computation.4 | async-start | bytes 1048576 | tf_op jit(solution)/shard_map/all_to_all | solution.py:452
  143.3 19.9 %copy-start.4 = (bf16[64,512]{1,0:T(8,128)(2,1)}, bf16[64,512]{1,0:T(8,128)(2,1)S(1)}, u32[]{:S(2)}) copy-start(bf16[64,512]{1,0:T(8,128)(2,1)S(1)} %add_convert_fusion) | copy-start | bytes 196612
  144.2 18.1 %all-to-all-start.5 = ((bf16[64,2,512]{2,1,0:T(2,128)(2,1)}), bf16[64,2,512]{2,1,0:T(2,128)(2,1)S(1)}, u32[]{:S(2)}, u32[]{:S(2)}) async-start(bf16[64,2,512]{2,1,0:T(2,128)(2,1)} %reshape.58), calls=%async_computation.5 | async-start | bytes 262144 | tf_op jit(solution)/shard_map/all_to_all | solution.py:458

commit v12 on v11

--- a/solution.py
+++ b/solution.py
@@ -130,7 +130,7 @@
         message_ref[z, :, WIDTH:] = plan_ref[z]
 
 
-def gather_kernel(spread_ref, out_ref, target_ref, gate_ref, pick_ref, rows_ref):
+def gather_kernel(spread_ref, out_ref, weight_ref, target_ref, gate_ref, pick_ref, rows_ref):
     low = lax.broadcasted_iota(jnp.int32, (PLANE, 2 * REQ), 1) < REQ
     for pair in range(NZ // 2):
         left = spread_ref[2 * pair, :, WIDTH:].astype(jnp.float32)
@@ -148,6 +148,8 @@
     for e in range(PLANE):
         hit = target_ref[e : e + 1, :] == slot
         pick_ref[e * BLOCK : (e + 1) * BLOCK, :] = jnp.where(hit, 1.0, 0.0).astype(jnp.bfloat16)
+        weight = jnp.where(hit, gate_ref[e : e + 1, :], 0.0)
+        weight_ref[e * BLOCK : (e + 1) * BLOCK, :] = weight.astype(jnp.bfloat16)
     for e in range(0, PLANE, 4):
         rows = jnp.dot(
             pick_ref[e * BLOCK : (e + 4) * BLOCK, :],
@@ -162,17 +164,11 @@
     del refs
 
 
-def combine_kernel(target_ref, gate_ref, rows_ref, out_ref, weight_ref, packed_ref):
-    slot = lax.broadcasted_iota(jnp.int32, (BLOCK, TOKENS), 0).astype(jnp.float32)
-    for e in range(PLANE):
-        hit = target_ref[e : e + 1, :] == slot
-        weight = jnp.where(hit, gate_ref[e : e + 1, :], 0.0)
-        weight_ref[e * BLOCK : (e + 1) * BLOCK, :] = weight.astype(jnp.bfloat16)
-        packed_ref[e * BLOCK : (e + 1) * BLOCK, :] = rows_ref[e]
+def combine_kernel(weight_ref, rows_ref, out_ref):
+    rows = rows_ref[...].reshape(PLANE * BLOCK, QUARTER)
     dims = (((0,), (0,)), ((), ()))
-    total = lax.dot_general(
-        weight_ref[...], packed_ref[...], dims, preferred_element_type=jnp.float32
-    ).astype(jnp.bfloat16)
+    total = lax.dot_general(weight_ref[...], rows, dims, preferred_element_type=jnp.float32)
+    total = total.astype(jnp.bfloat16)
     for z in range(NZ):
         out_ref[z] = total[z * REQ : (z + 1) * REQ, :]
 
@@ -303,12 +299,13 @@
         gather_kernel,
         out_shape=(
             shape(PLANE, BLOCK, QUARTER),
-            shape(PLANE, TOKENS, dtype=jnp.float32),
-            shape(PLANE, TOKENS, dtype=jnp.float32),
+            shape(PLANE * BLOCK, TOKENS),
         ),
         in_specs=[vmem()],
-        out_specs=(vmem(), vmem(), vmem()),
+        out_specs=(vmem(), vmem()),
         scratch_shapes=[
+            pltpu.VMEM((PLANE, TOKENS), jnp.float32),
+            pltpu.VMEM((PLANE, TOKENS), jnp.float32),
             pltpu.VMEM((PLANE * BLOCK, TOKENS), jnp.bfloat16),
             pltpu.VMEM((TOKENS, QUARTER), jnp.bfloat16),
         ],
@@ -329,19 +326,15 @@
     )(after, block)
 
 
-def combine_rows(target, gate, rows):
+def combine_rows(weight, rows):
     return pl.pallas_call(
         combine_kernel,
         out_shape=shape(NZ, REQ, QUARTER),
-        in_specs=[vmem(), vmem(), vmem()],
+        in_specs=[vmem(), vmem()],
         out_specs=vmem(),
-        scratch_shapes=[
-            pltpu.VMEM((PLANE * BLOCK, TOKENS), jnp.bfloat16),
-            pltpu.VMEM((PLANE * BLOCK, QUARTER), jnp.bfloat16),
-        ],
         compiler_params=params(),
         name="combine_rows",
-    )(target, gate, rows)
+    )(weight, rows)
 
 
 def first_half(rows, gain, blocks):
@@ -440,7 +433,7 @@
     swap = [(0, 1), (1, 0)]
 
     spread = lax.all_to_all(message, "z", 0, 0, tiled=True)
-    send, target, gate = gather_rows(spread)
+    send, weight = gather_rows(spread)
     rows = lax.all_to_all(send, ("x", "y"), 0, 0, tiled=True)
     odd = hold(rows, odd)
     even_swapped = lax.ppermute(even, "c", swap)
@@ -448,7 +441,7 @@
     normed, half = first_half(rows, moe_gain.reshape(1, WIDTH), (even, even_swapped))
     done = second_half(normed, half, (odd, odd_swapped))
     back = lax.all_to_all(done, ("x", "y"), 0, 0, tiled=True)
-    part = combine_rows(target, gate, back)
+    part = combine_rows(weight, back)
     part = lax.all_to_all(part, "z", 0, 0, tiled=True)
     out = middle.astype(jnp.float32) + jnp.sum(part.astype(jnp.float32), axis=0)
     out = out.astype(jnp.bfloat16)

time: 164 us -> 164 us (level)
  transfers between devices with their start and end apart: 8 -> 8, of which waited for: 5 -> 5; matrix products, arithmetic and copies ran while one was open for 1% -> 1% of each run, Pallas kernels for 4% -> 3%
where the time goes in v12:
time: 164 us; the launch traced here: 163 us
  waiting for transfers between devices  58.5 us (36%)
  blocking collectives  44.8 us (27%)
  starting transfers between devices  37.4 us (23%)
  Pallas kernels  17.8 us (11%)
  local copies, waits for them, and re-layouts  2.19 us (1%)
    ppermute x2, waiting for transfers between devices, move_weights(): lax.ppermute(block, ('c', 'y'), to)  30.7 us
    all_to_all x1, blocking collectives, local(): spread = lax.all_to_all(message, 'z', 0, 0, tiled=True)  22.6 us
    all_to_all x1, blocking collectives, local(): back = lax.all_to_all(done, ('x', 'y'), 0, 0, tiled=True)  22.2 us
    all_to_all x1, waiting for transfers between devices, local(): part = lax.all_to_all(part, 'z', 0, 0, tiled=True)  15.1 us
    all_to_all x1, waiting for transfers between devices, local(): lax.all_to_all(leaving.reshape(SECTIONS, HCAP, QUARTER), ('z', 'x', 'c'),...  11 us
    all_to_all x1, starting transfers between devices, local(): part = lax.all_to_all(part, 'z', 0, 0, tiled=True)  8.18 us
    pallas_call x1, Pallas kernels, attend(): pl.pallas_call(attention_kernel, out_shape=(shape(NY, REQ, QUARTER), bloc...  7.43 us
    all_to_all x1, starting transfers between devices, local(): lax.all_to_all(leaving.reshape(SECTIONS, HCAP, QUARTER), ('z', 'x', 'c'),...  6.81 us
  transfers between devices with their start and end apart: 8, of which 5 were waited for; matrix products, arithmetic and copies ran while one was open for 1% of the time, Pallas kernels for 3%

profile of v12, /device:TPU:1, one launch (start us, length us, event | category | flops | bytes accessed | tf_op | source)
XLA Modules:
  0.0 163.2 jit_solution(16096750676832036878)
XLA Ops:
  0.7 7.4 %attend.1 = (bf16[4,64,512]{2,1,0:T(8,128)(2,1)}, bf16[3,192,2048]{2,1,0:T(8,128)(2,1)}, bf16[3,192,2048]{2,1,0:T(8,128)(2,1)}) custom-call(s32[1]{0:T(128)} %bitcast.first_ref, s32[64]{0:T(128)} %lengths_ref.1, bf16[64,1024]{1,0:T(8,128)(2,1)} %queries_ref.1, bf16[64,2,128]{2,1,0:T(2,128)(2,1)} %fresh_ref.1, bf16[64,2,96,128]{3,2,1,0:T(8,128)(2,1)} %cache.1, ...), custom_call_target="tpu_custom_call" | custom-call | tf_op jit(solution)/shard_map/attend/pallas_call | solution.py:254
  8.1 5.0 %all-to-all-start = ((bf16[4,64,512]{2,1,0:T(8,128)(2,1)}), bf16[4,64,512]{2,1,0:T(8,128)(2,1)S(1)}, u32[]{:S(2)}, u32[]{:S(2)}) async-start(bf16[4,64,512]{2,1,0:T(8,128)(2,1)} %get-tuple-element.14), calls=%async_computation | async-start | bytes 524288 | tf_op jit(solution)/shard_map/all_to_all | solution.py:429
  13.1 0.3 plan.1
  13.4 3.0 %collective-permute-start = (bf16[3,192,2048]{2,1,0:T(8,128)(2,1)}, bf16[3,192,2048]{2,1,0:T(8,128)(2,1)}, u32[]{:S(2)}, u32[]{:S(2)}) collective-permute-start(bf16[3,192,2048]{2,1,0:T(8,128)(2,1)} %get-tuple-element.22), channel_id=1, source_target_pairs={{0,4},{1,5},{2,0},{3,1},{4,6},{5,7},{6,2},{7,3},{8,12},{9,13},{10,... | collective-permute-start | bytes 7077896 | tf_op jit(solution)/shard_map/ppermute | solution.py:377
  16.5 2.9 %collective-permute-start.2 = (bf16[3,192,2048]{2,1,0:T(8,128)(2,1)}, bf16[3,192,2048]{2,1,0:T(8,128)(2,1)}, u32[]{:S(2)}, u32[]{:S(2)}) collective-permute-start(bf16[3,192,2048]{2,1,0:T(8,128)(2,1)} %get-tuple-element.25), channel_id=1, source_target_pairs={{0,1},{1,0},{2,5},{3,4},{4,3},{5,2},{6,7},{7,6},{8,9},{9,8},{10,13... | collective-permute-start | bytes 7077896 | tf_op jit(solution)/shard_map/ppermute | solution.py:377
  19.5 22.6 %all_to_all.30.spread_ref = bf16[8,16,2176]{2,1,0:T(8,128)(2,1)S(1)} all-to-all(bf16[8,16,2176]{2,1,0:T(8,128)(2,1)S(1)} %get-tuple-element.19), channel_id=1, replica_groups=mesh['z'=8,'x'=4,'c'=2,'y'=4] {'z'}, dimensions={0} | all-to-all | bytes 1114112 | tf_op jit(solution)/shard_map/all_to_all | solution.py:435
  42.1 1.0 gather_rows.1
  43.1 1.1 copy-done.1
  44.2 4.1 %all-to-all-start.2 = ((bf16[16,80,512]{2,1,0:T(8,128)(2,1)}), bf16[16,80,512]{2,1,0:T(8,128)(2,1)S(1)}, u32[]{:S(2)}, u32[]{:S(2)}) async-start(bf16[16,80,512]{2,1,0:T(8,128)(2,1)} %copy-done.1), calls=%async_computation.2 | async-start | bytes 2621440 | tf_op jit(solution)/shard_map/all_to_all | solution.py:437
  48.3 29.3 %collective-permute-done.w0 = bf16[3,192,2048]{2,1,0:T(8,128)(2,1)} collective-permute-done((bf16[3,192,2048]{2,1,0:T(8,128)(2,1)}, bf16[3,192,2048]{2,1,0:T(8,128)(2,1)}, u32[]{:S(2)}, u32[]{:S(2)}) %collective-permute-start) | collective-permute-done | bytes 2359328 | tf_op jit(solution)/shard_map/ppermute | solution.py:377
  77.6 5.8 %collective-permute-start.1 = (bf16[3,192,2048]{2,1,0:T(8,128)(2,1)}, bf16[3,192,2048]{2,1,0:T(8,128)(2,1)}, u32[]{:S(2)}, u32[]{:S(2)}) collective-permute-start(bf16[3,192,2048]{2,1,0:T(8,128)(2,1)} %collective-permute-done.w0), channel_id=1, source_target_pairs={{0,4},{4,0},{1,5},{5,1},{2,6},{6,2},{3,7},{7,3},{8,12},{12,8},{9,1... | collective-permute-start | bytes 7077896 | tf_op jit(solution)/shard_map/ppermute | solution.py:439
  83.4 1.4 collective-permute-done.2.refs_1_
  84.8 1.5 collective-permute-start.3
  86.3 1.6 collective-permute-done.1.w1
  87.9 4.2 %first_half.1 = (bf16[320,2048]{1,0:T(8,128)(2,1)S(1)}, f32[320,2048]{1,0:T(8,128)S(1)}) custom-call(bf16[16,80,512]{2,1,0:T(8,128)(2,1)S(1)} %all-to-all-done.2.rows_ref.refs_0_, f32[1,2048]{1,0:T(1,128)S(1)} %bitcast.7, bf16[3,192,2048]{2,1,0:T(8,128)(2,1)} %collective-permute-done.w0, bf16[3,192,2048]{2,1,0:T(8,128)(2,1)} %collective-permute-done.1.w1), custom_call_target="tpu_custom_call" | custom-call | tf_op jit(solution)/shard_map/first_half/pallas_call | solution.py:341
  92.1 3.3 %second_half.1 = bf16[16,80,512]{2,1,0:T(8,128)(2,1)S(1)} custom-call(bf16[320,2048]{1,0:T(8,128)(2,1)S(1)} %get-tuple-element.23.normed_ref, f32[320,2048]{1,0:T(8,128)S(1)} %get-tuple-element.24.part_ref, bf16[3,192,2048]{2,1,0:T(8,128)(2,1)} %hold.1.w2, bf16[3,192,2048]{2,1,0:T(8,128)(2,1)S(1)} %collective-permute-done.3.w3_ref), custom_call_target="tpu_custom_call" | custom-call | tf_op jit(solution)/shard_map/second_half/pallas_call | solution.py:357
  95.3 22.2 %all_to_all.31.rows_ref = bf16[16,80,512]{2,1,0:T(8,128)(2,1)S(1)} all-to-all(bf16[16,80,512]{2,1,0:T(8,128)(2,1)S(1)} %second_half.1), channel_id=1, replica_groups=mesh['z'=8,'x'=4,'c'=2,'y'=4] {'x','y'}, dimensions={0} | all-to-all | bytes 2621440 | tf_op jit(solution)/shard_map/all_to_all | solution.py:443
  117.6 1.7 %combine_rows.1 = bf16[8,64,512]{2,1,0:T(8,128)(2,1)} custom-call(bf16[1280,512]{1,0:T(8,128)(2,1)S(1)} %get-tuple-element.20.weight_ref, bf16[16,80,512]{2,1,0:T(8,128)(2,1)S(1)} %all_to_all.31.rows_ref), custom_call_target="tpu_custom_call" | custom-call | tf_op jit(solution)/shard_map/combine_rows/pallas_call | solution.py:330
  119.2 8.2 %all-to-all-start.4 = ((bf16[8,64,512]{2,1,0:T(8,128)(2,1)}), bf16[8,64,512]{2,1,0:T(8,128)(2,1)S(1)}, u32[]{:S(2)}, u32[]{:S(2)}) async-start(bf16[8,64,512]{2,1,0:T(8,128)(2,1)} %combine_rows.1), calls=%async_computation.4 | async-start | bytes 1048576 | tf_op jit(solution)/shard_map/all_to_all | solution.py:445
  128.0 15.1 %all-to-all-done.4 = bf16[8,64,512]{2,1,0:T(8,128)(2,1)S(1)} async-done(((bf16[8,64,512]{2,1,0:T(8,128)(2,1)}), bf16[8,64,512]{2,1,0:T(8,128)(2,1)S(1)}, u32[]{:S(2)}, u32[]{:S(2)}) %all-to-all-start.4) | async-done | bytes 524320 | tf_op jit(solution)/shard_map/all_to_all | solution.py:445
  143.4 0.7 reshape.58
  144.1 6.8 %all-to-all-start.5 = ((bf16[64,2,512]{2,1,0:T(2,128)(2,1)}), bf16[64,2,512]{2,1,0:T(2,128)(2,1)S(1)}, u32[]{:S(2)}, u32[]{:S(2)}) async-start(bf16[64,2,512]{2,1,0:T(2,128)(2,1)} %reshape.58), calls=%async_computation.5 | async-start | bytes 262144 | tf_op jit(solution)/shard_map/all_to_all | solution.py:451
  151.3 11.0 %all-to-all-done.5 = bf16[64,2,512]{2,1,0:T(2,128)(2,1)S(1)} async-done(((bf16[64,2,512]{2,1,0:T(2,128)(2,1)}), bf16[64,2,512]{2,1,0:T(2,128)(2,1)S(1)}, u32[]{:S(2)}, u32[]{:S(2)}) %all-to-all-start.5) | async-done | bytes 131104 | tf_op jit(solution)/shard_map/all_to_all | solution.py:451
  162.3 0.8 convolution_convert_fusion
  (32 shorter events, 1.3 us)
Async XLA Ops:
  0.6 18.8 %copy-start = (bf16[64,2048]{1,0:T(8,128)(2,1)S(1)}, bf16[64,2048]{1,0:T(8,128)(2,1)}, u32[]{:S(2)}) copy-start(bf16[64,2048]{1,0:T(8,128)(2,1)} %param.12) | copy-start | bytes 786436
  0.7 12.5 %copy-start.3 = (s32[64,8]{0,1:T(8,128)S(1)}, s32[64,8]{0,1:T(8,128)}, u32[]{:S(2)}) copy-start(s32[64,8]{0,1:T(8,128)} %param.19) | copy-start | bytes 6148
  0.7 12.5 %copy-start.4 = (f32[64,8]{0,1:T(8,128)S(1)}, f32[64,8]{0,1:T(8,128)}, u32[]{:S(2)}) copy-start(f32[64,8]{0,1:T(8,128)} %param.20) | copy-start | bytes 6148
  8.1 11.3 %all-to-all-start = ((bf16[4,64,512]{2,1,0:T(8,128)(2,1)}), bf16[4,64,512]{2,1,0:T(8,128)(2,1)S(1)}, u32[]{:S(2)}, u32[]{:S(2)}) async-start(bf16[4,64,512]{2,1,0:T(8,128)(2,1)} %get-tuple-element.14), calls=%async_computation | async-start | bytes 524288 | tf_op jit(solution)/shard_map/all_to_all | solution.py:429
  13.4 64.2 %collective-permute-start = (bf16[3,192,2048]{2,1,0:T(8,128)(2,1)}, bf16[3,192,2048]{2,1,0:T(8,128)(2,1)}, u32[]{:S(2)}, u32[]{:S(2)}) collective-permute-start(bf16[3,192,2048]{2,1,0:T(8,128)(2,1)} %get-tuple-element.22), channel_id=1, source_target_pairs={{0,4},{1,5},{2,0},{3,1},{4,6},{5,7},{6,2},{7,3},{8,12},{9,13},{10,... | collective-permute-start | bytes 7077896 | tf_op jit(solution)/shard_map/ppermute | solution.py:377
  16.5 68.3 %collective-permute-start.2 = (bf16[3,192,2048]{2,1,0:T(8,128)(2,1)}, bf16[3,192,2048]{2,1,0:T(8,128)(2,1)}, u32[]{:S(2)}, u32[]{:S(2)}) collective-permute-start(bf16[3,192,2048]{2,1,0:T(8,128)(2,1)} %get-tuple-element.25), channel_id=1, source_target_pairs={{0,1},{1,0},{2,5},{3,4},{4,3},{5,2},{6,7},{7,6},{8,9},{9,8},{10,13... | collective-permute-start | bytes 7077896 | tf_op jit(solution)/shard_map/ppermute | solution.py:377
  43.1 1.1 copy-start.1
  44.2 40.6 %all-to-all-start.2 = ((bf16[16,80,512]{2,1,0:T(8,128)(2,1)}), bf16[16,80,512]{2,1,0:T(8,128)(2,1)S(1)}, u32[]{:S(2)}, u32[]{:S(2)}) async-start(bf16[16,80,512]{2,1,0:T(8,128)(2,1)} %copy-done.1), calls=%async_computation.2 | async-start | bytes 2621440 | tf_op jit(solution)/shard_map/all_to_all | solution.py:437
  48.3 39.6 %copy-start.2 = (f32[2048]{0:T(1024)S(1)}, f32[2048]{0:T(1024)}, u32[]{:S(2)}) copy-start(f32[2048]{0:T(1024)} %param.18) | copy-start | bytes 24580
  77.6 10.3 %collective-permute-start.1 = (bf16[3,192,2048]{2,1,0:T(8,128)(2,1)}, bf16[3,192,2048]{2,1,0:T(8,128)(2,1)}, u32[]{:S(2)}, u32[]{:S(2)}) collective-permute-start(bf16[3,192,2048]{2,1,0:T(8,128)(2,1)} %collective-permute-done.w0), channel_id=1, source_target_pairs={{0,4},{4,0},{1,5},{5,1},{2,6},{6,2},{3,7},{7,3},{8,12},{12,8},{9,1... | collective-permute-start | bytes 7077896 | tf_op jit(solution)/shard_map/ppermute | solution.py:439
  84.8 7.3 %collective-permute-start.3 = (bf16[3,192,2048]{2,1,0:T(8,128)(2,1)}, bf16[3,192,2048]{2,1,0:T(8,128)(2,1)S(1)}, u32[]{:S(2)}, u32[]{:S(2)}) collective-permute-start(bf16[3,192,2048]{2,1,0:T(8,128)(2,1)} %hold.1.w2), channel_id=1, source_target_pairs={{0,4},{4,0},{1,5},{5,1},{2,6},{6,2},{3,7},{7,3},{8,12},{12,8},{9,1... | collective-permute-start | bytes 7077896 | tf_op jit(solution)/shard_map/ppermute | solution.py:440
  117.6 9.9 %copy-start.6 = (s32[4096]{0:T(1024)S(1)}, s32[4096]{0:T(1024)}, u32[]{:S(2)}) copy-start(s32[4096]{0:T(1024)} %param.23) | copy-start | bytes 49156
  119.2 23.9 %all-to-all-start.4 = ((bf16[8,64,512]{2,1,0:T(8,128)(2,1)}), bf16[8,64,512]{2,1,0:T(8,128)(2,1)S(1)}, u32[]{:S(2)}, u32[]{:S(2)}) async-start(bf16[8,64,512]{2,1,0:T(8,128)(2,1)} %combine_rows.1), calls=%async_computation.4 | async-start | bytes 1048576 | tf_op jit(solution)/shard_map/all_to_all | solution.py:445
  143.2 20.0 %copy-start.5 = (bf16[64,512]{1,0:T(8,128)(2,1)}, bf16[64,512]{1,0:T(8,128)(2,1)S(1)}, u32[]{:S(2)}) copy-start(bf16[64,512]{1,0:T(8,128)(2,1)S(1)} %add_convert_fusion) | copy-start | bytes 196612
  144.1 18.2 %all-to-all-start.5 = ((bf16[64,2,512]{2,1,0:T(2,128)(2,1)}), bf16[64,2,512]{2,1,0:T(2,128)(2,1)S(1)}, u32[]{:S(2)}, u32[]{:S(2)}) async-start(bf16[64,2,512]{2,1,0:T(2,128)(2,1)} %reshape.58), calls=%async_computation.5 | async-start | bytes 262144 | tf_op jit(solution)/shard_map/all_to_all | solution.py:451
